TPU v7x, 256 devices: a whole 4x4x8 slice. The times are simulated.
256 devices in a mesh: lon: 32 (over y_lo, z, core), lat: 8 (over y_hi, x).
Axes of the slice: x: 4, y: 4 (y_hi: 2, y_lo: 2; y = y_hi * 2 + y_lo), z: 8, core: 2. Of those that a mesh axis runs over, the one named last changes fastest.
Arguments:
- tracer: float32 [192, 2880, 128], P('lat', 'lon'), may hold values from -6 to 6
- wind_u: float32 [192, 2880, 128], P('lat', 'lon'), may hold values from -0.9 to 0.9
- wind_v: float32 [192, 2880, 128], P('lat', 'lon'), may hold values from -0.9 to 0.9
- cotangent: float32 [192, 2880, 128], P('lat', 'lon'), may hold values from -6 to 6
- cutoff: int32 [192], P('lat'), may hold values from 1 to 1440, as said below
Outputs:
- advanced: float32 [192, 2880, 128], P('lat', 'lon')
- grad_tracer: float32 [192, 2880, 128], P('lat', 'lon')
- grad_u: float32 [192, 2880, 128], P('lat', 'lon')
- grad_v: float32 [192, 2880, 128], P('lat', 'lon')
Inputs may be any that keep to these rules, and one draw needn't show every extreme that they name: cutoff is 1440 on every latitude except the 12 nearest each pole, where it rises from 1 on the latitude next to the pole and stays below 1440.
All inputs are finite; a program needn't handle non-finite values.
Results may differ from a plain program's by a relative error of at most 0.00007.
Values sent between devices are 32-bit elements; how exact they have to be, the bound alone decides.
No kernel may reach another device: no remote copies, remote signals or barrier semaphores. Data moves between devices by JAX's collectives and lax.ppermute only.
A program may use at most 128 MiB of HBM per device.

v0:
```python
import math

import jax
import jax.numpy as jnp
from jax import lax
from jax.sharding import PartitionSpec as P

DIFFUSION = 0.125


def with_halo(block, sides, width, periodic):
    for axis, dim in sides:
        count = lax.axis_size(axis)
        forward = [(i, i + 1) for i in range(count - 1)]
        if periodic:
            forward.append((count - 1, 0))
        backward = [(target, source) for source, target in forward]
        low = lax.ppermute(
            lax.slice_in_dim(block, block.shape[dim] - width, None, axis=dim), axis, forward
        )
        high = lax.ppermute(lax.slice_in_dim(block, 0, width, axis=dim), axis, backward)
        block = jnp.concatenate([low, block, high], axis=dim)
    return block


def passed_along(value, axis, steps):
    count = lax.axis_size(axis)
    pairs = [(source, (source + steps) % count) for source in range(count)]
    return lax.ppermute(value, axis, pairs)


def spectral_tables(lon_total):
    columns = jnp.arange(lon_total, dtype=jnp.int32)
    wavenumber = jnp.arange(1, lon_total // 2 + 1, dtype=jnp.int32)
    phase = columns[:, None] * wavenumber[None, :] % lon_total
    angles = phase.astype(jnp.float32) * (2.0 * math.pi / lon_total)
    return (jnp.cos(angles), jnp.sin(angles))


def lookup_table(table_values, positions):
    places = jnp.arange(table_values.shape[0], dtype=jnp.int32)
    onehot = (positions[:, None] == places[None, :]).astype(jnp.int32)
    return jnp.sum(onehot * table_values[None, :], axis=1)


def highpass_lines(line_rows, line_cut, tables):
    cos_table, sine_table = tables
    lon_total = line_rows.shape[1]
    wavenumber = jnp.arange(1, lon_total // 2 + 1, dtype=jnp.int32)
    weight_base = jnp.where(wavenumber == lon_total // 2, 1.0 / lon_total, 2.0 / lon_total).astype(
        jnp.float32
    )
    kept_scale = (wavenumber[None, :] > line_cut[:, None]).astype(jnp.float32) * weight_base[
        None, :
    ]
    highest = lax.Precision.HIGHEST
    real_part = (
        jnp.dot(line_rows, cos_table, precision=highest, preferred_element_type=jnp.float32)
        * kept_scale
    )
    imag_part = (
        jnp.dot(line_rows, sine_table, precision=highest, preferred_element_type=jnp.float32)
        * kept_scale
    )
    return jnp.dot(
        real_part, cos_table.T, precision=highest, preferred_element_type=jnp.float32
    ) + jnp.dot(imag_part, sine_table.T, precision=highest, preferred_element_type=jnp.float32)


def polar_start(row_count, polar_rows):
    lat_index = lax.axis_index("lat")
    return jnp.where(lat_index == 0, 0, row_count - polar_rows).astype(jnp.int32)


def band_highpass(field, cutoff, tables):
    row_count, lon_local, levels = field.shape
    polar_rows = row_count // 2
    start = polar_start(row_count, polar_rows)
    edge_rows = lax.dynamic_slice_in_dim(field, start, polar_rows, 0)
    line_rows = jnp.transpose(edge_rows, (0, 2, 1)).reshape(polar_rows * levels, lon_local)
    full_lines = lax.all_to_all(line_rows, "lon", split_axis=0, concat_axis=1, tiled=True)
    line_total = full_lines.shape[0]
    line_ids = lax.axis_index("lon") * line_total + jnp.arange(line_total, dtype=jnp.int32)
    line_cut = lookup_table(cutoff, start + line_ids // levels)
    high_part = highpass_lines(full_lines, line_cut, tables)
    returned = lax.all_to_all(high_part, "lon", split_axis=1, concat_axis=0, tiled=True)
    returned = jnp.transpose(returned.reshape(polar_rows, levels, lon_local), (0, 2, 1))
    return lax.dynamic_update_slice_in_dim(jnp.zeros_like(field), returned, start, 0)


def neighbours(stacked, sign_flip):
    lon_padded = with_halo(stacked, (("lon", 2),), 1, True)
    lat_padded = with_halo(stacked, (("lat", 1),), 1, False)
    east_side = lon_padded[:, :, 2:]
    west_side = lon_padded[:, :, :-2]
    north_side = lat_padded[:, :-2]
    south_side = lat_padded[:, 2:]
    edge_rows = jnp.concatenate([stacked[:, :1], stacked[:, -1:]], axis=1)
    across = (
        passed_along(edge_rows, "lon", lax.axis_size("lon") // 2) * sign_flip[:, None, None, None]
    )
    lat_index = lax.axis_index("lat")
    top_row = jnp.where(lat_index == 0, across[:, 0], north_side[:, 0])
    north_side = north_side.at[:, 0].set(top_row)
    bottom_row = jnp.where(lat_index == lax.axis_size("lat") - 1, across[:, 1], south_side[:, -1])
    south_side = south_side.at[:, -1].set(bottom_row)
    return (east_side, west_side, north_side, south_side)


def body(tracer, wind_u, wind_v, cotangent, cutoff):
    lon_total = tracer.shape[1] * lax.axis_size("lon")
    tables = spectral_tables(lon_total)

    def filter_high(field):
        return band_highpass(field, cutoff, tables)

    plus_one = jnp.ones((1,), jnp.float32)
    east_q, west_q, north_q, south_q = neighbours(tracer[None], plus_one)
    east_q, west_q, north_q, south_q = (east_q[0], west_q[0], north_q[0], south_q[0])
    stepped = (
        tracer
        - 0.5 * wind_u * (east_q - west_q)
        - 0.5 * wind_v * (north_q - south_q)
        + DIFFUSION * (east_q + west_q + north_q + south_q - 4.0 * tracer)
    )
    advanced = stepped - filter_high(stepped)
    adjoint = cotangent - filter_high(cotangent)
    stacked = jnp.stack([adjoint, wind_u * adjoint, wind_v * adjoint], axis=0)
    sign_flip = jnp.array([1.0, 1.0, -1.0], jnp.float32)
    east_s, west_s, north_s, south_s = neighbours(stacked, sign_flip)
    grad_tracer = (
        adjoint
        + 0.5 * (east_s[1] - west_s[1])
        + 0.5 * (north_s[2] - south_s[2])
        + DIFFUSION * (east_s[0] + west_s[0] + north_s[0] + south_s[0] - 4.0 * adjoint)
    )
    grad_u = -0.5 * (east_q - west_q) * adjoint
    grad_v = -0.5 * (north_q - south_q) * adjoint
    return (advanced, grad_tracer, grad_u, grad_v)


def solution(mesh):
    placed = (
        P("lat", "lon", None),
        P("lat", "lon", None),
        P("lat", "lon", None),
        P("lat", "lon", None),
        P("lat"),
    )
    return jax.shard_map(
        body,
        mesh=mesh,
        in_specs=placed,
        out_specs=(
            P("lat", "lon", None),
            P("lat", "lon", None),
            P("lat", "lon", None),
            P("lat", "lon", None),
        ),
        check_vma=False,
    )
```

profile of v0, /device:TPU:6, one launch (start us, length us, event | category | flops | bytes accessed | tf_op | source)
XLA Modules:
  0.0 810.3 jit_solution(13460672502583795510)
XLA Ops:
  0.7 1.2 constant_dynamic-slice_fusion
  1.9 1.2 copy.43
  3.1 9.9 %all-to-all-start.2 = ((f32[32,48,90]{2,1,0:T(8,128)}), f32[32,48,90]{2,1,0:T(8,128)S(1)}, u32[]{:S(2)}, u32[]{:S(2)}) async-start(f32[32,48,90]{2,1,0:T(8,128)} %bitcast.14), calls=%async_computation.2 | async-start | bytes 1572864 | tf_op jit(solution)/shard_map/all_to_all | solution.py:81
  13.0 0.1 select_reduce_fusion
  13.1 23.2 %all-to-all-done.2 = f32[32,48,90]{2,1,0:T(8,128)S(1)} async-done(((f32[32,48,90]{2,1,0:T(8,128)}), f32[32,48,90]{2,1,0:T(8,128)S(1)}, u32[]{:S(2)}, u32[]{:S(2)}) %all-to-all-start.2) | async-done | bytes 552992 | tf_op jit(solution)/shard_map/all_to_all | solution.py:81
  36.3 0.3 copy.40
  36.5 0.4 all_to_all.62
  37.0 77.6 %fusion.70 = f32[48,1440]{1,0:T(8,128)S(1)} fusion(f32[48,2880]{1,0:T(8,128)S(1)} %all_to_all.62, s32[1440]{0:T(1024)S(1)} %iota_add_fusion, f32[1440]{0:T(1024)S(1)} %compare_select_fusion, s32[48]{0:T(128)S(1)} %select_reduce_fusion), kind=kOutput, calls=%fused_computation.52 | convolution fusion | flops 2426319360 | bytes 841152 | tf_op jit(solution)/shard_map/dot_general | solution.py:58
  114.6 78.4 %fusion.64 = f32[48,1440]{1,0:T(8,128)S(1)} fusion(f32[48,2880]{1,0:T(8,128)S(1)} %all_to_all.62, s32[1440]{0:T(1024)S(1)} %iota_add_fusion, f32[1440]{0:T(1024)S(1)} %compare_select_fusion, s32[48]{0:T(128)S(1)} %select_reduce_fusion), kind=kOutput, calls=%fused_computation.50 | convolution fusion | flops 2426319360 | bytes 841152 | tf_op jit(solution)/shard_map/dot_general | solution.py:62
  193.0 83.9 %fusion.6 = f32[48,2880]{1,0:T(8,128)S(1)} fusion(f32[48,1440]{1,0:T(8,128)S(1)} %fusion.70, s32[1440]{0:T(1024)S(1)} %iota_add_fusion), kind=kOutput, calls=%fused_computation.8 | convolution fusion | flops 2426112000 | bytes 835200 | tf_op jit(solution)/shard_map/dot_general | solution.py:65
  276.9 84.2 %fusion.58 = f32[48,2880]{1,0:T(8,128)S(1)} fusion(f32[48,2880]{1,0:T(8,128)S(1)} %fusion.6, f32[48,1440]{1,0:T(8,128)S(1)} %fusion.64, s32[1440]{0:T(1024)S(1)} %iota_add_fusion), kind=kOutput, calls=%fused_computation.42 | convolution fusion | flops 2426250240 | bytes 1388160 | tf_op jit(solution)/shard_map/dot_general | solution.py:67
  361.2 1.4 all_to_all.63
  362.5 1.3 copy.41
  363.9 4.6 all-to-all-start.3
  368.5 0.1 fusion.122
  368.6 4.7 collective-permute-start.2
  373.3 1.9 collective-permute-start.4
  375.2 0.1 pad_maximum_fusion.20
  375.3 1.2 collective-permute-start.3
  376.5 0.6 fusion.121
  377.1 3.9 collective-permute-start
  381.0 2.1 collective-permute-done.4
  383.1 0.3 fusion.85
  383.4 1.1 fusion.94
  384.5 2.5 scatter.14
  387.0 2.5 scatter.15
  389.6 2.2 all-to-all-done.3
  391.8 2.4 copy.42
  394.2 1.1 broadcast.187.clone
  395.3 5.0 dynamic_update_slice.7
  400.3 4.2 multiply_multiply_fusion
  404.5 1.0 copy-done.1
  405.5 0.1 dynamic-slice_bitcast_fusion
  405.6 1.2 copy.35
  406.8 5.7 all-to-all-start
  412.5 3.5 fusion.92
  416.0 0.9 pad_maximum_fusion.19
  416.9 6.0 collective-permute-start.7
  423.0 2.1 collective-permute-start.9
  425.0 1.9 pad_maximum_fusion.16
  426.9 1.1 collective-permute-start.8
  428.0 0.6 pad_maximum_fusion.22
  428.7 3.9 collective-permute-start.5
  432.5 3.3 all-to-all-done
  435.8 2.3 copy.36
  438.1 2.4 all_to_all.55
  440.5 78.9 %fusion.67 = f32[48,1440]{1,0:T(8,128)S(1)} fusion(f32[48,2880]{1,0:T(8,128)} %all_to_all.55, s32[1440]{0:T(1024)S(1)} %copy-done.6, f32[1440]{0:T(1024)S(1)} %copy-done.8, s32[48]{0:T(128)S(1)} %select_reduce_fusion), kind=kOutput, calls=%fused_computation.51 | convolution fusion | flops 2426319360 | bytes 841152 | tf_op jit(solution)/shard_map/dot_general | solution.py:58
  519.4 78.6 %fusion.61 = f32[48,1440]{1,0:T(8,128)S(1)} fusion(f32[48,2880]{1,0:T(8,128)S(1)} %copy-done.4, s32[1440]{0:T(1024)S(1)} %copy-done.6, f32[1440]{0:T(1024)S(1)} %copy-done.8, s32[48]{0:T(128)S(1)} %select_reduce_fusion), kind=kOutput, calls=%fused_computation.49 | convolution fusion | flops 2426319360 | bytes 841152 | tf_op jit(solution)/shard_map/dot_general | solution.py:62
  598.0 83.6 %fusion.10 = f32[48,2880]{1,0:T(8,128)S(1)} fusion(f32[48,1440]{1,0:T(8,128)S(1)} %fusion.67, s32[1440]{0:T(1024)S(1)} %copy-done.6), kind=kOutput, calls=%fused_computation.10 | convolution fusion | flops 2426112000 | bytes 835200 | tf_op jit(solution)/shard_map/dot_general | solution.py:65
  681.6 84.9 %fusion.55 = f32[48,2880]{1,0:T(8,128)} fusion(f32[48,2880]{1,0:T(8,128)S(1)} %fusion.10, f32[48,1440]{1,0:T(8,128)S(1)} %fusion.61, s32[1440]{0:T(1024)S(1)} %copy-done.6), kind=kOutput, calls=%fused_computation.41 | convolution fusion | flops 2426250240 | bytes 1388160 | tf_op jit(solution)/shard_map/dot_general | solution.py:67
  766.5 3.3 all_to_all.56
  769.8 2.6 copy.37
  772.4 4.6 all-to-all-start.1
  777.0 0.0 copy-start.9
  777.1 4.3 pad_maximum_fusion.3
  781.4 1.1 broadcast_multiply_fusion
  782.5 2.0 broadcast_select_fusion.1
  784.4 6.3 scatter.19
  790.7 6.2 scatter.16
  797.0 3.6 fusion.76
  800.6 1.7 copy.38
  802.3 0.1 broadcast.187
  802.4 6.3 dynamic_update_slice.6
  808.7 1.1 sub.52
  (35 shorter events, 0.1 us)
Async XLA Ops:
  0.6 12.4 %copy-start.10 = (s32[24]{0:T(128)S(1)}, s32[24]{0:T(128)}, u32[]{:S(2)}) copy-start(s32[24]{0:T(128)} %param.18) | copy-start | bytes 292
  3.1 33.2 %all-to-all-start.2 = ((f32[32,48,90]{2,1,0:T(8,128)}), f32[32,48,90]{2,1,0:T(8,128)S(1)}, u32[]{:S(2)}, u32[]{:S(2)}) async-start(f32[32,48,90]{2,1,0:T(8,128)} %bitcast.14), calls=%async_computation.2 | async-start | bytes 1572864 | tf_op jit(solution)/shard_map/all_to_all | solution.py:81
  13.0 263.9 %copy-start.5 = (s32[1440]{0:T(1024)}, s32[1440]{0:T(1024)S(1)}, u32[]{:S(2)}) copy-start(s32[1440]{0:T(1024)S(1)} %iota_add_fusion) | copy-start | bytes 17284
  13.0 101.6 %copy-start.7 = (f32[1440]{0:T(1024)}, f32[1440]{0:T(1024)S(1)}, u32[]{:S(2)}) copy-start(f32[1440]{0:T(1024)S(1)} %compare_select_fusion) | copy-start | bytes 17284
  361.1 7.4 copy-start
  363.9 27.9 %all-to-all-start.3 = ((f32[48,32,90]{2,0,1:T(8,128)}), f32[48,32,90]{2,0,1:T(8,128)}, u32[]{:S(2)}, u32[]{:S(2)}) async-start(f32[48,32,90]{2,0,1:T(8,128)} %copy.41), calls=%async_computation.3 | async-start | bytes 1572864 | tf_op jit(solution)/shard_map/all_to_all | solution.py:86
  368.6 12.4 %collective-permute-start.2 = (f32[1,1,90,128]{3,1,2,0:T(1,128)S(1)}, f32[1,1,90,128]{3,1,2,0:T(1,128)S(1)}, u32[]{:S(2)}, u32[]{:S(2)}) collective-permute-start(f32[1,1,90,128]{3,1,2,0:T(1,128)S(1)} %get-tuple-element.68), channel_id=1, source_target_pairs={{0,1},{1,2},{2,3},{3,4},{4,5},{5,6},{6,7},{8,9},{9,10},{10,11},{11... | collective-permute-start | bytes 138248 | tf_op jit(solution)/shard_map/ppermute | solution.py:18
  373.3 9.8 %collective-permute-start.4 = (f32[1,1,90,128]{3,1,2,0:T(1,128)S(1)}, f32[1,1,90,128]{3,1,2,0:T(1,128)S(1)}, u32[]{:S(2)}, u32[]{:S(2)}) collective-permute-start(f32[1,1,90,128]{3,1,2,0:T(1,128)S(1)} %get-tuple-element.69), channel_id=1, source_target_pairs={{1,0},{2,1},{3,2},{4,3},{5,4},{6,5},{7,6},{9,8},{10,9},{11,10},{12... | collective-permute-start | bytes 138248 | tf_op jit(solution)/shard_map/ppermute | solution.py:21
  375.3 8.0 collective-permute-start.3
  377.1 23.2 %collective-permute-start.1 = (f32[1,24,1,128]{3,1,2,0:T(8,128)}, f32[1,24,1,128]{3,1,2,0:T(8,128)S(1)}, u32[]{:S(2)}, u32[]{:S(2)}) collective-permute-start(f32[1,24,1,128]{3,1,2,0:T(8,128)} %get-tuple-element.64), channel_id=1, source_target_pairs={{0,8},{8,16},{16,24},{24,32},{32,40},{40,48},{48,56},{56,64},{64,7... | collective-permute-start | bytes 36872 | tf_op jit(solution)/shard_map/ppermute | solution.py:18
  377.1 23.2 %collective-permute-start = (f32[1,24,1,128]{3,1,2,0:T(8,128)S(1)}, f32[1,24,1,128]{3,1,2,0:T(8,128)S(1)}, u32[]{:S(2)}, u32[]{:S(2)}) collective-permute-start(f32[1,24,1,128]{3,1,2,0:T(8,128)S(1)} %get-tuple-element.65), channel_id=1, source_target_pairs={{8,0},{16,8},{24,16},{32,24},{40,32},{48,40},{56,48},{64,56},{72,6... | collective-permute-start | bytes 36872 | tf_op jit(solution)/shard_map/ppermute | solution.py:21
  387.0 13.3 %copy-start.3 = (f32[24,90,128]{2,0,1:T(8,128)}, f32[24,90,128]{2,0,1:T(8,128)S(1)}, u32[]{:S(2)}) copy-start(f32[24,90,128]{2,0,1:T(8,128)S(1)} %scatter.14) | copy-start | bytes 3317764
  404.5 1.0 copy-start.1
  406.8 29.0 %all-to-all-start = ((f32[32,48,90]{2,1,0:T(8,128)}), f32[32,48,90]{2,1,0:T(8,128)}, u32[]{:S(2)}, u32[]{:S(2)}) async-start(f32[32,48,90]{2,1,0:T(8,128)} %bitcast.8), calls=%async_computation | async-start | bytes 1572864 | tf_op jit(solution)/shard_map/all_to_all | solution.py:81
  416.9 360.1 %collective-permute-start.7 = (f32[3,1,90,128]{3,1,2,0:T(1,128)}, f32[3,1,90,128]{3,1,2,0:T(1,128)}, u32[]{:S(2)}, u32[]{:S(2)}) collective-permute-start(f32[3,1,90,128]{3,1,2,0:T(1,128)} %get-tuple-element.58), channel_id=1, source_target_pairs={{0,1},{1,2},{2,3},{3,4},{4,5},{5,6},{6,7},{8,9},{9,10},{10,11},{11... | collective-permute-start | bytes 414728 | tf_op jit(solution)/shard_map/ppermute | solution.py:18
  422.9 17.5 %copy-start.6 = (s32[1440]{0:T(1024)S(1)}, s32[1440]{0:T(1024)}, u32[]{:S(2)}) copy-start(s32[1440]{0:T(1024)} %copy-done.5) | copy-start | bytes 17284
  423.0 17.5 %copy-start.8 = (f32[1440]{0:T(1024)S(1)}, f32[1440]{0:T(1024)}, u32[]{:S(2)}) copy-start(f32[1440]{0:T(1024)} %copy-done.7) | copy-start | bytes 17284
  423.0 354.1 %collective-permute-start.9 = (f32[3,1,90,128]{3,1,2,0:T(1,128)S(1)}, f32[3,1,90,128]{3,1,2,0:T(1,128)}, u32[]{:S(2)}, u32[]{:S(2)}) collective-permute-start(f32[3,1,90,128]{3,1,2,0:T(1,128)S(1)} %get-tuple-element.59), channel_id=1, source_target_pairs={{1,0},{2,1},{3,2},{4,3},{5,4},{6,5},{7,6},{9,8},{10,9},{11,10},{12... | collective-permute-start | bytes 414728 | tf_op jit(solution)/shard_map/ppermute | solution.py:21
  426.9 354.4 %collective-permute-start.8 = (f32[3,2,90,128]{3,1,2,0:T(2,128)}, f32[3,2,90,128]{3,1,2,0:T(2,128)}, u32[]{:S(2)}, u32[]{:S(2)}) collective-permute-start(f32[3,2,90,128]{3,1,2,0:T(2,128)} %pad_maximum_fusion.16), channel_id=1, source_target_pairs={{0,128},{8,136},{16,144},{24,152},{32,160},{40,168},{48,176},{56,1... | collective-permute-start | bytes 829448 | tf_op jit(solution)/shard_map/ppermute | solution.py:29
  428.7 368.3 %collective-permute-start.6 = (f32[3,24,1,128]{3,1,2,0:T(8,128)}, f32[3,24,1,128]{3,1,2,0:T(8,128)S(1)}, u32[]{:S(2)}, u32[]{:S(2)}) collective-permute-start(f32[3,24,1,128]{3,1,2,0:T(8,128)} %get-tuple-element.55), channel_id=1, source_target_pairs={{0,8},{8,16},{16,24},{24,32},{32,40},{40,48},{48,56},{56,64},{64,7... | collective-permute-start | bytes 110600 | tf_op jit(solution)/shard_map/ppermute | solution.py:18
  428.7 368.3 %collective-permute-start.5 = (f32[3,24,1,128]{3,1,2,0:T(8,128)}, f32[3,24,1,128]{3,1,2,0:T(8,128)S(1)}, u32[]{:S(2)}, u32[]{:S(2)}) collective-permute-start(f32[3,24,1,128]{3,1,2,0:T(8,128)} %get-tuple-element.54), channel_id=1, source_target_pairs={{8,0},{16,8},{24,16},{32,24},{40,32},{48,40},{56,48},{64,56},{72,6... | collective-permute-start | bytes 110600 | tf_op jit(solution)/shard_map/ppermute | solution.py:21
  440.5 78.9 %copy-start.4 = (f32[48,2880]{1,0:T(8,128)S(1)}, f32[48,2880]{1,0:T(8,128)}, u32[]{:S(2)}) copy-start(f32[48,2880]{1,0:T(8,128)} %all_to_all.55) | copy-start | bytes 1658884
  772.4 28.2 %all-to-all-start.1 = ((f32[48,32,90]{2,0,1:T(8,128)}), f32[48,32,90]{2,0,1:T(8,128)}, u32[]{:S(2)}, u32[]{:S(2)}) async-start(f32[48,32,90]{2,0,1:T(8,128)} %copy.37), calls=%async_computation.1 | async-start | bytes 1572864 | tf_op jit(solution)/shard_map/all_to_all | solution.py:86
  777.0 4.3 copy-start.9
  800.6 8.1 %copy-start.2 = (f32[24,90,128]{2,0,1:T(8,128)S(1)}, f32[24,90,128]{2,0,1:T(8,128)}, u32[]{:S(2)}) copy-start(f32[24,90,128]{2,0,1:T(8,128)} %copy-done.1) | copy-start | bytes 3317764
where the time goes:
time: 824 us; the launch traced here: 810 us
  matrix products  650 us (79%)
  local copies, waits for them, and re-layouts  53.5 us (6%)
  starting transfers between devices  49.6 us (6%)
  waiting for transfers between devices  30.8 us (4%)
  other arithmetic  24.9 us (3%)
    dot_general x2, matrix products, highpass_lines(): jnp.dot(imag_part, sine_table.T, precision=highest, preferred_element_typ...  169 us
    dot_general x2, matrix products, highpass_lines(): jnp.dot(real_part, cos_table.T, precision=highest, preferred_element_type...  167 us
    dot_general x2, matrix products, highpass_lines(): jnp.dot(line_rows, sine_table, precision=highest, preferred_element_type=...  157 us
    dot_general x2, matrix products, highpass_lines(): jnp.dot(line_rows, cos_table, precision=highest, preferred_element_type=j...  157 us
    all_to_all x2, waiting for transfers between devices, band_highpass(): lax.all_to_all(line_rows, 'lon', split_axis=0, concat_axis=1, tiled=True)  26.5 us
  transfers between devices with their start and end apart: 14, of which 4 were waited for; matrix products, arithmetic and copies ran while one was open for 47% of the time, Pallas kernels for 0%

commit v1 on v0

v1 whole, which is shorter than its diff:
```python
import functools

import jax
import jax.numpy as jnp
import ml_dtypes
import numpy as np
from jax import lax
from jax.experimental import pallas as pl
from jax.experimental.pallas import tpu as pltpu
from jax.sharding import PartitionSpec as P

F32 = jnp.float32
BF16 = jnp.bfloat16
LON, LAT = 32, 8
ROWS, COLS, LEV = 24, 90, 128
NLON = LON * COLS
POLAR = 12
MODES = LON // 2 + 1
PAD = 96
SUB = PAD // 4
GROUPS = 5
VMEM = 32 * 1024 * 1024
WINDOW = 16
CHUNK = 15

SPREAD_A = ((0, 1), (7, 6))
SPREAD_B = ((0, 3), (7, 4))


def dft_tables():
    place = np.arange(PAD)
    inside = place < COLS
    wave = np.arange(PAD)
    angle = 2 * np.pi * (wave[:, None] * place[None, :] % COLS) / COLS
    live = (wave[:, None] < COLS) & inside[None, :]
    cos, sin = np.where(live, np.cos(angle), 0), np.where(live, np.sin(angle), 0)
    forward = np.block([[cos, sin], [-sin, cos]])

    where = np.where(inside, place, 0)
    where[91] = -1
    where[90] = COLS
    valid = place < COLS + 2
    back_angle = 2 * np.pi * (where[:, None] * wave[None, :] % COLS) / COLS
    back_live = valid[:, None] & (wave[None, :] < COLS)
    bcos, bsin = np.where(back_live, np.cos(back_angle), 0), np.where(back_live, np.sin(back_angle), 0)
    bcos[92, 0] = 1.0
    backward = np.block([[bcos, -bsin], [bsin, bcos]]) / NLON

    def packed(values):
        spread = values.reshape(MODES, 4, SUB).transpose(0, 2, 1)
        return np.repeat(spread, 32, axis=2).astype(np.float32)

    mode = np.arange(MODES)
    turn = 2 * np.pi * (mode[:, None] * np.where(inside, place, 0)[None, :] % NLON) / NLON
    back_turn = 2 * np.pi * (mode[:, None] * where[None, :] % NLON) / NLON
    back_on = np.where(valid[None, :], 1.0, 0.0) * np.ones((MODES, 1))
    back_on[0, 92] = 1.0
    twiddle = np.stack([packed(np.cos(turn)), packed(-np.sin(turn))])
    back_twiddle = np.stack([packed(np.cos(back_turn) * back_on), packed(np.sin(back_turn) * back_on)])

    def split(matrix):
        high = matrix.astype(ml_dtypes.bfloat16)
        low = (matrix - high.astype(np.float64)).astype(ml_dtypes.bfloat16)
        return np.stack([high, low]).astype(np.float32)

    return split(forward), split(backward), twiddle, back_twiddle


def swap_blocks(parts):
    lane = lax.broadcasted_iota(jnp.int32, parts[0].shape, 1)
    low_half, even_block = lane < 64, (lane // 32) % 2 == 0
    first = [None] * 4
    for i in (0, 1):
        a, b = parts[i], parts[i + 2]
        first[i] = jnp.where(low_half, a, pltpu.roll(b, 64, 1))
        first[i + 2] = jnp.where(low_half, pltpu.roll(a, 64, 1), b)
    second = [None] * 4
    for i in (0, 2):
        a, b = first[i], first[i + 1]
        second[i] = jnp.where(even_block, a, pltpu.roll(b, 32, 1))
        second[i + 1] = jnp.where(even_block, pltpu.roll(a, 96, 1), b)
    return second


def start_of(lat):
    return jnp.where(lat[0] == 0, 0, ROWS - POLAR)


def window_of(lat):
    return pl.multiple_of(jnp.where(lat[0] == 0, 0, ROWS - WINDOW), 8)


def line_of(ref, row, count=COLS, first=0):
    rows = ref.shape[1]
    return ref.reshape(ref.shape[0] * rows, LEV)[pl.ds(first * rows + row, count, stride=rows), :]


def shifted(x, above, below):
    rows = x.shape[0]
    place = lax.broadcasted_iota(jnp.int32, x.shape, 0)
    north = jnp.where(place == 0, above, pltpu.roll(x, 1, 0))
    south = jnp.where(place == rows - 1, below, pltpu.roll(x, rows - 1, 0))
    return north, south


def pack_rows(lat, cutoff, slabs, outs):
    first = start_of(lat) - window_of(lat)
    place = lax.broadcasted_iota(jnp.int32, (WINDOW, LEV), 0)
    cuts = jnp.zeros((WINDOW, LEV), F32)
    for k in range(POLAR):
        cuts = jnp.where(place == first + k, cutoff[start_of(lat) + k].astype(F32), cuts)
    for j in range(COLS, PAD - 1):
        slabs[j] = jnp.zeros((WINDOW, LEV), F32)
    slabs[PAD - 1] = cuts
    for k in range(POLAR):
        parts = [line_of(slabs, first + k, SUB, SUB * s) for s in range(4)]
        for q, part in enumerate(swap_blocks(parts)):
            outs[k // 4][4 * (k % 4) + q] = part


def borders(
    lat, t0, t1, c0, c1, u0, u1, tt0, tt1, ct0, ct1, vt0, vt1, first_cols, last_cols, first_rows, last_rows, edge
):
    for i, (first_col, last_col) in enumerate(((t0, t1), (c0, c1), (u0, u1))):
        first_cols[i] = first_col[0]
        last_cols[i] = last_col[0]
    for i, (first_tile, last_tile) in enumerate(((tt0, tt1), (ct0, ct1), (vt0, vt1))):
        first_rows[i] = line_of(first_tile, 0)
        last_rows[i] = line_of(last_tile, 7)
    is0 = lat[0] == 0
    for i, j in enumerate((0, 2)):
        edge[i] = jnp.where(is0, first_rows[j], last_rows[j])


def pack_cotangent(lat, cutoff, ct, out0, out1, out2, slabs):
    rows = pl.ds(window_of(lat), WINDOW)
    for j in range(COLS):
        slabs[j] = ct[j, rows, :]
    pack_rows(lat, cutoff, slabs, (out0, out1, out2))


def pack_stepped(lat, cutoff, tr, wu, wv, he, hw, ac, out0, out1, out2, slabs):
    rows = pl.ds(window_of(lat), WINDOW)

    def step(j, east, west):
        x = tr[j, rows, :]
        beyond = ac[0, pl.ds(j, 1), :]
        north, south = shifted(x, beyond, beyond)
        slabs[j] = (
            x
            - 0.5 * wu[j, rows, :] * (east - west)
            - 0.5 * wv[j, rows, :] * (north - south)
            + 0.125 * (east + west + north + south - 4.0 * x)
        )

    def middle(i, carry):
        for m in range(8):
            j = 8 * i + m + 1
            step(j, tr[j + 1, rows, :], tr[j - 1, rows, :])
        return carry

    step(0, tr[1, rows, :], hw[0, rows, :])
    lax.fori_loop(0, (COLS - 2) // 8, middle, 0)
    step(COLS - 1, he[0, rows, :], tr[COLS - 2, rows, :])
    pack_rows(lat, cutoff, slabs, (out0, out1, out2))


def times(a, cos, sin):
    if isinstance(sin, float) and sin == 0.0:
        return (a[0] * cos, None if a[1] is None else a[1] * cos) if cos != 1.0 else a
    if a[1] is None:
        return a[0] * cos, a[0] * sin
    return a[0] * cos - a[1] * sin, a[0] * sin + a[1] * cos


def plus(a, b):
    im = b[1] if a[1] is None else (a[1] if b[1] is None else a[1] + b[1])
    return a[0] + b[0], im


def minus(a, b):
    if a[1] is None:
        im = None if b[1] is None else -b[1]
    else:
        im = a[1] if b[1] is None else a[1] - b[1]
    return a[0] - b[0], im


def conj(a):
    return a[0], None if a[1] is None else -a[1]


def quarter(a, sign):
    re, im = a
    return (None if im is None else -sign * im), sign * re


def turned(a, k, n, sign):
    if k == 0:
        return a
    if 4 * k == n:
        re = jnp.zeros_like(a[0]) if a[1] is None else (-a[1] if sign > 0 else a[1])
        return re, (a[0] if sign > 0 else -a[0])
    return times(a, float(np.cos(2 * np.pi * k / n)), float(sign * np.sin(2 * np.pi * k / n)))


def real_dft(values):
    n = len(values)
    if n == 1:
        return [(values[0], None)]
    even, odd = real_dft(values[0::2]), real_dft(values[1::2])
    out = [None] * (n // 2 + 1)
    for k in range(n // 4 + 1):
        t = turned(odd[k], k, n, -1)
        out[k] = plus(even[k], t)
        if n // 2 - k != k:
            out[n // 2 - k] = conj(minus(even[k], t))
    return out


def real_inverse(modes):
    n = 2 * (len(modes) - 1)
    if n == 2:
        return [modes[0][0] + modes[1][0], modes[0][0] - modes[1][0]]
    even, odd = [], []
    for k in range(n // 4 + 1):
        a, b = modes[k], conj(modes[n // 2 - k])
        even.append(plus(a, b))
        odd.append(turned(minus(a, b), k, n, 1))
    out = [None] * n
    out[0::2], out[1::2] = real_inverse(even), real_inverse(odd)
    return out


def three_products(matrix, x):
    high = x.astype(BF16)
    low = (x - high.astype(F32)).astype(BF16)
    dot = functools.partial(jnp.dot, preferred_element_type=F32)
    main, rest = matrix[0].astype(BF16), matrix[1].astype(BF16)
    return dot(main, high) + (dot(main, low) + dot(rest, high))


def pick(lat, own_c, a_c, b_c, own_s, a_s, b_s, out, sems):
    polar = (lat[0] == 0) | (lat[0] == LAT - 1)
    in_a = (lat[0] == 1) | (lat[0] == LAT - 2)

    def copies(c, s):
        return [
            pltpu.make_async_copy(c, out.at[pl.ds(0, 16)], sems.at[0]),
            pltpu.make_async_copy(s, out.at[pl.ds(16, 16)], sems.at[1]),
        ]

    for chosen, c, s in (
        (polar, own_c, own_s),
        (in_a, a_c, a_s),
        (jnp.logical_not(polar | in_a), b_c, b_s),
    ):

        @pl.when(chosen)
        def _():
            for copy in copies(c, s):
                copy.start()

    for copy in copies(own_c, own_s):
        copy.wait()


def keep_low(x, forward, backward, twiddle, back_twiddle, out, lines, rhs):
    lane = lax.broadcasted_iota(jnp.int32, (8, LEV), 1)
    spot = lax.broadcasted_iota(jnp.int32, (8, LEV), 0)
    cut = jnp.max(jnp.where((lane >= 96) & (spot == 7), x[0, SUB - 8 : SUB, :], 0.0))
    for i in range(SUB // 8):
        at = slice(8 * i, 8 * i + 8)
        modes = real_dft([x[b, at, :] for b in range(LON)])
        for k, mode in enumerate(modes):
            re, im = times(mode, twiddle[0, k, at, :], twiddle[1, k, at, :])
            lines[0, k, at, :] = re
            lines[1, k, at, :] = im
    zero = jnp.zeros((SUB, LEV), F32)
    for g in range(GROUPS):
        for part in range(2):
            stack = [lines[part, 4 * g + m] if 4 * g + m < MODES else zero for m in range(4)]
            for s, block in enumerate(swap_blocks(stack)):
                rhs[PAD * part + SUB * s : PAD * part + SUB * s + SUB, LEV * g : LEV * g + LEV] = block
    spectrum = three_products(forward, rhs[...])
    shape = (PAD, LEV * GROUPS)
    number = 4 * (lax.broadcasted_iota(jnp.int32, shape, 1) // LEV)
    number = number + (lax.broadcasted_iota(jnp.int32, shape, 1) // 32) % 4
    number = number + 32 * lax.broadcasted_iota(jnp.int32, shape, 0)
    kept = jnp.minimum(number, NLON - number).astype(F32) <= cut
    kept = jnp.concatenate([kept.astype(F32)] * 2, axis=0) > 0.5
    rhs[...] = three_products(backward, jnp.where(kept, spectrum, 0.0))
    for g in range(GROUPS):
        for part in range(2):
            stack = [
                rhs[PAD * part + SUB * s : PAD * part + SUB * s + SUB, LEV * g : LEV * g + LEV]
                for s in range(4)
            ]
            for m, block in enumerate(swap_blocks(stack)):
                if 4 * g + m < MODES:
                    lines[part, 4 * g + m] = block
    for i in range(SUB // 8):
        at = slice(8 * i, 8 * i + 8)
        modes = [
            times(
                (lines[0, k, at, :], lines[1, k, at, :]),
                back_twiddle[0, k, at, :],
                back_twiddle[1, k, at, :],
            )
            for k in range(MODES)
        ]
        for b, value in enumerate(real_inverse(modes)):
            out[b, at, :] = value


def outputs(
    lat, ret0, ret1, ret2, tr, wu, wv, ct, he, hw, n3, s3, ac,
    adv, gt, gu, gv, adjoint, low_stepped, top, bottom,
):
    is0, is7 = lat[0] == 0, lat[0] == LAT - 1
    step = pl.program_id(0)
    rets = (ret0, ret1, ret2)
    start = start_of(lat)

    @pl.when(step == 0)
    def _():
        def fill(i, carry):
            for m in range(10):
                adjoint[10 * i + m] = ct[10 * i + m]
            return carry

        lax.fori_loop(0, COLS // 10, fill, 0)
        adjoint[COLS] = he[1]
        adjoint[COLS + 1] = hw[1]

        @pl.when(is0 | is7)
        def _():
            flat = adjoint.reshape(PAD * ROWS, LEV)
            flat_stepped = low_stepped.reshape(PAD * ROWS, LEV)
            for k in range(POLAR):
                ret, kk = rets[k // 4], k % 4
                for target, base in ((flat, 0), (flat_stepped, 16)):
                    line = swap_blocks([ret[base + 4 * kk + q] for q in range(4)])
                    for s, part in enumerate(line):
                        target[pl.ds(SUB * s * ROWS + start + k, SUB, stride=ROWS), :] = part

        outer = jnp.where(is0, 0, ROWS - 1)
        mean = adjoint[COLS + 2, pl.ds(outer, 1), :]
        opposite = 2.0 * mean - line_of(adjoint, outer)
        top[0] = jnp.where(is0, ac[0], n3[0])
        top[1] = jnp.where(is0, (0.125 - 0.5 * ac[1]) * opposite, (0.125 + 0.5 * n3[2]) * n3[1])
        bottom[0] = jnp.where(is7, ac[0], s3[0])
        bottom[1] = jnp.where(is7, (0.125 + 0.5 * ac[1]) * opposite, (0.125 - 0.5 * s3[2]) * s3[1])

    place = lax.broadcasted_iota(jnp.int32, (ROWS, LEV), 0)
    filtered = (is0 & (place < POLAR)) | (is7 & (place >= ROWS - POLAR))
    base = step * CHUNK

    for m in range(CHUNK):
        j = base + m
        one = pl.ds(j, 1)
        x, u, v, a = tr[j], wu[j], wv[j], adjoint[j]
        if m == 0:
            at_edge = step == 0
            before = jnp.maximum(j - 1, 0)
            west = jnp.where(at_edge, hw[0], tr[before])
            u_west = jnp.where(at_edge, hw[2], wu[before])
            a_west = adjoint[jnp.where(at_edge, COLS + 1, before)]
        else:
            west, u_west, a_west = tr[j - 1], wu[j - 1], adjoint[j - 1]
        a_east = adjoint[j + 1]
        if m == CHUNK - 1:
            at_edge = j == COLS - 1
            beyond = jnp.minimum(j + 1, COLS - 1)
            east = jnp.where(at_edge, he[0], tr[beyond])
            u_east = jnp.where(at_edge, he[2], wu[beyond])
        else:
            east, u_east = tr[j + 1], wu[j + 1]
        north, south = shifted(x, top[0, one, :], bottom[0, one, :])
        across, along = east - west, north - south
        stepped = (
            x - 0.5 * u * across - 0.5 * v * along + 0.125 * (east + west + north + south - 4.0 * x)
        )
        adv[m] = jnp.where(filtered, low_stepped[j], stepped)
        half = -0.5 * a
        gu[m] = across * half
        gv[m] = along * half
        place_north = jnp.where(
            place == 0, top[1, one, :], pltpu.roll((0.125 + 0.5 * v) * a, 1, 0)
        )
        place_south = jnp.where(
            place == ROWS - 1, bottom[1, one, :], pltpu.roll((0.125 - 0.5 * v) * a, ROWS - 1, 0)
        )
        gt[m] = (
            0.5 * a
            + (0.125 + 0.5 * u_east) * a_east
            + (0.125 - 0.5 * u_west) * a_west
            + place_north
            + place_south
        )


def whole(*shape):
    return pl.BlockSpec(shape, lambda i, *m: (0,) * len(shape))


def column(j):
    return pl.BlockSpec((1, ROWS, LEV), lambda i, *m: (j, 0, 0))


FULL = whole(COLS, ROWS, LEV)
FIRST_TILES = pl.BlockSpec((COLS, 8, LEV), lambda i, *m: (0, 0, 0))
LAST_TILES = pl.BlockSpec((COLS, 8, LEV), lambda i, *m: (0, ROWS // 8 - 1, 0))
OUTER_TILES = pl.BlockSpec(
    (COLS, 8, LEV), lambda i, lat, *m: (0, jnp.where(lat[0] == 0, 0, ROWS // 8 - 1), 0)
)
OUT = pl.BlockSpec((CHUNK, ROWS, LEV), lambda i, *m: (i, 0, 0))
LINES = whole(16, SUB, LEV)
UNITS = whole(32, SUB, LEV)
EDGE = whole(2, COLS, LEV)
SIDE = whole(3, ROWS, LEV)
BAND = whole(3, COLS, LEV)
ANYWHERE = pl.BlockSpec(memory_space=pl.ANY)


def call(kernel, name, scalars, in_specs, outs, cost, scratch=(), grid=1, vmem=VMEM):
    return pl.pallas_call(
        kernel,
        name=name,
        grid_spec=pltpu.PrefetchScalarGridSpec(
            num_scalar_prefetch=scalars,
            grid=(grid,),
            in_specs=in_specs,
            out_specs=[spec for _, spec in outs],
            scratch_shapes=list(scratch),
        ),
        out_shape=[jax.ShapeDtypeStruct(shape, F32) for shape, _ in outs],
        compiler_params=pltpu.CompilerParams(vmem_limit_bytes=vmem),
        cost_estimate=pl.CostEstimate(flops=cost, bytes_accessed=cost, transcendentals=0),
    )


def moved(x, pairs):
    full = [(lon * LAT + a, lon * LAT + b) for lon in range(LON) for a, b in pairs]
    return lax.ppermute(x, ("lon", "lat"), full)


def body(tables, tracer, wind_u, wind_v, cotangent, cutoff):
    lat = lax.axis_index("lat").astype(jnp.int32).reshape(1)
    ring = [(i, (i + 1) % LON) for i in range(LON)]
    back_ring = [(b, a) for a, b in ring]
    opposite = [(i, (i + LON // 2) % LON) for i in range(LON)]
    tracer, wind_u, wind_v, cotangent = (
        jnp.transpose(f, (1, 0, 2)) for f in (tracer, wind_u, wind_v, cotangent)
    )
    chunks = [((16, SUB, LEV), LINES)] * 3
    slabs = pltpu.VMEM((PAD, WINDOW, LEV), F32)

    first_cols, last_cols, first_rows, last_rows, edge = call(
        borders,
        "borders",
        1,
        [column(0), column(COLS - 1)] * 3 + [FIRST_TILES, LAST_TILES] * 3,
        [((3, ROWS, LEV), SIDE)] * 2 + [((3, COLS, LEV), BAND)] * 2 + [((2, COLS, LEV), EDGE)],
        1_000_000,
        vmem=60 * 1024 * 1024,
    )(
        lat, tracer, tracer, cotangent, cotangent, wind_u, wind_u,
        tracer, tracer, cotangent, cotangent, wind_v, wind_v,
    )
    cot = call(pack_cotangent, "pack_cotangent", 2, [FULL], chunks, 1_000_000, [slabs])(
        lat, cutoff, cotangent
    )
    east = lax.ppermute(first_cols, "lon", back_ring)
    west = lax.ppermute(last_cols, "lon", ring)
    across = lax.ppermute(edge, "lon", opposite)
    down = [(i, i + 1) for i in range(LAT - 1)]
    north = lax.ppermute(last_rows, "lat", down)
    south = lax.ppermute(first_rows, "lat", [(b, a) for a, b in down])
    cot_a, cot_b = moved(cot[1], SPREAD_A), moved(cot[2], SPREAD_B)

    step = call(
        pack_stepped,
        "pack_stepped",
        2,
        [FULL] * 3 + [SIDE, SIDE, EDGE],
        chunks,
        3_000_000,
        [slabs],
    )(lat, cutoff, tracer, wind_u, wind_v, east, west, across)
    step_a, step_b = moved(step[1], SPREAD_A), moved(step[2], SPREAD_B)
    (lines,) = call(
        pick, "pick", 1, [ANYWHERE] * 6, [((32, SUB, LEV), ANYWHERE)], 500_000,
        [pltpu.SemaphoreType.DMA((2,))],
    )(lat, cot[0], cot_a, cot_b, step[0], step_a, step_b)
    lines = lax.all_to_all(lines, "lon", 0, 0, tiled=True)

    low = pl.pallas_call(
        keep_low,
        name="keep_low",
        in_specs=[pl.BlockSpec(memory_space=pltpu.VMEM)] * 5,
        out_shape=jax.ShapeDtypeStruct((LON, SUB, LEV), F32),
        scratch_shapes=[
            pltpu.VMEM((2, MODES, SUB, LEV), F32),
            pltpu.VMEM((2 * PAD, LEV * GROUPS), F32),
        ],
        compiler_params=pltpu.CompilerParams(vmem_limit_bytes=VMEM),
        cost_estimate=pl.CostEstimate(flops=5_000_000, bytes_accessed=3_000_000, transcendentals=0),
    )(lines, *tables)
    back = lax.all_to_all(low, "lon", 0, 0, tiled=True)
    back_a = moved(back, [(b, a) for a, b in SPREAD_A])
    back_b = moved(back, [(b, a) for a, b in SPREAD_B])

    results = call(
        outputs,
        "outputs",
        1,
        [UNITS] * 3 + [FULL] * 4 + [SIDE, SIDE, BAND, BAND, EDGE],
        [((COLS, ROWS, LEV), OUT)] * 4,
        9_000_000,
        [pltpu.VMEM((PAD, ROWS, LEV), F32)] * 2 + [pltpu.VMEM((2, COLS, LEV), F32)] * 2,
        grid=COLS // CHUNK,
    )(
        lat, back, back_a, back_b, tracer, wind_u, wind_v, cotangent, east, west, north, south, across,
    )
    return [jnp.transpose(r, (1, 0, 2)) for r in results]


def solution(mesh):
    field = P("lat", "lon", None)
    tables = tuple(jnp.asarray(t) for t in dft_tables())

    def run(*args):
        return jax.shard_map(
            lambda t, *a: tuple(body(t, *a)),
            mesh=mesh,
            in_specs=(P(), field, field, field, field, P("lat")),
            out_specs=(field,) * 4,
            check_vma=False,
        )(tables, *args)

    return run
```

time: 824 us -> 91.5 us (0.11); the launches traced: 810 us -> 91.2 us
  matrix products: 650 us -> 0 us
  local copies, waits for them, and re-layouts: 53.5 us -> 0.05 us
  blocking collectives: 0 us -> 39.4 us
  starting transfers between devices: 49.6 us -> 20.4 us
  other arithmetic: 24.9 us -> 0 us
  waiting for transfers between devices: 30.8 us -> 18.4 us
  Pallas kernels: 0 us -> 12 us
    dot_general x8 -> x0, matrix products: 650 us -> none  [the longest x2 169 us: highpass_lines(): jnp.dot(imag_part, sine_table.T, precision=highest, preferred_element_typ...]
    all_to_all x0 -> x2, blocking collectives: none -> 39.4 us  [the longest x1 20.5 us: body(): lines = lax.all_to_all(lines, 'lon', 0, 0, tiled=True)]
    all_to_all x4 -> x0, waiting for transfers between devices: 28.7 us -> none  [the longest x2 26.5 us: band_highpass(): lax.all_to_all(line_rows, 'lon', split_axis=0, concat_axis=1, tiled=True)]
    all_to_all x4 -> x0, starting transfers between devices: 24.8 us -> none  [the longest x2 15.6 us: band_highpass(): lax.all_to_all(line_rows, 'lon', split_axis=0, concat_axis=1, tiled=True)]
    scatter x4 -> x0, local copies, waits for them, and re-layouts: 17.6 us -> none  [the longest x2 8.8 us: neighbours(): south_side = south_side.at[:, -1].set(bottom_row)]
    ppermute x10 -> x11, waiting for transfers between devices: 2.12 us -> 18.4 us  [the longest x6 7.47 us: moved(): return lax.ppermute(x, ('lon', 'lat'), full)]
    all_to_all x8 -> x0, local copies, waits for them, and re-layouts: 13.9 us -> none  [the longest x4 8.59 us: band_highpass(): lax.all_to_all(high_part, 'lon', split_axis=1, concat_axis=0, tiled=True)]
    pallas_call x0 -> x6, Pallas kernels: none -> 12 us  [the longest x1 3.76 us: body(): call(outputs, 'outputs', 1, [UNITS] * 3 + [FULL] * 4 + [SIDE, SIDE, BAND,...]
  transfers between devices with their start and end apart: 14 -> 11, of which waited for: 4 -> 5; matrix products, arithmetic and copies ran while one was open for 47% -> 0% of each run, Pallas kernels for 0% -> 4%
where the time goes in v1:
time: 91.5 us; the launch traced here: 91.2 us
  blocking collectives  39.4 us (43%)
  starting transfers between devices  20.4 us (22%)
  waiting for transfers between devices  18.4 us (20%)
  Pallas kernels  12 us (13%)
    all_to_all x1, blocking collectives, body(): lines = lax.all_to_all(lines, 'lon', 0, 0, tiled=True)  20.5 us
    all_to_all x1, blocking collectives, body(): back = lax.all_to_all(low, 'lon', 0, 0, tiled=True)  18.9 us
    ppermute x6, waiting for transfers between devices, moved(): return lax.ppermute(x, ('lon', 'lat'), full)  7.47 us
    ppermute x1, waiting for transfers between devices, body(): south = lax.ppermute(first_rows, 'lat', [(b, a) for a, b in down])  6.98 us
    ppermute x6, starting transfers between devices, moved(): return lax.ppermute(x, ('lon', 'lat'), full)  6.07 us
    ppermute x1, starting transfers between devices, body(): north = lax.ppermute(last_rows, 'lat', down)  5.88 us
    ppermute x1, starting transfers between devices, body(): east = lax.ppermute(first_cols, 'lon', back_ring)  4.9 us
    pallas_call x1, Pallas kernels, body(): call(outputs, 'outputs', 1, [UNITS] * 3 + [FULL] * 4 + [SIDE, SIDE, BAND,...  3.76 us
  transfers between devices with their start and end apart: 11, of which 5 were waited for; matrix products, arithmetic and copies ran while one was open for 0% of the time, Pallas kernels for 4%

profile of v1, /device:TPU:6, one launch (start us, length us, event | category | flops | bytes accessed | tf_op | source)
XLA Modules:
  0.0 91.2 jit_solution(6590746298403825300)
XLA Ops:
  0.6 0.0 copy-start.1
  0.6 0.0 copy-start.8
  0.7 0.0 copy-start.2
  0.7 0.0 copy-start.3
  0.7 2.6 %borders.1 = (f32[3,24,128]{2,1,0:T(8,128)}, f32[3,24,128]{2,1,0:T(8,128)}, f32[3,90,128]{2,1,0:T(8,128)}, f32[3,90,128]{2,1,0:T(8,128)}, f32[2,90,128]{2,1,0:T(8,128)}) custom-call(s32[1]{0:T(128)} %bitcast.lat, f32[90,24,128]{2,1,0:T(8,128)} %bitcast.9, f32[90,24,128]{2,1,0:T(8,128)} %bitcast.10, f32[90,24,128]{2,1,0:T(8,128)} %bitcast.15, ...), custom_call_target="tpu_custom_call" | custom-call | flops 1000000 | bytes 1000000 | tf_op jit(solution)/shard_map/borders/pallas_call | solution.py:459
  3.3 0.0 copy-start
  3.3 1.6 %collective-permute-start.4 = (f32[2,90,128]{2,1,0:T(8,128)}, f32[2,90,128]{2,1,0:T(8,128)S(1)}, u32[]{:S(2)}, u32[]{:S(2)}) collective-permute-start(f32[2,90,128]{2,1,0:T(8,128)} %get-tuple-element.24), channel_id=1, source_target_pairs={{0,128},{8,136},{16,144},{24,152},{32,160},{40,168},{48,176},{56,1... | collective-permute-start | bytes 276488 | tf_op jit(solution)/shard_map/ppermute | solution.py:476
  4.9 4.9 %collective-permute-start.2 = (f32[3,24,128]{2,1,0:T(8,128)}, f32[3,24,128]{2,1,0:T(8,128)S(1)}, u32[]{:S(2)}, u32[]{:S(2)}) collective-permute-start(f32[3,24,128]{2,1,0:T(8,128)} %get-tuple-element.22), channel_id=1, source_target_pairs={{8,0},{16,8},{24,16},{32,24},{40,32},{48,40},{56,48},{64,56},{72,6... | collective-permute-start | bytes 110600 | tf_op jit(solution)/shard_map/ppermute | solution.py:474
  9.8 0.0 collective-permute-start.3
  9.8 0.0 copy-done.1
  9.8 0.0 copy-done.8
  9.8 1.5 %pack_cotangent.1 = (f32[16,24,128]{2,1,0:T(8,128)S(1)}, f32[16,24,128]{2,1,0:T(8,128)S(1)}, f32[16,24,128]{2,1,0:T(8,128)S(1)}) custom-call(s32[1]{0:T(128)} %bitcast.lat, s32[24]{0:T(128)S(1)} %copy-done.8, f32[90,24,128]{2,1,0:T(8,128)S(1)} %bitcast.19), custom_call_target="tpu_custom_call" | custom-call | flops 1000000 | bytes 1000000 | tf_op jit(solution)/shard_map/pack_cotangent/pallas_call | solution.py:471
  11.3 0.7 collective-permute-start
  12.0 1.3 %collective-permute-start.1 = (f32[16,24,128]{2,1,0:T(8,128)S(1)}, f32[16,24,128]{2,1,0:T(8,128)S(1)}, u32[]{:S(2)}, u32[]{:S(2)}) collective-permute-start(f32[16,24,128]{2,1,0:T(8,128)S(1)} %get-tuple-element.21), channel_id=1, source_target_pairs={{0,3},{7,4},{8,11},{15,12},{16,19},{23,20},{24,27},{31,28},{32,35}... | collective-permute-start | bytes 589832 | tf_op jit(solution)/shard_map/ppermute | solution.py:445
  13.3 0.0 collective-permute-done.2.he
  13.3 2.2 %collective-permute-done.3.hw = f32[3,24,128]{2,1,0:T(8,128)S(1)} collective-permute-done((f32[3,24,128]{2,1,0:T(8,128)}, f32[3,24,128]{2,1,0:T(8,128)S(1)}, u32[]{:S(2)}, u32[]{:S(2)}) %collective-permute-start.3) | collective-permute-done | bytes 36896 | tf_op jit(solution)/shard_map/ppermute | solution.py:475
  15.5 0.0 collective-permute-done.4.ac
  15.5 0.0 copy-done.2
  15.5 0.0 copy-done.3
  15.5 0.0 copy-done
  15.5 1.9 %pack_stepped.1 = (f32[16,24,128]{2,1,0:T(8,128)S(1)}, f32[16,24,128]{2,1,0:T(8,128)S(1)}, f32[16,24,128]{2,1,0:T(8,128)S(1)}) custom-call(s32[1]{0:T(128)} %bitcast.lat, s32[24]{0:T(128)S(1)} %copy-done.8, f32[90,24,128]{2,1,0:T(8,128)S(1)} %bitcast.13, f32[90,24,128]{2,1,0:T(8,128)S(1)} %bitcast.23, f32[90,24,128]{2,1,0:T(8,128)S(1)} %bitcast.27, ...), custom_call_target="tpu_custom_call" | custom-call | flops 3000000 | bytes 3000000 | tf_op jit(solution)/shard_map/pack_stepped/pallas_call | solution.py:482
  17.5 0.7 collective-permute-start.5
  18.2 1.3 %collective-permute-start.6 = (f32[16,24,128]{2,1,0:T(8,128)S(1)}, f32[16,24,128]{2,1,0:T(8,128)S(1)}, u32[]{:S(2)}, u32[]{:S(2)}) collective-permute-start(f32[16,24,128]{2,1,0:T(8,128)S(1)} %get-tuple-element.27), channel_id=1, source_target_pairs={{0,3},{7,4},{8,11},{15,12},{16,19},{23,20},{24,27},{31,28},{32,35}... | collective-permute-start | bytes 589832 | tf_op jit(solution)/shard_map/ppermute | solution.py:445
  19.5 0.0 collective-permute-done.a_c
  19.5 2.4 %collective-permute-done.1.b_c = f32[16,24,128]{2,1,0:T(8,128)S(1)} collective-permute-done((f32[16,24,128]{2,1,0:T(8,128)S(1)}, f32[16,24,128]{2,1,0:T(8,128)S(1)}, u32[]{:S(2)}, u32[]{:S(2)}) %collective-permute-start.1) | collective-permute-done | bytes 196640 | tf_op jit(solution)/shard_map/ppermute | solution.py:445
  21.9 0.0 collective-permute-done.5.a_s
  21.9 5.1 %collective-permute-done.6.b_s = f32[16,24,128]{2,1,0:T(8,128)S(1)} collective-permute-done((f32[16,24,128]{2,1,0:T(8,128)S(1)}, f32[16,24,128]{2,1,0:T(8,128)S(1)}, u32[]{:S(2)}, u32[]{:S(2)}) %collective-permute-start.6) | collective-permute-done | bytes 196640 | tf_op jit(solution)/shard_map/ppermute | solution.py:445
  26.9 0.0 copy-start.4
  27.0 0.0 copy-start.5
  27.0 0.0 copy-start.6
  27.0 0.0 copy-start.7
  27.0 0.5 pick.1
  27.5 20.5 %all_to_all.10.x = f32[32,24,128]{2,1,0:T(8,128)S(1)} all-to-all(f32[32,24,128]{2,1,0:T(8,128)S(1)} %pick.1), channel_id=1, replica_groups=mesh['lon'=32,'lat'=8] {'lon'}, dimensions={0} | all-to-all | bytes 786432 | tf_op jit(solution)/shard_map/all_to_all | solution.py:496
  48.0 0.0 copy-done.4
  48.0 0.0 copy-done.5
  48.0 0.0 copy-done.6
  48.0 0.0 copy-done.7
  48.0 0.0 copy-start.10
  48.0 0.0 copy-start.9
  48.1 1.8 %keep_low.1 = f32[32,24,128]{2,1,0:T(8,128)S(1)} custom-call(f32[32,24,128]{2,1,0:T(8,128)S(1)} %all_to_all.10.x, f32[2,192,192]{2,1,0:T(8,128)S(1)} %copy-done.7, f32[2,192,192]{2,1,0:T(8,128)S(1)} %copy-done.6, f32[2,17,24,128]{3,2,1,0:T(8,128)S(1)} %copy-done.5, f32[2,17,24,128]{3,2,1,0:T(8,128)S(1)} %copy-done.4), custom_call_target="tpu_custom_call" | custom-call | flops 5000000 | bytes 3000000 | tf_op jit(solution)/shard_map/keep_low/pallas_call | solution.py:498
  49.8 18.9 %all_to_all.11.ret0 = f32[32,24,128]{2,1,0:T(8,128)S(1)} all-to-all(f32[32,24,128]{2,1,0:T(8,128)S(1)} %keep_low.1), channel_id=1, replica_groups=mesh['lon'=32,'lat'=8] {'lon'}, dimensions={0} | all-to-all | bytes 786432 | tf_op jit(solution)/shard_map/all_to_all | solution.py:510
  68.7 1.5 %collective-permute-start.8 = (f32[32,24,128]{2,1,0:T(8,128)S(1)}, f32[32,24,128]{2,1,0:T(8,128)S(1)}, u32[]{:S(2)}, u32[]{:S(2)}) collective-permute-start(f32[32,24,128]{2,1,0:T(8,128)S(1)} %all_to_all.11.ret0), channel_id=1, source_target_pairs={{3,0},{4,7},{11,8},{12,15},{19,16},{20,23},{27,24},{28,31},{35,32}... | collective-permute-start | bytes 1179656 | tf_op jit(solution)/shard_map/ppermute | solution.py:445
  70.2 0.7 collective-permute-start.7
  70.9 0.0 copy-done.10
  70.9 5.9 %collective-permute-start.9 = (f32[3,90,128]{2,1,0:T(8,128)S(1)}, f32[3,90,128]{2,1,0:T(8,128)S(1)}, u32[]{:S(2)}, u32[]{:S(2)}) collective-permute-start(f32[3,90,128]{2,1,0:T(8,128)S(1)} %copy-done.10), channel_id=1, source_target_pairs={{0,1},{1,2},{2,3},{3,4},{4,5},{5,6},{6,7},{8,9},{9,10},{10,11},{11... | collective-permute-start | bytes 414728 | tf_op jit(solution)/shard_map/ppermute | solution.py:478
  76.8 0.0 copy-done.9
  76.8 1.9 %collective-permute-start.10 = (f32[3,90,128]{2,1,0:T(8,128)S(1)}, f32[3,90,128]{2,1,0:T(8,128)S(1)}, u32[]{:S(2)}, u32[]{:S(2)}) collective-permute-start(f32[3,90,128]{2,1,0:T(8,128)S(1)} %copy-done.9), channel_id=1, source_target_pairs={{1,0},{2,1},{3,2},{4,3},{5,4},{6,5},{7,6},{9,8},{10,9},{11,10},{12... | collective-permute-start | bytes 414728 | tf_op jit(solution)/shard_map/ppermute | solution.py:479
  78.7 1.7 %collective-permute-done.9.n3 = f32[3,90,128]{2,1,0:T(8,128)S(1)} collective-permute-done((f32[3,90,128]{2,1,0:T(8,128)S(1)}, f32[3,90,128]{2,1,0:T(8,128)S(1)}, u32[]{:S(2)}, u32[]{:S(2)}) %collective-permute-start.9) | collective-permute-done | bytes 138272 | tf_op jit(solution)/shard_map/ppermute | solution.py:478
  80.4 7.0 %collective-permute-done.10.s3 = f32[3,90,128]{2,1,0:T(8,128)S(1)} collective-permute-done((f32[3,90,128]{2,1,0:T(8,128)S(1)}, f32[3,90,128]{2,1,0:T(8,128)S(1)}, u32[]{:S(2)}, u32[]{:S(2)}) %collective-permute-start.10) | collective-permute-done | bytes 138272 | tf_op jit(solution)/shard_map/ppermute | solution.py:479
  87.4 0.0 collective-permute-done.8.ret2
  87.4 0.0 collective-permute-done.7.ret1
  87.4 3.8 %outputs.1 = (f32[90,24,128]{2,1,0:T(8,128)}, f32[90,24,128]{2,1,0:T(8,128)}, f32[90,24,128]{2,1,0:T(8,128)}, f32[90,24,128]{2,1,0:T(8,128)}) custom-call(s32[1]{0:T(128)} %bitcast.lat, f32[32,24,128]{2,1,0:T(8,128)S(1)} %all_to_all.11.ret0, f32[32,24,128]{2,1,0:T(8,128)S(1)} %collective-permute-done.7.ret1, f32[32,24,128]{2,1,0:T(8,128)S(1)} %collective-permute-done.8.ret2, ...), custom_call_target="tpu_custom_call" | custom-call | flops 9000000 | bytes 9000000 | tf_op jit(solution)/shard_map/outputs/pallas_call | solution.py:514
Async XLA Ops:
  0.6 9.2 %copy-start.1 = (f32[24,90,128]{2,0,1:T(8,128)S(1)}, f32[24,90,128]{2,0,1:T(8,128)}, u32[]{:S(2)}) copy-start(f32[24,90,128]{2,0,1:T(8,128)} %param.12) | copy-start | bytes 3317764
  0.6 9.2 %copy-start.8 = (s32[24]{0:T(128)S(1)}, s32[24]{0:T(128)}, u32[]{:S(2)}) copy-start(s32[24]{0:T(128)} %cutoff.3) | copy-start | bytes 292
  0.7 14.9 %copy-start.2 = (f32[24,90,128]{2,0,1:T(8,128)S(1)}, f32[24,90,128]{2,0,1:T(8,128)}, u32[]{:S(2)}) copy-start(f32[24,90,128]{2,0,1:T(8,128)} %param.10) | copy-start | bytes 3317764
  0.7 14.9 %copy-start.3 = (f32[24,90,128]{2,0,1:T(8,128)S(1)}, f32[24,90,128]{2,0,1:T(8,128)}, u32[]{:S(2)}) copy-start(f32[24,90,128]{2,0,1:T(8,128)} %param.11) | copy-start | bytes 3317764
  3.3 12.3 %copy-start = (f32[24,90,128]{2,0,1:T(8,128)S(1)}, f32[24,90,128]{2,0,1:T(8,128)}, u32[]{:S(2)}) copy-start(f32[24,90,128]{2,0,1:T(8,128)} %param.9) | copy-start | bytes 3317764
  3.3 12.3 %collective-permute-start.4 = (f32[2,90,128]{2,1,0:T(8,128)}, f32[2,90,128]{2,1,0:T(8,128)S(1)}, u32[]{:S(2)}, u32[]{:S(2)}) collective-permute-start(f32[2,90,128]{2,1,0:T(8,128)} %get-tuple-element.24), channel_id=1, source_target_pairs={{0,128},{8,136},{16,144},{24,152},{32,160},{40,168},{48,176},{56,1... | collective-permute-start | bytes 276488 | tf_op jit(solution)/shard_map/ppermute | solution.py:476
  4.9 8.4 %collective-permute-start.2 = (f32[3,24,128]{2,1,0:T(8,128)}, f32[3,24,128]{2,1,0:T(8,128)S(1)}, u32[]{:S(2)}, u32[]{:S(2)}) collective-permute-start(f32[3,24,128]{2,1,0:T(8,128)} %get-tuple-element.22), channel_id=1, source_target_pairs={{8,0},{16,8},{24,16},{32,24},{40,32},{48,40},{56,48},{64,56},{72,6... | collective-permute-start | bytes 110600 | tf_op jit(solution)/shard_map/ppermute | solution.py:474
  9.8 5.7 %collective-permute-start.3 = (f32[3,24,128]{2,1,0:T(8,128)}, f32[3,24,128]{2,1,0:T(8,128)S(1)}, u32[]{:S(2)}, u32[]{:S(2)}) collective-permute-start(f32[3,24,128]{2,1,0:T(8,128)} %get-tuple-element.23), channel_id=1, source_target_pairs={{0,8},{8,16},{16,24},{24,32},{32,40},{40,48},{48,56},{56,64},{64,7... | collective-permute-start | bytes 110600 | tf_op jit(solution)/shard_map/ppermute | solution.py:475
  11.3 8.2 %collective-permute-start = (f32[16,24,128]{2,1,0:T(8,128)S(1)}, f32[16,24,128]{2,1,0:T(8,128)S(1)}, u32[]{:S(2)}, u32[]{:S(2)}) collective-permute-start(f32[16,24,128]{2,1,0:T(8,128)S(1)} %get-tuple-element.20), channel_id=1, source_target_pairs={{0,1},{7,6},{8,9},{15,14},{16,17},{23,22},{24,25},{31,30},{32,33},... | collective-permute-start | bytes 589832 | tf_op jit(solution)/shard_map/ppermute | solution.py:445
  12.0 9.9 %collective-permute-start.1 = (f32[16,24,128]{2,1,0:T(8,128)S(1)}, f32[16,24,128]{2,1,0:T(8,128)S(1)}, u32[]{:S(2)}, u32[]{:S(2)}) collective-permute-start(f32[16,24,128]{2,1,0:T(8,128)S(1)} %get-tuple-element.21), channel_id=1, source_target_pairs={{0,3},{7,4},{8,11},{15,12},{16,19},{23,20},{24,27},{31,28},{32,35}... | collective-permute-start | bytes 589832 | tf_op jit(solution)/shard_map/ppermute | solution.py:445
  17.5 4.4 %collective-permute-start.5 = (f32[16,24,128]{2,1,0:T(8,128)S(1)}, f32[16,24,128]{2,1,0:T(8,128)S(1)}, u32[]{:S(2)}, u32[]{:S(2)}) collective-permute-start(f32[16,24,128]{2,1,0:T(8,128)S(1)} %get-tuple-element.26), channel_id=1, source_target_pairs={{0,1},{7,6},{8,9},{15,14},{16,17},{23,22},{24,25},{31,30},{32,33},... | collective-permute-start | bytes 589832 | tf_op jit(solution)/shard_map/ppermute | solution.py:445
  18.2 8.8 %collective-permute-start.6 = (f32[16,24,128]{2,1,0:T(8,128)S(1)}, f32[16,24,128]{2,1,0:T(8,128)S(1)}, u32[]{:S(2)}, u32[]{:S(2)}) collective-permute-start(f32[16,24,128]{2,1,0:T(8,128)S(1)} %get-tuple-element.27), channel_id=1, source_target_pairs={{0,3},{7,4},{8,11},{15,12},{16,19},{23,20},{24,27},{31,28},{32,35}... | collective-permute-start | bytes 589832 | tf_op jit(solution)/shard_map/ppermute | solution.py:445
  26.9 21.1 %copy-start.4 = (f32[2,17,24,128]{3,2,1,0:T(8,128)S(1)}, f32[2,17,24,128]{3,2,1,0:T(8,128)}, u32[]{:S(2)}) copy-start(f32[2,17,24,128]{3,2,1,0:T(8,128)} %constant.15.clone.back_twiddle) | copy-start | bytes 1253380
  27.0 21.1 %copy-start.5 = (f32[2,17,24,128]{3,2,1,0:T(8,128)S(1)}, f32[2,17,24,128]{3,2,1,0:T(8,128)}, u32[]{:S(2)}) copy-start(f32[2,17,24,128]{3,2,1,0:T(8,128)} %constant.14.clone.twiddle) | copy-start | bytes 1253380
  27.0 21.1 %copy-start.6 = (f32[2,192,192]{2,1,0:T(8,128)S(1)}, f32[2,192,192]{2,1,0:T(8,128)}, u32[]{:S(2)}) copy-start(f32[2,192,192]{2,1,0:T(8,128)} %constant.13.clone.backward) | copy-start | bytes 884740
  27.0 21.1 %copy-start.7 = (f32[2,192,192]{2,1,0:T(8,128)S(1)}, f32[2,192,192]{2,1,0:T(8,128)}, u32[]{:S(2)}) copy-start(f32[2,192,192]{2,1,0:T(8,128)} %constant.12.clone.forward) | copy-start | bytes 884740
  48.0 22.8 %copy-start.10 = (f32[3,90,128]{2,1,0:T(8,128)S(1)}, f32[3,90,128]{2,1,0:T(8,128)}, u32[]{:S(2)}) copy-start(f32[3,90,128]{2,1,0:T(8,128)} %get-tuple-element.28) | copy-start | bytes 414724
  48.0 28.7 %copy-start.9 = (f32[3,90,128]{2,1,0:T(8,128)S(1)}, f32[3,90,128]{2,1,0:T(8,128)}, u32[]{:S(2)}) copy-start(f32[3,90,128]{2,1,0:T(8,128)} %get-tuple-element.29) | copy-start | bytes 414724
  68.7 18.7 %collective-permute-start.8 = (f32[32,24,128]{2,1,0:T(8,128)S(1)}, f32[32,24,128]{2,1,0:T(8,128)S(1)}, u32[]{:S(2)}, u32[]{:S(2)}) collective-permute-start(f32[32,24,128]{2,1,0:T(8,128)S(1)} %all_to_all.11.ret0), channel_id=1, source_target_pairs={{3,0},{4,7},{11,8},{12,15},{19,16},{20,23},{27,24},{28,31},{35,32}... | collective-permute-start | bytes 1179656 | tf_op jit(solution)/shard_map/ppermute | solution.py:445
  70.2 17.3 %collective-permute-start.7 = (f32[32,24,128]{2,1,0:T(8,128)S(1)}, f32[32,24,128]{2,1,0:T(8,128)S(1)}, u32[]{:S(2)}, u32[]{:S(2)}) collective-permute-start(f32[32,24,128]{2,1,0:T(8,128)S(1)} %all_to_all.11.ret0), channel_id=1, source_target_pairs={{1,0},{6,7},{9,8},{14,15},{17,16},{22,23},{25,24},{30,31},{33,32},... | collective-permute-start | bytes 1179656 | tf_op jit(solution)/shard_map/ppermute | solution.py:445
  70.9 9.6 %collective-permute-start.9 = (f32[3,90,128]{2,1,0:T(8,128)S(1)}, f32[3,90,128]{2,1,0:T(8,128)S(1)}, u32[]{:S(2)}, u32[]{:S(2)}) collective-permute-start(f32[3,90,128]{2,1,0:T(8,128)S(1)} %copy-done.10), channel_id=1, source_target_pairs={{0,1},{1,2},{2,3},{3,4},{4,5},{5,6},{6,7},{8,9},{9,10},{10,11},{11... | collective-permute-start | bytes 414728 | tf_op jit(solution)/shard_map/ppermute | solution.py:478
  76.8 10.7 %collective-permute-start.10 = (f32[3,90,128]{2,1,0:T(8,128)S(1)}, f32[3,90,128]{2,1,0:T(8,128)S(1)}, u32[]{:S(2)}, u32[]{:S(2)}) collective-permute-start(f32[3,90,128]{2,1,0:T(8,128)S(1)} %copy-done.9), channel_id=1, source_target_pairs={{1,0},{2,1},{3,2},{4,3},{5,4},{6,5},{7,6},{9,8},{10,9},{11,10},{12... | collective-permute-start | bytes 414728 | tf_op jit(solution)/shard_map/ppermute | solution.py:479

commit v2 on v1

--- a/solution.py
+++ b/solution.py
@@ -109,8 +109,7 @@
     cuts = jnp.zeros((WINDOW, LEV), F32)
     for k in range(POLAR):
         cuts = jnp.where(place == first + k, cutoff[start_of(lat) + k].astype(F32), cuts)
-    for j in range(COLS, PAD - 1):
-        slabs[j] = jnp.zeros((WINDOW, LEV), F32)
+    slabs[PAD - 2] = jnp.zeros((WINDOW, LEV), F32)
     slabs[PAD - 1] = cuts
     for k in range(POLAR):
         parts = [line_of(slabs, first + k, SUB, SUB * s) for s in range(4)]
@@ -118,28 +117,29 @@
             outs[k // 4][4 * (k % 4) + q] = part
 
 
-def borders(
-    lat, t0, t1, c0, c1, u0, u1, tt0, tt1, ct0, ct1, vt0, vt1, first_cols, last_cols, first_rows, last_rows, edge
-):
-    for i, (first_col, last_col) in enumerate(((t0, t1), (c0, c1), (u0, u1))):
-        first_cols[i] = first_col[0]
-        last_cols[i] = last_col[0]
-    for i, (first_tile, last_tile) in enumerate(((tt0, tt1), (ct0, ct1), (vt0, vt1))):
-        first_rows[i] = line_of(first_tile, 0)
-        last_rows[i] = line_of(last_tile, 7)
-    is0 = lat[0] == 0
-    for i, j in enumerate((0, 2)):
-        edge[i] = jnp.where(is0, first_rows[j], last_rows[j])
-
-
-def pack_cotangent(lat, cutoff, ct, out0, out1, out2, slabs):
+def pole_row(lat, tr, wv, edge):
+    outer = jnp.where(lat[0] == 0, 0, 7)
+    edge[0] = line_of(tr, outer)
+    edge[1] = line_of(wv, outer)
+
+
+def pack_cotangent(lat, cutoff, ct, out0, out1, out2, cols, border, slabs):
     rows = pl.ds(window_of(lat), WINDOW)
     for j in range(COLS):
         slabs[j] = ct[j, rows, :]
+    for j in range(COLS, PAD - 2):
+        slabs[j] = jnp.zeros((WINDOW, LEV), F32)
     pack_rows(lat, cutoff, slabs, (out0, out1, out2))
-
-
-def pack_stepped(lat, cutoff, tr, wu, wv, he, hw, ac, out0, out1, out2, slabs):
+    cols[0] = ct[0]
+    cols[1] = ct[COLS - 1]
+    border[0] = line_of(ct, 0)
+    border[1] = line_of(ct, ROWS - 1)
+
+
+def pack_stepped(
+    lat, cutoff, tr, wu, wv, ac, ct_cols, ct_rows,
+    out0, out1, out2, first_cols, last_cols, first_rows, last_rows, slabs,
+):
     rows = pl.ds(window_of(lat), WINDOW)
 
     def step(j, east, west):
@@ -159,10 +159,23 @@
             step(j, tr[j + 1, rows, :], tr[j - 1, rows, :])
         return carry
 
-    step(0, tr[1, rows, :], hw[0, rows, :])
+    nothing = jnp.zeros((WINDOW, LEV), F32)
+    step(0, tr[1, rows, :], nothing)
     lax.fori_loop(0, (COLS - 2) // 8, middle, 0)
-    step(COLS - 1, he[0, rows, :], tr[COLS - 2, rows, :])
+    step(COLS - 1, nothing, tr[COLS - 2, rows, :])
+    slabs[COLS] = tr[0, rows, :]
+    slabs[COLS + 1] = tr[COLS - 1, rows, :]
+    slabs[COLS + 2] = 0.125 + 0.5 * wu[0, rows, :]
+    slabs[COLS + 3] = 0.125 - 0.5 * wu[COLS - 1, rows, :]
     pack_rows(lat, cutoff, slabs, (out0, out1, out2))
+    for i, (j, out) in enumerate(((0, first_cols), (COLS - 1, last_cols))):
+        out[0] = tr[j]
+        out[1] = ct_cols[i]
+        out[2] = wu[j]
+    first_rows[0] = line_of(tr, 0)
+    last_rows[0] = line_of(tr, ROWS - 1)
+    first_rows[1] = (0.125 - 0.5 * line_of(wv, 0)) * ct_rows[0]
+    last_rows[1] = (0.125 + 0.5 * line_of(wv, ROWS - 1)) * ct_rows[1]
 
 
 def times(a, cos, sin):
@@ -265,13 +278,24 @@
         copy.wait()
 
 
-def keep_low(x, forward, backward, twiddle, back_twiddle, out, lines, rhs):
+def keep_low(x, forward, backward, twiddle, back_twiddle, out, lines, rhs, added):
     lane = lax.broadcasted_iota(jnp.int32, (8, LEV), 1)
     spot = lax.broadcasted_iota(jnp.int32, (8, LEV), 0)
     cut = jnp.max(jnp.where((lane >= 96) & (spot == 7), x[0, SUB - 8 : SUB, :], 0.0))
+    wide = lax.broadcasted_iota(jnp.int32, (LON, LEV), 1)
+    from_west = line_of(x, 20, LON) * pltpu.roll(line_of(x, 19, LON), 1, 0)
+    added[0] = jnp.where(wide < 32, pltpu.roll(from_west, 32, 1), 0.0)
+    from_east = line_of(x, 21, LON) * pltpu.roll(line_of(x, 18, LON), LON - 1, 0)
+    added[1] = jnp.where(wide >= 96, from_east, 0.0)
     for i in range(SUB // 8):
         at = slice(8 * i, 8 * i + 8)
-        modes = real_dft([x[b, at, :] for b in range(LON)])
+        values = [x[b, at, :] for b in range(LON)]
+        if i != 1:
+            values = [
+                v + jnp.where(spot == i // 2, added[i // 2, b : b + 1, :], 0.0)
+                for b, v in enumerate(values)
+            ]
+        modes = real_dft(values)
         for k, mode in enumerate(modes):
             re, im = times(mode, twiddle[0, k, at, :], twiddle[1, k, at, :])
             lines[0, k, at, :] = re
@@ -315,121 +339,104 @@
 
 def outputs(
     lat, ret0, ret1, ret2, tr, wu, wv, ct, he, hw, n3, s3, ac,
-    adv, gt, gu, gv, adjoint, low_stepped, top, bottom,
+    adv, gt, gu, gv, adjoint, low_stepped, top, bottom, adv_all, gt_all, gu_all, gv_all, sems,
 ):
     is0, is7 = lat[0] == 0, lat[0] == LAT - 1
-    step = pl.program_id(0)
     rets = (ret0, ret1, ret2)
     start = start_of(lat)
 
-    @pl.when(step == 0)
+    def fill(i, carry):
+        for m in range(10):
+            adjoint[10 * i + m] = ct[10 * i + m]
+        return carry
+
+    lax.fori_loop(0, COLS // 10, fill, 0)
+    adjoint[COLS] = he[1]
+    adjoint[COLS + 1] = hw[1]
+
+    @pl.when(is0 | is7)
     def _():
-        def fill(i, carry):
-            for m in range(10):
-                adjoint[10 * i + m] = ct[10 * i + m]
-            return carry
-
-        lax.fori_loop(0, COLS // 10, fill, 0)
-        adjoint[COLS] = he[1]
-        adjoint[COLS + 1] = hw[1]
-
-        @pl.when(is0 | is7)
-        def _():
-            flat = adjoint.reshape(PAD * ROWS, LEV)
-            flat_stepped = low_stepped.reshape(PAD * ROWS, LEV)
-            for k in range(POLAR):
-                ret, kk = rets[k // 4], k % 4
-                for target, base in ((flat, 0), (flat_stepped, 16)):
-                    line = swap_blocks([ret[base + 4 * kk + q] for q in range(4)])
-                    for s, part in enumerate(line):
-                        target[pl.ds(SUB * s * ROWS + start + k, SUB, stride=ROWS), :] = part
-
-        outer = jnp.where(is0, 0, ROWS - 1)
-        mean = adjoint[COLS + 2, pl.ds(outer, 1), :]
-        opposite = 2.0 * mean - line_of(adjoint, outer)
-        top[0] = jnp.where(is0, ac[0], n3[0])
-        top[1] = jnp.where(is0, (0.125 - 0.5 * ac[1]) * opposite, (0.125 + 0.5 * n3[2]) * n3[1])
-        bottom[0] = jnp.where(is7, ac[0], s3[0])
-        bottom[1] = jnp.where(is7, (0.125 + 0.5 * ac[1]) * opposite, (0.125 - 0.5 * s3[2]) * s3[1])
+        flat = adjoint.reshape(PAD * ROWS, LEV)
+        flat_stepped = low_stepped.reshape(PAD * ROWS, LEV)
+        for k in range(POLAR):
+            ret, kk = rets[k // 4], k % 4
+            for target, base in ((flat, 0), (flat_stepped, 16)):
+                line = swap_blocks([ret[base + 4 * kk + q] for q in range(4)])
+                for s, part in enumerate(line):
+                    target[pl.ds(SUB * s * ROWS + start + k, SUB, stride=ROWS), :] = part
+
+    outer = jnp.where(is0, 0, ROWS - 1)
+    mean = adjoint[COLS + 2, pl.ds(outer, 1), :]
+    opposite = 2.0 * mean - line_of(adjoint, outer)
+    top[0] = jnp.where(is0, ac[0], n3[0])
+    top[1] = jnp.where(is0, (0.125 - 0.5 * ac[1]) * opposite, n3[1])
+    bottom[0] = jnp.where(is7, ac[0], s3[0])
+    bottom[1] = jnp.where(is7, (0.125 + 0.5 * ac[1]) * opposite, s3[1])
 
     place = lax.broadcasted_iota(jnp.int32, (ROWS, LEV), 0)
     filtered = (is0 & (place < POLAR)) | (is7 & (place >= ROWS - POLAR))
-    base = step * CHUNK
-
-    for m in range(CHUNK):
-        j = base + m
-        one = pl.ds(j, 1)
+    results = ((adv_all, adv), (gt_all, gt), (gu_all, gu), (gv_all, gv))
+
+    def sent(step, i):
+        block = pl.ds(step * CHUNK, CHUNK)
+        return pltpu.make_async_copy(results[i][0].at[block], results[i][1].at[block], sems.at[step, i])
+
+    for j in range(COLS):
+        one = slice(j, j + 1)
         x, u, v, a = tr[j], wu[j], wv[j], adjoint[j]
-        if m == 0:
-            at_edge = step == 0
-            before = jnp.maximum(j - 1, 0)
-            west = jnp.where(at_edge, hw[0], tr[before])
-            u_west = jnp.where(at_edge, hw[2], wu[before])
-            a_west = adjoint[jnp.where(at_edge, COLS + 1, before)]
-        else:
-            west, u_west, a_west = tr[j - 1], wu[j - 1], adjoint[j - 1]
+        west, u_west, a_west = (
+            (tr[j - 1], wu[j - 1], adjoint[j - 1]) if j else (hw[0], hw[2], adjoint[COLS + 1])
+        )
+        east, u_east = (tr[j + 1], wu[j + 1]) if j < COLS - 1 else (he[0], he[2])
         a_east = adjoint[j + 1]
-        if m == CHUNK - 1:
-            at_edge = j == COLS - 1
-            beyond = jnp.minimum(j + 1, COLS - 1)
-            east = jnp.where(at_edge, he[0], tr[beyond])
-            u_east = jnp.where(at_edge, he[2], wu[beyond])
-        else:
-            east, u_east = tr[j + 1], wu[j + 1]
         north, south = shifted(x, top[0, one, :], bottom[0, one, :])
         across, along = east - west, north - south
         stepped = (
             x - 0.5 * u * across - 0.5 * v * along + 0.125 * (east + west + north + south - 4.0 * x)
         )
-        adv[m] = jnp.where(filtered, low_stepped[j], stepped)
+        adv_all[j] = jnp.where(filtered, low_stepped[j], stepped)
         half = -0.5 * a
-        gu[m] = across * half
-        gv[m] = along * half
+        gu_all[j] = across * half
+        gv_all[j] = along * half
         place_north = jnp.where(
             place == 0, top[1, one, :], pltpu.roll((0.125 + 0.5 * v) * a, 1, 0)
         )
         place_south = jnp.where(
             place == ROWS - 1, bottom[1, one, :], pltpu.roll((0.125 - 0.5 * v) * a, ROWS - 1, 0)
         )
-        gt[m] = (
+        gt_all[j] = (
             0.5 * a
             + (0.125 + 0.5 * u_east) * a_east
             + (0.125 - 0.5 * u_west) * a_west
             + place_north
             + place_south
         )
+        if j % CHUNK == CHUNK - 1:
+            for i in range(4):
+                sent(j // CHUNK, i).start()
+    for step in range(COLS // CHUNK):
+        for i in range(4):
+            sent(step, i).wait()
 
 
 def whole(*shape):
     return pl.BlockSpec(shape, lambda i, *m: (0,) * len(shape))
 
 
-def column(j):
-    return pl.BlockSpec((1, ROWS, LEV), lambda i, *m: (j, 0, 0))
-
-
-FULL = whole(COLS, ROWS, LEV)
-FIRST_TILES = pl.BlockSpec((COLS, 8, LEV), lambda i, *m: (0, 0, 0))
-LAST_TILES = pl.BlockSpec((COLS, 8, LEV), lambda i, *m: (0, ROWS // 8 - 1, 0))
 OUTER_TILES = pl.BlockSpec(
     (COLS, 8, LEV), lambda i, lat, *m: (0, jnp.where(lat[0] == 0, 0, ROWS // 8 - 1), 0)
 )
-OUT = pl.BlockSpec((CHUNK, ROWS, LEV), lambda i, *m: (i, 0, 0))
-LINES = whole(16, SUB, LEV)
-UNITS = whole(32, SUB, LEV)
 EDGE = whole(2, COLS, LEV)
-SIDE = whole(3, ROWS, LEV)
-BAND = whole(3, COLS, LEV)
 ANYWHERE = pl.BlockSpec(memory_space=pl.ANY)
 
 
-def call(kernel, name, scalars, in_specs, outs, cost, scratch=(), grid=1, vmem=VMEM):
+def call(kernel, name, scalars, in_specs, outs, cost, scratch=(), vmem=VMEM):
     return pl.pallas_call(
         kernel,
         name=name,
         grid_spec=pltpu.PrefetchScalarGridSpec(
             num_scalar_prefetch=scalars,
-            grid=(grid,),
+            grid=(1,),
             in_specs=in_specs,
             out_specs=[spec for _, spec in outs],
             scratch_shapes=list(scratch),
@@ -440,6 +447,20 @@
     )
 
 
+def local_call(kernel, name, scalars, inputs, shapes, cost, scratch=(), out_space=pltpu.VMEM):
+    return pl.pallas_call(
+        kernel,
+        name=name,
+        in_specs=[pl.BlockSpec(memory_space=pltpu.SMEM)] * scalars
+        + [pl.BlockSpec(memory_space=pltpu.VMEM)] * inputs,
+        out_specs=[pl.BlockSpec(memory_space=out_space)] * len(shapes),
+        scratch_shapes=list(scratch),
+        out_shape=[jax.ShapeDtypeStruct(shape, F32) for shape in shapes],
+        compiler_params=pltpu.CompilerParams(vmem_limit_bytes=VMEM),
+        cost_estimate=pl.CostEstimate(flops=cost, bytes_accessed=cost, transcendentals=0),
+    )
+
+
 def moved(x, pairs):
     full = [(lon * LAT + a, lon * LAT + b) for lon in range(LON) for a, b in pairs]
     return lax.ppermute(x, ("lon", "lat"), full)
@@ -453,42 +474,40 @@
     tracer, wind_u, wind_v, cotangent = (
         jnp.transpose(f, (1, 0, 2)) for f in (tracer, wind_u, wind_v, cotangent)
     )
-    chunks = [((16, SUB, LEV), LINES)] * 3
+    chunk = (16, SUB, LEV)
     slabs = pltpu.VMEM((PAD, WINDOW, LEV), F32)
 
-    first_cols, last_cols, first_rows, last_rows, edge = call(
-        borders,
-        "borders",
+    border = ((2, COLS, LEV), EDGE)
+    (edge,) = call(
+        pole_row, "pole_row", 1, [OUTER_TILES] * 2, [border], 1_000_000, vmem=60 * 1024 * 1024
+    )(lat, tracer, wind_v)
+    across = lax.ppermute(edge, "lon", opposite)
+    *cot, ct_cols, ct_rows = local_call(
+        pack_cotangent,
+        "pack_cotangent",
+        2,
         1,
-        [column(0), column(COLS - 1)] * 3 + [FIRST_TILES, LAST_TILES] * 3,
-        [((3, ROWS, LEV), SIDE)] * 2 + [((3, COLS, LEV), BAND)] * 2 + [((2, COLS, LEV), EDGE)],
+        [chunk] * 3 + [(2, ROWS, LEV), (2, COLS, LEV)],
         1_000_000,
-        vmem=60 * 1024 * 1024,
-    )(
-        lat, tracer, tracer, cotangent, cotangent, wind_u, wind_u,
-        tracer, tracer, cotangent, cotangent, wind_v, wind_v,
-    )
-    cot = call(pack_cotangent, "pack_cotangent", 2, [FULL], chunks, 1_000_000, [slabs])(
-        lat, cutoff, cotangent
-    )
+        [slabs],
+    )(lat, cutoff, cotangent)
+    cot_a, cot_b = moved(cot[1], SPREAD_A), moved(cot[2], SPREAD_B)
+
+    *step, first_cols, last_cols, first_rows, last_rows = local_call(
+        pack_stepped,
+        "pack_stepped",
+        2,
+        6,
+        [chunk] * 3 + [(3, ROWS, LEV)] * 2 + [(2, COLS, LEV)] * 2,
+        3_000_000,
+        [slabs],
+    )(lat, cutoff, tracer, wind_u, wind_v, across, ct_cols, ct_rows)
+    step_a, step_b = moved(step[1], SPREAD_A), moved(step[2], SPREAD_B)
     east = lax.ppermute(first_cols, "lon", back_ring)
     west = lax.ppermute(last_cols, "lon", ring)
-    across = lax.ppermute(edge, "lon", opposite)
     down = [(i, i + 1) for i in range(LAT - 1)]
     north = lax.ppermute(last_rows, "lat", down)
     south = lax.ppermute(first_rows, "lat", [(b, a) for a, b in down])
-    cot_a, cot_b = moved(cot[1], SPREAD_A), moved(cot[2], SPREAD_B)
-
-    step = call(
-        pack_stepped,
-        "pack_stepped",
-        2,
-        [FULL] * 3 + [SIDE, SIDE, EDGE],
-        chunks,
-        3_000_000,
-        [slabs],
-    )(lat, cutoff, tracer, wind_u, wind_v, east, west, across)
-    step_a, step_b = moved(step[1], SPREAD_A), moved(step[2], SPREAD_B)
     (lines,) = call(
         pick, "pick", 1, [ANYWHERE] * 6, [((32, SUB, LEV), ANYWHERE)], 500_000,
         [pltpu.SemaphoreType.DMA((2,))],
@@ -503,6 +522,7 @@
         scratch_shapes=[
             pltpu.VMEM((2, MODES, SUB, LEV), F32),
             pltpu.VMEM((2 * PAD, LEV * GROUPS), F32),
+            pltpu.VMEM((2, LON, LEV), F32),
         ],
         compiler_params=pltpu.CompilerParams(vmem_limit_bytes=VMEM),
         cost_estimate=pl.CostEstimate(flops=5_000_000, bytes_accessed=3_000_000, transcendentals=0),
@@ -511,15 +531,19 @@
     back_a = moved(back, [(b, a) for a, b in SPREAD_A])
     back_b = moved(back, [(b, a) for a, b in SPREAD_B])
 
-    results = call(
+    whole_block = (COLS, ROWS, LEV)
+    results = local_call(
         outputs,
         "outputs",
         1,
-        [UNITS] * 3 + [FULL] * 4 + [SIDE, SIDE, BAND, BAND, EDGE],
-        [((COLS, ROWS, LEV), OUT)] * 4,
+        12,
+        [whole_block] * 4,
         9_000_000,
-        [pltpu.VMEM((PAD, ROWS, LEV), F32)] * 2 + [pltpu.VMEM((2, COLS, LEV), F32)] * 2,
-        grid=COLS // CHUNK,
+        [pltpu.VMEM((PAD, ROWS, LEV), F32)] * 2
+        + [pltpu.VMEM((2, COLS, LEV), F32)] * 2
+        + [pltpu.VMEM(whole_block, F32)] * 4
+        + [pltpu.SemaphoreType.DMA((COLS // CHUNK, 4))],
+        out_space=pl.ANY,
     )(
         lat, back, back_a, back_b, tracer, wind_u, wind_v, cotangent, east, west, north, south, across,
     )

time: 91.5 us -> 90.3 us (0.987)
  the two profiles are of different devices: /device:TPU:6 before, /device:TPU:16 now
where the time goes in v2:
time: 90.3 us; the launch traced here: 89.9 us
  blocking collectives  43.6 us (48%)
  starting transfers between devices  17.9 us (20%)
  waiting for transfers between devices  16 us (18%)
  Pallas kernels  10.4 us (12%)
  local copies, waits for them, and re-layouts  1.28 us (1%)
    all_to_all x1, blocking collectives, body(): lines = lax.all_to_all(lines, 'lon', 0, 0, tiled=True)  24.7 us
    all_to_all x1, blocking collectives, body(): back = lax.all_to_all(low, 'lon', 0, 0, tiled=True)  18.9 us
    ppermute x6, waiting for transfers between devices, moved(): return lax.ppermute(x, ('lon', 'lat'), full)  9.71 us
    ppermute x1, starting transfers between devices, body(): south = lax.ppermute(first_rows, 'lat', [(b, a) for a, b in down])  7.54 us
    ppermute x6, starting transfers between devices, moved(): return lax.ppermute(x, ('lon', 'lat'), full)  6.07 us
    ppermute x1, waiting for transfers between devices, body(): west = lax.ppermute(last_cols, 'lon', ring)  4.54 us
    pallas_call x1, Pallas kernels, body(): local_call(outputs, 'outputs', 1, 12, [whole_block] * 4, 9000000, [pltpu....  2.72 us
    pallas_call x1, Pallas kernels, body(): local_call(pack_stepped, 'pack_stepped', 2, 6, [chunk] * 3 + [(3, ROWS, L...  1.94 us
  transfers between devices with their start and end apart: 11, of which 5 were waited for; matrix products, arithmetic and copies ran while one was open for 0% of the time, Pallas kernels for 4%

profile of v2, /device:TPU:16, one launch (start us, length us, event | category | flops | bytes accessed | tf_op | source)
XLA Modules:
  0.0 89.9 jit_solution(14993439880104714124)
XLA Ops:
  0.6 0.0 copy-start.2
  0.6 0.0 copy-start.9
  0.7 0.0 copy-start.1
  0.7 1.9 %pole_row.1 = f32[2,90,128]{2,1,0:T(8,128)} custom-call(s32[1]{0:T(128)} %bitcast.lat, f32[90,24,128]{2,1,0:T(8,128)} %bitcast.9, f32[90,24,128]{2,1,0:T(8,128)} %bitcast.12), custom_call_target="tpu_custom_call" | custom-call | flops 1000000 | bytes 1000000 | tf_op jit(solution)/shard_map/pole_row/pallas_call | solution.py:481
  2.6 0.0 copy-start
  2.6 1.3 %collective-permute-start.2 = (f32[2,90,128]{2,1,0:T(8,128)}, f32[2,90,128]{2,1,0:T(8,128)S(1)}, u32[]{:S(2)}, u32[]{:S(2)}) collective-permute-start(f32[2,90,128]{2,1,0:T(8,128)} %pole_row.1), channel_id=1, source_target_pairs={{0,128},{8,136},{16,144},{24,152},{32,160},{40,168},{48,176},{56,1... | collective-permute-start | bytes 276488 | tf_op jit(solution)/shard_map/ppermute | solution.py:484
  3.9 0.0 copy-done.2
  3.9 0.0 copy-done.9
  3.9 1.5 %pack_cotangent.1 = (f32[16,24,128]{2,1,0:T(8,128)S(1)}, f32[16,24,128]{2,1,0:T(8,128)S(1)}, f32[16,24,128]{2,1,0:T(8,128)S(1)}, f32[2,24,128]{2,1,0:T(8,128)S(1)}, f32[2,90,128]{2,1,0:T(8,128)S(1)}) custom-call(s32[1]{0:T(128)} %bitcast.lat, s32[24]{0:T(128)S(1)} %copy-done.9, f32[90,24,128]{2,1,0:T(8,128)S(1)} %bitcast.15), custom_call_target="tpu_custom_call" | custom-call | flops 1000000 | bytes 1000000 | tf_op jit(solution)/shard_map/pack_cotangent/pallas_call | solution.py:485
  5.3 0.7 collective-permute-start
  6.0 1.3 %collective-permute-start.1 = (f32[16,24,128]{2,1,0:T(8,128)S(1)}, f32[16,24,128]{2,1,0:T(8,128)S(1)}, u32[]{:S(2)}, u32[]{:S(2)}) collective-permute-start(f32[16,24,128]{2,1,0:T(8,128)S(1)} %get-tuple-element.22), channel_id=1, source_target_pairs={{0,3},{7,4},{8,11},{15,12},{16,19},{23,20},{24,27},{31,28},{32,35}... | collective-permute-start | bytes 589832 | tf_op jit(solution)/shard_map/ppermute | solution.py:466
  7.3 0.1 collective-permute-done.2.ac
  7.4 0.0 copy-done.1
  7.4 0.0 copy-done
  7.4 0.0 copy-start.3
  7.4 1.2 %copy-done.3 = f32[24,90,128]{2,0,1:T(8,128)S(1)} copy-done((f32[24,90,128]{2,0,1:T(8,128)S(1)}, f32[24,90,128]{2,0,1:T(8,128)}, u32[]{:S(2)}) %copy-start.3) | copy-done | bytes 1105944
  8.7 1.9 %pack_stepped.1 = (f32[16,24,128]{2,1,0:T(8,128)S(1)}, f32[16,24,128]{2,1,0:T(8,128)S(1)}, f32[16,24,128]{2,1,0:T(8,128)S(1)}, f32[3,24,128]{2,1,0:T(8,128)S(1)}...) custom-call(s32[1]{0:T(128)} %bitcast.lat, s32[24]{0:T(128)S(1)} %copy-done.9, ...), custom_call_target="tpu_custom_call" | custom-call | flops 3000000 | bytes 3000000 | tf_op jit(solution)/shard_map/pack_stepped/pallas_call | solution.py:496
  10.6 0.7 collective-permute-start.3
  11.3 1.3 %collective-permute-start.4 = (f32[16,24,128]{2,1,0:T(8,128)S(1)}, f32[16,24,128]{2,1,0:T(8,128)S(1)}, u32[]{:S(2)}, u32[]{:S(2)}) collective-permute-start(f32[16,24,128]{2,1,0:T(8,128)S(1)} %get-tuple-element.27), channel_id=1, source_target_pairs={{0,3},{7,4},{8,11},{15,12},{16,19},{23,20},{24,27},{31,28},{32,35}... | collective-permute-start | bytes 589832 | tf_op jit(solution)/shard_map/ppermute | solution.py:466
  12.6 0.0 collective-permute-done.a_c
  12.6 3.9 %collective-permute-done.1.b_c = f32[16,24,128]{2,1,0:T(8,128)S(1)} collective-permute-done((f32[16,24,128]{2,1,0:T(8,128)S(1)}, f32[16,24,128]{2,1,0:T(8,128)S(1)}, u32[]{:S(2)}, u32[]{:S(2)}) %collective-permute-start.1) | collective-permute-done | bytes 196640 | tf_op jit(solution)/shard_map/ppermute | solution.py:466
  16.5 0.0 collective-permute-done.3.a_s
  16.5 5.8 %collective-permute-done.4.b_s = f32[16,24,128]{2,1,0:T(8,128)S(1)} collective-permute-done((f32[16,24,128]{2,1,0:T(8,128)S(1)}, f32[16,24,128]{2,1,0:T(8,128)S(1)}, u32[]{:S(2)}, u32[]{:S(2)}) %collective-permute-start.4) | collective-permute-done | bytes 196640 | tf_op jit(solution)/shard_map/ppermute | solution.py:466
  22.3 0.0 copy-start.5
  22.3 0.0 copy-start.6
  22.3 0.0 copy-start.7
  22.3 0.0 copy-start.8
  22.3 0.5 pick.1
  22.9 24.7 %all_to_all.10.x = f32[32,24,128]{2,1,0:T(8,128)S(1)} all-to-all(f32[32,24,128]{2,1,0:T(8,128)S(1)} %pick.1), channel_id=1, replica_groups=mesh['lon'=32,'lat'=8] {'lon'}, dimensions={0} | all-to-all | bytes 786432 | tf_op jit(solution)/shard_map/all_to_all | solution.py:515
  47.6 0.0 copy-done.5
  47.6 0.0 copy-done.6
  47.6 0.0 copy-done.7
  47.6 0.0 copy-done.8
  47.6 0.0 copy-start.4
  47.6 1.8 %keep_low.1 = f32[32,24,128]{2,1,0:T(8,128)S(1)} custom-call(f32[32,24,128]{2,1,0:T(8,128)S(1)} %all_to_all.10.x, f32[2,192,192]{2,1,0:T(8,128)S(1)} %copy-done.8, f32[2,192,192]{2,1,0:T(8,128)S(1)} %copy-done.7, f32[2,17,24,128]{3,2,1,0:T(8,128)S(1)} %copy-done.6, f32[2,17,24,128]{3,2,1,0:T(8,128)S(1)} %copy-done.5), custom_call_target="tpu_custom_call" | custom-call | flops 5000000 | bytes 3000000 | tf_op jit(solution)/shard_map/keep_low/pallas_call | solution.py:517
  49.4 18.9 %all_to_all.11.ret0 = f32[32,24,128]{2,1,0:T(8,128)S(1)} all-to-all(f32[32,24,128]{2,1,0:T(8,128)S(1)} %keep_low.1), channel_id=1, replica_groups=mesh['lon'=32,'lat'=8] {'lon'}, dimensions={0} | all-to-all | bytes 786432 | tf_op jit(solution)/shard_map/all_to_all | solution.py:530
  68.3 1.5 %collective-permute-start.6 = (f32[32,24,128]{2,1,0:T(8,128)S(1)}, f32[32,24,128]{2,1,0:T(8,128)S(1)}, u32[]{:S(2)}, u32[]{:S(2)}) collective-permute-start(f32[32,24,128]{2,1,0:T(8,128)S(1)} %all_to_all.11.ret0), channel_id=1, source_target_pairs={{3,0},{4,7},{11,8},{12,15},{19,16},{20,23},{27,24},{28,31},{35,32}... | collective-permute-start | bytes 1179656 | tf_op jit(solution)/shard_map/ppermute | solution.py:466
  69.8 0.7 collective-permute-start.5
  70.4 1.9 %collective-permute-start.9 = (f32[2,90,128]{2,1,0:T(8,128)S(1)}, f32[2,90,128]{2,1,0:T(8,128)S(1)}, u32[]{:S(2)}, u32[]{:S(2)}) collective-permute-start(f32[2,90,128]{2,1,0:T(8,128)S(1)} %get-tuple-element.30), channel_id=1, source_target_pairs={{0,1},{1,2},{2,3},{3,4},{4,5},{5,6},{6,7},{8,9},{9,10},{10,11},{11... | collective-permute-start | bytes 276488 | tf_op jit(solution)/shard_map/ppermute | solution.py:509
  72.4 7.5 %collective-permute-start.10 = (f32[2,90,128]{2,1,0:T(8,128)S(1)}, f32[2,90,128]{2,1,0:T(8,128)S(1)}, u32[]{:S(2)}, u32[]{:S(2)}) collective-permute-start(f32[2,90,128]{2,1,0:T(8,128)S(1)} %get-tuple-element.31), channel_id=1, source_target_pairs={{1,0},{2,1},{3,2},{4,3},{5,4},{6,5},{7,6},{9,8},{10,9},{11,10},{12... | collective-permute-start | bytes 276488 | tf_op jit(solution)/shard_map/ppermute | solution.py:510
  79.9 0.1 collective-permute-start.7
  80.0 1.6 %collective-permute-done.7.he = f32[3,24,128]{2,1,0:T(8,128)S(1)} collective-permute-done((f32[3,24,128]{2,1,0:T(8,128)S(1)}, f32[3,24,128]{2,1,0:T(8,128)S(1)}, u32[]{:S(2)}, u32[]{:S(2)}) %collective-permute-start.7) | collective-permute-done | bytes 36896 | tf_op jit(solution)/shard_map/ppermute | solution.py:506
  81.6 1.0 %collective-permute-start.8 = (f32[3,24,128]{2,1,0:T(8,128)S(1)}, f32[3,24,128]{2,1,0:T(8,128)S(1)}, u32[]{:S(2)}, u32[]{:S(2)}) collective-permute-start(f32[3,24,128]{2,1,0:T(8,128)S(1)} %get-tuple-element.29), channel_id=1, source_target_pairs={{0,8},{8,16},{16,24},{24,32},{32,40},{40,48},{48,56},{56,64},{64,7... | collective-permute-start | bytes 110600 | tf_op jit(solution)/shard_map/ppermute | solution.py:507
  82.6 4.5 %collective-permute-done.8.hw = f32[3,24,128]{2,1,0:T(8,128)S(1)} collective-permute-done((f32[3,24,128]{2,1,0:T(8,128)S(1)}, f32[3,24,128]{2,1,0:T(8,128)S(1)}, u32[]{:S(2)}, u32[]{:S(2)}) %collective-permute-start.8) | collective-permute-done | bytes 36896 | tf_op jit(solution)/shard_map/ppermute | solution.py:507
  87.1 0.0 collective-permute-done.9.n3
  87.1 0.0 collective-permute-done.10.s3
  87.1 0.0 collective-permute-done.6.ret2
  87.2 0.0 collective-permute-done.5.ret1
  87.2 0.0 copy-done.4
  87.2 2.7 %outputs.1 = (f32[90,24,128]{2,1,0:T(8,128)}, f32[90,24,128]{2,1,0:T(8,128)}, f32[90,24,128]{2,1,0:T(8,128)}, f32[90,24,128]{2,1,0:T(8,128)}) custom-call(s32[1]{0:T(128)} %bitcast.lat, f32[32,24,128]{2,1,0:T(8,128)S(1)} %all_to_all.11.ret0, f32[32,24,128]{2,1,0:T(8,128)S(1)} %collective-permute-done.5.ret1, f32[32,24,128]{2,1,0:T(8,128)S(1)} %collective-permute-done.6.ret2, ...), custom_call_target="tpu_custom_call" | custom-call | flops 9000000 | bytes 9000000 | tf_op jit(solution)/shard_map/outputs/pallas_call | solution.py:535
Async XLA Ops:
  0.6 3.2 %copy-start.2 = (f32[24,90,128]{2,0,1:T(8,128)S(1)}, f32[24,90,128]{2,0,1:T(8,128)}, u32[]{:S(2)}) copy-start(f32[24,90,128]{2,0,1:T(8,128)} %param.12) | copy-start | bytes 3317764
  0.6 3.2 %copy-start.9 = (s32[24]{0:T(128)S(1)}, s32[24]{0:T(128)}, u32[]{:S(2)}) copy-start(s32[24]{0:T(128)} %cutoff.3) | copy-start | bytes 292
  0.7 6.8 %copy-start.1 = (f32[24,90,128]{2,0,1:T(8,128)S(1)}, f32[24,90,128]{2,0,1:T(8,128)}, u32[]{:S(2)}) copy-start(f32[24,90,128]{2,0,1:T(8,128)} %param.11) | copy-start | bytes 3317764
  2.6 4.8 %copy-start = (f32[24,90,128]{2,0,1:T(8,128)S(1)}, f32[24,90,128]{2,0,1:T(8,128)}, u32[]{:S(2)}) copy-start(f32[24,90,128]{2,0,1:T(8,128)} %param.9) | copy-start | bytes 3317764
  2.6 4.8 %collective-permute-start.2 = (f32[2,90,128]{2,1,0:T(8,128)}, f32[2,90,128]{2,1,0:T(8,128)S(1)}, u32[]{:S(2)}, u32[]{:S(2)}) collective-permute-start(f32[2,90,128]{2,1,0:T(8,128)} %pole_row.1), channel_id=1, source_target_pairs={{0,128},{8,136},{16,144},{24,152},{32,160},{40,168},{48,176},{56,1... | collective-permute-start | bytes 276488 | tf_op jit(solution)/shard_map/ppermute | solution.py:484
  5.3 7.3 %collective-permute-start = (f32[16,24,128]{2,1,0:T(8,128)S(1)}, f32[16,24,128]{2,1,0:T(8,128)S(1)}, u32[]{:S(2)}, u32[]{:S(2)}) collective-permute-start(f32[16,24,128]{2,1,0:T(8,128)S(1)} %get-tuple-element.21), channel_id=1, source_target_pairs={{0,1},{7,6},{8,9},{15,14},{16,17},{23,22},{24,25},{31,30},{32,33},... | collective-permute-start | bytes 589832 | tf_op jit(solution)/shard_map/ppermute | solution.py:466
  6.0 10.4 %collective-permute-start.1 = (f32[16,24,128]{2,1,0:T(8,128)S(1)}, f32[16,24,128]{2,1,0:T(8,128)S(1)}, u32[]{:S(2)}, u32[]{:S(2)}) collective-permute-start(f32[16,24,128]{2,1,0:T(8,128)S(1)} %get-tuple-element.22), channel_id=1, source_target_pairs={{0,3},{7,4},{8,11},{15,12},{16,19},{23,20},{24,27},{31,28},{32,35}... | collective-permute-start | bytes 589832 | tf_op jit(solution)/shard_map/ppermute | solution.py:466
  7.4 1.2 %copy-start.3 = (f32[24,90,128]{2,0,1:T(8,128)S(1)}, f32[24,90,128]{2,0,1:T(8,128)}, u32[]{:S(2)}) copy-start(f32[24,90,128]{2,0,1:T(8,128)} %param.10) | copy-start | bytes 3317764
  10.6 5.8 %collective-permute-start.3 = (f32[16,24,128]{2,1,0:T(8,128)S(1)}, f32[16,24,128]{2,1,0:T(8,128)S(1)}, u32[]{:S(2)}, u32[]{:S(2)}) collective-permute-start(f32[16,24,128]{2,1,0:T(8,128)S(1)} %get-tuple-element.26), channel_id=1, source_target_pairs={{0,1},{7,6},{8,9},{15,14},{16,17},{23,22},{24,25},{31,30},{32,33},... | collective-permute-start | bytes 589832 | tf_op jit(solution)/shard_map/ppermute | solution.py:466
  11.3 11.0 %collective-permute-start.4 = (f32[16,24,128]{2,1,0:T(8,128)S(1)}, f32[16,24,128]{2,1,0:T(8,128)S(1)}, u32[]{:S(2)}, u32[]{:S(2)}) collective-permute-start(f32[16,24,128]{2,1,0:T(8,128)S(1)} %get-tuple-element.27), channel_id=1, source_target_pairs={{0,3},{7,4},{8,11},{15,12},{16,19},{23,20},{24,27},{31,28},{32,35}... | collective-permute-start | bytes 589832 | tf_op jit(solution)/shard_map/ppermute | solution.py:466
  22.3 25.3 %copy-start.5 = (f32[2,17,24,128]{3,2,1,0:T(8,128)S(1)}, f32[2,17,24,128]{3,2,1,0:T(8,128)}, u32[]{:S(2)}) copy-start(f32[2,17,24,128]{3,2,1,0:T(8,128)} %constant.15.clone.back_twiddle) | copy-start | bytes 1253380
  22.3 25.3 %copy-start.6 = (f32[2,17,24,128]{3,2,1,0:T(8,128)S(1)}, f32[2,17,24,128]{3,2,1,0:T(8,128)}, u32[]{:S(2)}) copy-start(f32[2,17,24,128]{3,2,1,0:T(8,128)} %constant.14.clone.twiddle) | copy-start | bytes 1253380
  22.3 25.3 %copy-start.7 = (f32[2,192,192]{2,1,0:T(8,128)S(1)}, f32[2,192,192]{2,1,0:T(8,128)}, u32[]{:S(2)}) copy-start(f32[2,192,192]{2,1,0:T(8,128)} %constant.13.clone.backward) | copy-start | bytes 884740
  22.3 25.3 %copy-start.8 = (f32[2,192,192]{2,1,0:T(8,128)S(1)}, f32[2,192,192]{2,1,0:T(8,128)}, u32[]{:S(2)}) copy-start(f32[2,192,192]{2,1,0:T(8,128)} %constant.12.clone.forward) | copy-start | bytes 884740
  47.6 39.5 %copy-start.4 = (f32[24,90,128]{2,0,1:T(8,128)S(1)}, f32[24,90,128]{2,0,1:T(8,128)}, u32[]{:S(2)}) copy-start(f32[24,90,128]{2,0,1:T(8,128)} %param.10) | copy-start | bytes 3317764
  68.3 18.9 %collective-permute-start.6 = (f32[32,24,128]{2,1,0:T(8,128)S(1)}, f32[32,24,128]{2,1,0:T(8,128)S(1)}, u32[]{:S(2)}, u32[]{:S(2)}) collective-permute-start(f32[32,24,128]{2,1,0:T(8,128)S(1)} %all_to_all.11.ret0), channel_id=1, source_target_pairs={{3,0},{4,7},{11,8},{12,15},{19,16},{20,23},{27,24},{28,31},{35,32}... | collective-permute-start | bytes 1179656 | tf_op jit(solution)/shard_map/ppermute | solution.py:466
  69.8 17.4 %collective-permute-start.5 = (f32[32,24,128]{2,1,0:T(8,128)S(1)}, f32[32,24,128]{2,1,0:T(8,128)S(1)}, u32[]{:S(2)}, u32[]{:S(2)}) collective-permute-start(f32[32,24,128]{2,1,0:T(8,128)S(1)} %all_to_all.11.ret0), channel_id=1, source_target_pairs={{1,0},{6,7},{9,8},{14,15},{17,16},{22,23},{25,24},{30,31},{33,32},... | collective-permute-start | bytes 1179656 | tf_op jit(solution)/shard_map/ppermute | solution.py:466
  70.4 16.7 %collective-permute-start.9 = (f32[2,90,128]{2,1,0:T(8,128)S(1)}, f32[2,90,128]{2,1,0:T(8,128)S(1)}, u32[]{:S(2)}, u32[]{:S(2)}) collective-permute-start(f32[2,90,128]{2,1,0:T(8,128)S(1)} %get-tuple-element.30), channel_id=1, source_target_pairs={{0,1},{1,2},{2,3},{3,4},{4,5},{5,6},{6,7},{8,9},{9,10},{10,11},{11... | collective-permute-start | bytes 276488 | tf_op jit(solution)/shard_map/ppermute | solution.py:509
  72.4 14.8 %collective-permute-start.10 = (f32[2,90,128]{2,1,0:T(8,128)S(1)}, f32[2,90,128]{2,1,0:T(8,128)S(1)}, u32[]{:S(2)}, u32[]{:S(2)}) collective-permute-start(f32[2,90,128]{2,1,0:T(8,128)S(1)} %get-tuple-element.31), channel_id=1, source_target_pairs={{1,0},{2,1},{3,2},{4,3},{5,4},{6,5},{7,6},{9,8},{10,9},{11,10},{12... | collective-permute-start | bytes 276488 | tf_op jit(solution)/shard_map/ppermute | solution.py:510
  79.9 1.7 %collective-permute-start.7 = (f32[3,24,128]{2,1,0:T(8,128)S(1)}, f32[3,24,128]{2,1,0:T(8,128)S(1)}, u32[]{:S(2)}, u32[]{:S(2)}) collective-permute-start(f32[3,24,128]{2,1,0:T(8,128)S(1)} %get-tuple-element.28), channel_id=1, source_target_pairs={{8,0},{16,8},{24,16},{32,24},{40,32},{48,40},{56,48},{64,56},{72,6... | collective-permute-start | bytes 110600 | tf_op jit(solution)/shard_map/ppermute | solution.py:506
  81.6 5.5 %collective-permute-start.8 = (f32[3,24,128]{2,1,0:T(8,128)S(1)}, f32[3,24,128]{2,1,0:T(8,128)S(1)}, u32[]{:S(2)}, u32[]{:S(2)}) collective-permute-start(f32[3,24,128]{2,1,0:T(8,128)S(1)} %get-tuple-element.29), channel_id=1, source_target_pairs={{0,8},{8,16},{16,24},{24,32},{32,40},{40,48},{48,56},{56,64},{64,7... | collective-permute-start | bytes 110600 | tf_op jit(solution)/shard_map/ppermute | solution.py:507

commit v3 on v2

--- a/solution.py
+++ b/solution.py
@@ -21,10 +21,14 @@
 GROUPS = 5
 VMEM = 32 * 1024 * 1024
 WINDOW = 16
+PITCH = 24
 CHUNK = 15
 
 SPREAD_A = ((0, 1), (7, 6))
 SPREAD_B = ((0, 3), (7, 4))
+EARLY = ((3, 4), (4, 3))
+SOUTHWARD = ((0, 1), (1, 2), (2, 3), (4, 5), (5, 6), (6, 7))
+NORTHWARD = ((1, 0), (2, 1), (3, 2), (5, 4), (6, 5), (7, 6))
 
 
 def dft_tables():
@@ -109,8 +113,8 @@
     cuts = jnp.zeros((WINDOW, LEV), F32)
     for k in range(POLAR):
         cuts = jnp.where(place == first + k, cutoff[start_of(lat) + k].astype(F32), cuts)
-    slabs[PAD - 2] = jnp.zeros((WINDOW, LEV), F32)
-    slabs[PAD - 1] = cuts
+    slabs[PAD - 2, 0:WINDOW, :] = jnp.zeros((WINDOW, LEV), F32)
+    slabs[PAD - 1, 0:WINDOW, :] = cuts
     for k in range(POLAR):
         parts = [line_of(slabs, first + k, SUB, SUB * s) for s in range(4)]
         for q, part in enumerate(swap_blocks(parts)):
@@ -126,9 +130,9 @@
 def pack_cotangent(lat, cutoff, ct, out0, out1, out2, cols, border, slabs):
     rows = pl.ds(window_of(lat), WINDOW)
     for j in range(COLS):
-        slabs[j] = ct[j, rows, :]
+        slabs[j, 0:WINDOW, :] = ct[j, rows, :]
     for j in range(COLS, PAD - 2):
-        slabs[j] = jnp.zeros((WINDOW, LEV), F32)
+        slabs[j, 0:WINDOW, :] = jnp.zeros((WINDOW, LEV), F32)
     pack_rows(lat, cutoff, slabs, (out0, out1, out2))
     cols[0] = ct[0]
     cols[1] = ct[COLS - 1]
@@ -138,7 +142,7 @@
 
 def pack_stepped(
     lat, cutoff, tr, wu, wv, ac, ct_cols, ct_rows,
-    out0, out1, out2, first_cols, last_cols, first_rows, last_rows, slabs,
+    out0, out1, out2, first_cols, last_cols, first_rows, last_rows, early_rows, slabs,
 ):
     rows = pl.ds(window_of(lat), WINDOW)
 
@@ -146,7 +150,7 @@
         x = tr[j, rows, :]
         beyond = ac[0, pl.ds(j, 1), :]
         north, south = shifted(x, beyond, beyond)
-        slabs[j] = (
+        slabs[j, 0:WINDOW, :] = (
             x
             - 0.5 * wu[j, rows, :] * (east - west)
             - 0.5 * wv[j, rows, :] * (north - south)
@@ -163,10 +167,10 @@
     step(0, tr[1, rows, :], nothing)
     lax.fori_loop(0, (COLS - 2) // 8, middle, 0)
     step(COLS - 1, nothing, tr[COLS - 2, rows, :])
-    slabs[COLS] = tr[0, rows, :]
-    slabs[COLS + 1] = tr[COLS - 1, rows, :]
-    slabs[COLS + 2] = 0.125 + 0.5 * wu[0, rows, :]
-    slabs[COLS + 3] = 0.125 - 0.5 * wu[COLS - 1, rows, :]
+    slabs[COLS, 0:WINDOW, :] = tr[0, rows, :]
+    slabs[COLS + 1, 0:WINDOW, :] = tr[COLS - 1, rows, :]
+    slabs[COLS + 2, 0:WINDOW, :] = 0.125 + 0.5 * wu[0, rows, :]
+    slabs[COLS + 3, 0:WINDOW, :] = 0.125 - 0.5 * wu[COLS - 1, rows, :]
     pack_rows(lat, cutoff, slabs, (out0, out1, out2))
     for i, (j, out) in enumerate(((0, first_cols), (COLS - 1, last_cols))):
         out[0] = tr[j]
@@ -176,6 +180,8 @@
     last_rows[0] = line_of(tr, ROWS - 1)
     first_rows[1] = (0.125 - 0.5 * line_of(wv, 0)) * ct_rows[0]
     last_rows[1] = (0.125 + 0.5 * line_of(wv, ROWS - 1)) * ct_rows[1]
+    for i in range(2):
+        early_rows[i] = jnp.where(lat[0] == 3, last_rows[i], first_rows[i])
 
 
 def times(a, cos, sin):
@@ -253,7 +259,7 @@
     return dot(main, high) + (dot(main, low) + dot(rest, high))
 
 
-def pick(lat, own_c, a_c, b_c, own_s, a_s, b_s, out, sems):
+def pick(lat, own_c, a_c, b_c, own_s, a_s, b_s, early, out, sems):
     polar = (lat[0] == 0) | (lat[0] == LAT - 1)
     in_a = (lat[0] == 1) | (lat[0] == LAT - 2)
 
@@ -338,7 +344,7 @@
 
 
 def outputs(
-    lat, ret0, ret1, ret2, tr, wu, wv, ct, he, hw, n3, s3, ac,
+    lat, ret0, ret1, ret2, tr, wu, wv, ct, he, hw, n3, s3, early, ac,
     adv, gt, gu, gv, adjoint, low_stepped, top, bottom, adv_all, gt_all, gu_all, gv_all, sems,
 ):
     is0, is7 = lat[0] == 0, lat[0] == LAT - 1
@@ -368,10 +374,13 @@
     outer = jnp.where(is0, 0, ROWS - 1)
     mean = adjoint[COLS + 2, pl.ds(outer, 1), :]
     opposite = 2.0 * mean - line_of(adjoint, outer)
-    top[0] = jnp.where(is0, ac[0], n3[0])
-    top[1] = jnp.where(is0, (0.125 - 0.5 * ac[1]) * opposite, n3[1])
-    bottom[0] = jnp.where(is7, ac[0], s3[0])
-    bottom[1] = jnp.where(is7, (0.125 + 0.5 * ac[1]) * opposite, s3[1])
+    early_north, early_south = lat[0] == 4, lat[0] == 3
+    tr_north, north = (jnp.where(early_north, early[i], n3[i]) for i in range(2))
+    tr_south, south = (jnp.where(early_south, early[i], s3[i]) for i in range(2))
+    top[0] = jnp.where(is0, ac[0], tr_north)
+    top[1] = jnp.where(is0, (0.125 - 0.5 * ac[1]) * opposite, north)
+    bottom[0] = jnp.where(is7, ac[0], tr_south)
+    bottom[1] = jnp.where(is7, (0.125 + 0.5 * ac[1]) * opposite, south)
 
     place = lax.broadcasted_iota(jnp.int32, (ROWS, LEV), 0)
     filtered = (is0 & (place < POLAR)) | (is7 & (place >= ROWS - POLAR))
@@ -475,7 +484,7 @@
         jnp.transpose(f, (1, 0, 2)) for f in (tracer, wind_u, wind_v, cotangent)
     )
     chunk = (16, SUB, LEV)
-    slabs = pltpu.VMEM((PAD, WINDOW, LEV), F32)
+    slabs = pltpu.VMEM((PAD, PITCH, LEV), F32)
 
     border = ((2, COLS, LEV), EDGE)
     (edge,) = call(
@@ -493,25 +502,24 @@
     )(lat, cutoff, cotangent)
     cot_a, cot_b = moved(cot[1], SPREAD_A), moved(cot[2], SPREAD_B)
 
-    *step, first_cols, last_cols, first_rows, last_rows = local_call(
+    *step, first_cols, last_cols, first_rows, last_rows, early_rows = local_call(
         pack_stepped,
         "pack_stepped",
         2,
         6,
-        [chunk] * 3 + [(3, ROWS, LEV)] * 2 + [(2, COLS, LEV)] * 2,
+        [chunk] * 3 + [(3, ROWS, LEV)] * 2 + [(2, COLS, LEV)] * 3,
         3_000_000,
         [slabs],
     )(lat, cutoff, tracer, wind_u, wind_v, across, ct_cols, ct_rows)
     step_a, step_b = moved(step[1], SPREAD_A), moved(step[2], SPREAD_B)
     east = lax.ppermute(first_cols, "lon", back_ring)
     west = lax.ppermute(last_cols, "lon", ring)
-    down = [(i, i + 1) for i in range(LAT - 1)]
-    north = lax.ppermute(last_rows, "lat", down)
-    south = lax.ppermute(first_rows, "lat", [(b, a) for a, b in down])
+    early = moved(early_rows, EARLY)
+    north, south = moved(last_rows, SOUTHWARD), moved(first_rows, NORTHWARD)
     (lines,) = call(
-        pick, "pick", 1, [ANYWHERE] * 6, [((32, SUB, LEV), ANYWHERE)], 500_000,
+        pick, "pick", 1, [ANYWHERE] * 7, [((32, SUB, LEV), ANYWHERE)], 500_000,
         [pltpu.SemaphoreType.DMA((2,))],
-    )(lat, cot[0], cot_a, cot_b, step[0], step_a, step_b)
+    )(lat, cot[0], cot_a, cot_b, step[0], step_a, step_b, early)
     lines = lax.all_to_all(lines, "lon", 0, 0, tiled=True)
 
     low = pl.pallas_call(
@@ -536,7 +544,7 @@
         outputs,
         "outputs",
         1,
-        12,
+        13,
         [whole_block] * 4,
         9_000_000,
         [pltpu.VMEM((PAD, ROWS, LEV), F32)] * 2
@@ -545,7 +553,8 @@
         + [pltpu.SemaphoreType.DMA((COLS // CHUNK, 4))],
         out_space=pl.ANY,
     )(
-        lat, back, back_a, back_b, tracer, wind_u, wind_v, cotangent, east, west, north, south, across,
+        lat, back, back_a, back_b, tracer, wind_u, wind_v, cotangent, east, west, north, south,
+        early, across,
     )
     return [jnp.transpose(r, (1, 0, 2)) for r in results]
 

time: 90.3 us -> 87.8 us (0.972)
  the two profiles are of different devices: /device:TPU:16 before, /device:TPU:6 now
where the time goes in v3:
time: 87.8 us; the launch traced here: 87.4 us
  blocking collectives  44.2 us (50%)
  starting transfers between devices  19.2 us (22%)
  waiting for transfers between devices  11.5 us (13%)
  Pallas kernels  10.3 us (12%)
  local copies, waits for them, and re-layouts  1.29 us (1%)
  between operations  0.89 us (1%)
    all_to_all x1, blocking collectives, body(): lines = lax.all_to_all(lines, 'lon', 0, 0, tiled=True)  25.4 us
    all_to_all x1, blocking collectives, body(): back = lax.all_to_all(low, 'lon', 0, 0, tiled=True)  18.9 us
    ppermute x9, starting transfers between devices, moved(): return lax.ppermute(x, ('lon', 'lat'), full)  16.6 us
    ppermute x9, waiting for transfers between devices, moved(): return lax.ppermute(x, ('lon', 'lat'), full)  5.33 us
    ppermute x1, waiting for transfers between devices, body(): west = lax.ppermute(last_cols, 'lon', ring)  4.54 us
    pallas_call x1, Pallas kernels, body(): local_call(outputs, 'outputs', 1, 13, [whole_block] * 4, 9000000, [pltpu....  2.72 us
    pallas_call x1, Pallas kernels, body(): local_call(pack_stepped, 'pack_stepped', 2, 6, [chunk] * 3 + [(3, ROWS, L...  1.93 us
    pallas_call x1, Pallas kernels, body(): call(pole_row, 'pole_row', 1, [OUTER_TILES] * 2, [border], 1000000, vmem=...  1.93 us
  transfers between devices with their start and end apart: 12, of which 3 were waited for; matrix products, arithmetic and copies ran while one was open for 0% of the time, Pallas kernels for 4%

profile of v3, /device:TPU:6, one launch (start us, length us, event | category | flops | bytes accessed | tf_op | source)
XLA Modules:
  0.0 87.4 jit_solution(13680207925033125969)
XLA Ops:
  0.6 0.0 copy-start.2
  0.6 0.0 copy-start.9
  0.7 0.0 copy-start.1
  0.7 1.9 %pole_row.1 = f32[2,90,128]{2,1,0:T(8,128)} custom-call(s32[1]{0:T(128)} %bitcast.lat, f32[90,24,128]{2,1,0:T(8,128)} %bitcast.9, f32[90,24,128]{2,1,0:T(8,128)} %bitcast.12), custom_call_target="tpu_custom_call" | custom-call | flops 1000000 | bytes 1000000 | tf_op jit(solution)/shard_map/pole_row/pallas_call | solution.py:490
  2.6 0.0 copy-start
  2.6 1.6 %collective-permute-start.2 = (f32[2,90,128]{2,1,0:T(8,128)}, f32[2,90,128]{2,1,0:T(8,128)S(1)}, u32[]{:S(2)}, u32[]{:S(2)}) collective-permute-start(f32[2,90,128]{2,1,0:T(8,128)} %pole_row.1), channel_id=1, source_target_pairs={{0,128},{8,136},{16,144},{24,152},{32,160},{40,168},{48,176},{56,1... | collective-permute-start | bytes 276488 | tf_op jit(solution)/shard_map/ppermute | solution.py:493
  4.2 0.0 copy-done.2
  4.2 0.0 copy-done.9
  4.2 1.4 %pack_cotangent.1 = (f32[16,24,128]{2,1,0:T(8,128)S(1)}, f32[16,24,128]{2,1,0:T(8,128)S(1)}, f32[16,24,128]{2,1,0:T(8,128)S(1)}, f32[2,24,128]{2,1,0:T(8,128)S(1)}, f32[2,90,128]{2,1,0:T(8,128)S(1)}) custom-call(s32[1]{0:T(128)} %bitcast.lat, s32[24]{0:T(128)S(1)} %copy-done.9, f32[90,24,128]{2,1,0:T(8,128)S(1)} %bitcast.15), custom_call_target="tpu_custom_call" | custom-call | flops 1000000 | bytes 1000000 | tf_op jit(solution)/shard_map/pack_cotangent/pallas_call | solution.py:494
  5.6 0.7 collective-permute-start
  6.3 1.3 %collective-permute-start.1 = (f32[16,24,128]{2,1,0:T(8,128)S(1)}, f32[16,24,128]{2,1,0:T(8,128)S(1)}, u32[]{:S(2)}, u32[]{:S(2)}) collective-permute-start(f32[16,24,128]{2,1,0:T(8,128)S(1)} %get-tuple-element.23), channel_id=1, source_target_pairs={{0,3},{7,4},{8,11},{15,12},{16,19},{23,20},{24,27},{31,28},{32,35}... | collective-permute-start | bytes 589832 | tf_op jit(solution)/shard_map/ppermute | solution.py:475
  7.6 0.0 collective-permute-done.2.ac
  7.6 0.0 copy-done.1
  7.6 0.0 copy-done
  7.6 0.0 copy-start.3
  7.6 1.2 %copy-done.3 = f32[24,90,128]{2,0,1:T(8,128)S(1)} copy-done((f32[24,90,128]{2,0,1:T(8,128)S(1)}, f32[24,90,128]{2,0,1:T(8,128)}, u32[]{:S(2)}) %copy-start.3) | copy-done | bytes 1105944
  8.9 1.9 %pack_stepped.1 = (f32[16,24,128]{2,1,0:T(8,128)S(1)}, f32[16,24,128]{2,1,0:T(8,128)S(1)}, f32[16,24,128]{2,1,0:T(8,128)S(1)}, f32[3,24,128]{2,1,0:T(8,128)S(1)}...) custom-call(s32[1]{0:T(128)} %bitcast.lat, ...), custom_call_target="tpu_custom_call" | custom-call | flops 3000000 | bytes 3000000 | tf_op jit(solution)/shard_map/pack_stepped/pallas_call | solution.py:505
  10.8 0.7 collective-permute-start.3
  11.5 1.3 %collective-permute-start.4 = (f32[16,24,128]{2,1,0:T(8,128)S(1)}, f32[16,24,128]{2,1,0:T(8,128)S(1)}, u32[]{:S(2)}, u32[]{:S(2)}) collective-permute-start(f32[16,24,128]{2,1,0:T(8,128)S(1)} %get-tuple-element.28), channel_id=1, source_target_pairs={{0,3},{7,4},{8,11},{15,12},{16,19},{23,20},{24,27},{31,28},{32,35}... | collective-permute-start | bytes 589832 | tf_op jit(solution)/shard_map/ppermute | solution.py:475
  12.8 4.8 %collective-permute-start.5 = (f32[2,90,128]{2,1,0:T(8,128)S(1)}, f32[2,90,128]{2,1,0:T(8,128)S(1)}, u32[]{:S(2)}, u32[]{:S(2)}) collective-permute-start(f32[2,90,128]{2,1,0:T(8,128)S(1)} %get-tuple-element.29), channel_id=1, source_target_pairs={{3,4},{4,3},{11,12},{12,11},{19,20},{20,19},{27,28},{28,27},{35,36... | collective-permute-start | bytes 276488 | tf_op jit(solution)/shard_map/ppermute | solution.py:475
  17.6 5.3 %collective-permute-done.5.early = f32[2,90,128]{2,1,0:T(8,128)S(1)} collective-permute-done((f32[2,90,128]{2,1,0:T(8,128)S(1)}, f32[2,90,128]{2,1,0:T(8,128)S(1)}, u32[]{:S(2)}, u32[]{:S(2)}) %collective-permute-start.5) | collective-permute-done | bytes 92192 | tf_op jit(solution)/shard_map/ppermute | solution.py:475
  22.9 0.0 collective-permute-done.a_c
  22.9 0.0 collective-permute-done.1.b_c
  22.9 0.0 collective-permute-done.3.a_s
  22.9 0.0 collective-permute-done.4.b_s
  22.9 0.0 copy-start.5
  23.0 0.0 copy-start.6
  23.0 0.0 copy-start.7
  23.0 0.0 copy-start.8
  23.0 0.5 pick.1
  23.5 25.4 %all_to_all.10.x = f32[32,24,128]{2,1,0:T(8,128)S(1)} all-to-all(f32[32,24,128]{2,1,0:T(8,128)S(1)} %pick.1), channel_id=1, replica_groups=mesh['lon'=32,'lat'=8] {'lon'}, dimensions={0} | all-to-all | bytes 786432 | tf_op jit(solution)/shard_map/all_to_all | solution.py:523
  48.9 0.0 copy-done.5
  48.9 0.0 copy-done.6
  48.9 0.0 copy-done.7
  48.9 0.0 copy-done.8
  48.9 0.0 copy-start.4
  48.9 1.8 %keep_low.1 = f32[32,24,128]{2,1,0:T(8,128)S(1)} custom-call(f32[32,24,128]{2,1,0:T(8,128)S(1)} %all_to_all.10.x, f32[2,192,192]{2,1,0:T(8,128)S(1)} %copy-done.8, f32[2,192,192]{2,1,0:T(8,128)S(1)} %copy-done.7, f32[2,17,24,128]{3,2,1,0:T(8,128)S(1)} %copy-done.6, f32[2,17,24,128]{3,2,1,0:T(8,128)S(1)} %copy-done.5), custom_call_target="tpu_custom_call" | custom-call | flops 5000000 | bytes 3000000 | tf_op jit(solution)/shard_map/keep_low/pallas_call | solution.py:525
  50.7 18.9 %all_to_all.11.ret0 = f32[32,24,128]{2,1,0:T(8,128)S(1)} all-to-all(f32[32,24,128]{2,1,0:T(8,128)S(1)} %keep_low.1), channel_id=1, replica_groups=mesh['lon'=32,'lat'=8] {'lon'}, dimensions={0} | all-to-all | bytes 786432 | tf_op jit(solution)/shard_map/all_to_all | solution.py:538
  69.6 1.3 %collective-permute-start.7 = (f32[32,24,128]{2,1,0:T(8,128)S(1)}, f32[32,24,128]{2,1,0:T(8,128)S(1)}, u32[]{:S(2)}, u32[]{:S(2)}) collective-permute-start(f32[32,24,128]{2,1,0:T(8,128)S(1)} %all_to_all.11.ret0), channel_id=1, source_target_pairs={{3,0},{4,7},{11,8},{12,15},{19,16},{20,23},{27,24},{28,31},{35,32}... | collective-permute-start | bytes 1179656 | tf_op jit(solution)/shard_map/ppermute | solution.py:475
  70.9 0.7 collective-permute-start.6
  71.6 1.3 %collective-permute-start.10 = (f32[2,90,128]{2,1,0:T(8,128)S(1)}, f32[2,90,128]{2,1,0:T(8,128)S(1)}, u32[]{:S(2)}, u32[]{:S(2)}) collective-permute-start(f32[2,90,128]{2,1,0:T(8,128)S(1)} %get-tuple-element.32), channel_id=1, source_target_pairs={{0,1},{1,2},{2,3},{4,5},{5,6},{6,7},{8,9},{9,10},{10,11},{12,13},{... | collective-permute-start | bytes 276488 | tf_op jit(solution)/shard_map/ppermute | solution.py:475
  72.9 4.6 %collective-permute-start.11 = (f32[2,90,128]{2,1,0:T(8,128)S(1)}, f32[2,90,128]{2,1,0:T(8,128)S(1)}, u32[]{:S(2)}, u32[]{:S(2)}) collective-permute-start(f32[2,90,128]{2,1,0:T(8,128)S(1)} %get-tuple-element.33), channel_id=1, source_target_pairs={{1,0},{2,1},{3,2},{5,4},{6,5},{7,6},{9,8},{10,9},{11,10},{13,12},{... | collective-permute-start | bytes 276488 | tf_op jit(solution)/shard_map/ppermute | solution.py:475
  77.5 0.1 collective-permute-start.8
  77.5 1.6 %collective-permute-done.8.he = f32[3,24,128]{2,1,0:T(8,128)S(1)} collective-permute-done((f32[3,24,128]{2,1,0:T(8,128)S(1)}, f32[3,24,128]{2,1,0:T(8,128)S(1)}, u32[]{:S(2)}, u32[]{:S(2)}) %collective-permute-start.8) | collective-permute-done | bytes 36896 | tf_op jit(solution)/shard_map/ppermute | solution.py:515
  79.2 1.0 %collective-permute-start.9 = (f32[3,24,128]{2,1,0:T(8,128)S(1)}, f32[3,24,128]{2,1,0:T(8,128)S(1)}, u32[]{:S(2)}, u32[]{:S(2)}) collective-permute-start(f32[3,24,128]{2,1,0:T(8,128)S(1)} %get-tuple-element.31), channel_id=1, source_target_pairs={{0,8},{8,16},{16,24},{24,32},{32,40},{40,48},{48,56},{56,64},{64,7... | collective-permute-start | bytes 110600 | tf_op jit(solution)/shard_map/ppermute | solution.py:516
  80.1 4.5 %collective-permute-done.9.hw = f32[3,24,128]{2,1,0:T(8,128)S(1)} collective-permute-done((f32[3,24,128]{2,1,0:T(8,128)S(1)}, f32[3,24,128]{2,1,0:T(8,128)S(1)}, u32[]{:S(2)}, u32[]{:S(2)}) %collective-permute-start.9) | collective-permute-done | bytes 36896 | tf_op jit(solution)/shard_map/ppermute | solution.py:516
  84.7 0.0 collective-permute-done.10.n3
  84.7 0.0 collective-permute-done.11.s3
  84.7 0.0 collective-permute-done.7.ret2
  84.7 0.0 collective-permute-done.6.ret1
  84.7 0.0 copy-done.4
  84.7 2.7 %outputs.1 = (f32[90,24,128]{2,1,0:T(8,128)}, f32[90,24,128]{2,1,0:T(8,128)}, f32[90,24,128]{2,1,0:T(8,128)}, f32[90,24,128]{2,1,0:T(8,128)}) custom-call(s32[1]{0:T(128)} %bitcast.lat, f32[32,24,128]{2,1,0:T(8,128)S(1)} %all_to_all.11.ret0, f32[32,24,128]{2,1,0:T(8,128)S(1)} %collective-permute-done.6.ret1, f32[32,24,128]{2,1,0:T(8,128)S(1)} %collective-permute-done.7.ret2, ...), custom_call_target="tpu_custom_call" | custom-call | flops 9000000 | bytes 9000000 | tf_op jit(solution)/shard_map/outputs/pallas_call | solution.py:543
Async XLA Ops:
  0.6 3.5 %copy-start.2 = (f32[24,90,128]{2,0,1:T(8,128)S(1)}, f32[24,90,128]{2,0,1:T(8,128)}, u32[]{:S(2)}) copy-start(f32[24,90,128]{2,0,1:T(8,128)} %param.12) | copy-start | bytes 3317764
  0.6 3.5 %copy-start.9 = (s32[24]{0:T(128)S(1)}, s32[24]{0:T(128)}, u32[]{:S(2)}) copy-start(s32[24]{0:T(128)} %cutoff.3) | copy-start | bytes 292
  0.7 7.0 %copy-start.1 = (f32[24,90,128]{2,0,1:T(8,128)S(1)}, f32[24,90,128]{2,0,1:T(8,128)}, u32[]{:S(2)}) copy-start(f32[24,90,128]{2,0,1:T(8,128)} %param.11) | copy-start | bytes 3317764
  2.6 5.0 %copy-start = (f32[24,90,128]{2,0,1:T(8,128)S(1)}, f32[24,90,128]{2,0,1:T(8,128)}, u32[]{:S(2)}) copy-start(f32[24,90,128]{2,0,1:T(8,128)} %param.9) | copy-start | bytes 3317764
  2.6 5.0 %collective-permute-start.2 = (f32[2,90,128]{2,1,0:T(8,128)}, f32[2,90,128]{2,1,0:T(8,128)S(1)}, u32[]{:S(2)}, u32[]{:S(2)}) collective-permute-start(f32[2,90,128]{2,1,0:T(8,128)} %pole_row.1), channel_id=1, source_target_pairs={{0,128},{8,136},{16,144},{24,152},{32,160},{40,168},{48,176},{56,1... | collective-permute-start | bytes 276488 | tf_op jit(solution)/shard_map/ppermute | solution.py:493
  5.6 17.3 %collective-permute-start = (f32[16,24,128]{2,1,0:T(8,128)S(1)}, f32[16,24,128]{2,1,0:T(8,128)S(1)}, u32[]{:S(2)}, u32[]{:S(2)}) collective-permute-start(f32[16,24,128]{2,1,0:T(8,128)S(1)} %get-tuple-element.22), channel_id=1, source_target_pairs={{0,1},{7,6},{8,9},{15,14},{16,17},{23,22},{24,25},{31,30},{32,33},... | collective-permute-start | bytes 589832 | tf_op jit(solution)/shard_map/ppermute | solution.py:475
  6.3 16.6 %collective-permute-start.1 = (f32[16,24,128]{2,1,0:T(8,128)S(1)}, f32[16,24,128]{2,1,0:T(8,128)S(1)}, u32[]{:S(2)}, u32[]{:S(2)}) collective-permute-start(f32[16,24,128]{2,1,0:T(8,128)S(1)} %get-tuple-element.23), channel_id=1, source_target_pairs={{0,3},{7,4},{8,11},{15,12},{16,19},{23,20},{24,27},{31,28},{32,35}... | collective-permute-start | bytes 589832 | tf_op jit(solution)/shard_map/ppermute | solution.py:475
  7.6 1.2 %copy-start.3 = (f32[24,90,128]{2,0,1:T(8,128)S(1)}, f32[24,90,128]{2,0,1:T(8,128)}, u32[]{:S(2)}) copy-start(f32[24,90,128]{2,0,1:T(8,128)} %param.10) | copy-start | bytes 3317764
  10.8 12.1 %collective-permute-start.3 = (f32[16,24,128]{2,1,0:T(8,128)S(1)}, f32[16,24,128]{2,1,0:T(8,128)S(1)}, u32[]{:S(2)}, u32[]{:S(2)}) collective-permute-start(f32[16,24,128]{2,1,0:T(8,128)S(1)} %get-tuple-element.27), channel_id=1, source_target_pairs={{0,1},{7,6},{8,9},{15,14},{16,17},{23,22},{24,25},{31,30},{32,33},... | collective-permute-start | bytes 589832 | tf_op jit(solution)/shard_map/ppermute | solution.py:475
  11.5 11.4 %collective-permute-start.4 = (f32[16,24,128]{2,1,0:T(8,128)S(1)}, f32[16,24,128]{2,1,0:T(8,128)S(1)}, u32[]{:S(2)}, u32[]{:S(2)}) collective-permute-start(f32[16,24,128]{2,1,0:T(8,128)S(1)} %get-tuple-element.28), channel_id=1, source_target_pairs={{0,3},{7,4},{8,11},{15,12},{16,19},{23,20},{24,27},{31,28},{32,35}... | collective-permute-start | bytes 589832 | tf_op jit(solution)/shard_map/ppermute | solution.py:475
  12.8 10.1 %collective-permute-start.5 = (f32[2,90,128]{2,1,0:T(8,128)S(1)}, f32[2,90,128]{2,1,0:T(8,128)S(1)}, u32[]{:S(2)}, u32[]{:S(2)}) collective-permute-start(f32[2,90,128]{2,1,0:T(8,128)S(1)} %get-tuple-element.29), channel_id=1, source_target_pairs={{3,4},{4,3},{11,12},{12,11},{19,20},{20,19},{27,28},{28,27},{35,36... | collective-permute-start | bytes 276488 | tf_op jit(solution)/shard_map/ppermute | solution.py:475
  22.9 26.0 %copy-start.5 = (f32[2,17,24,128]{3,2,1,0:T(8,128)S(1)}, f32[2,17,24,128]{3,2,1,0:T(8,128)}, u32[]{:S(2)}) copy-start(f32[2,17,24,128]{3,2,1,0:T(8,128)} %constant.15.clone.back_twiddle) | copy-start | bytes 1253380
  23.0 25.9 %copy-start.6 = (f32[2,17,24,128]{3,2,1,0:T(8,128)S(1)}, f32[2,17,24,128]{3,2,1,0:T(8,128)}, u32[]{:S(2)}) copy-start(f32[2,17,24,128]{3,2,1,0:T(8,128)} %constant.14.clone.twiddle) | copy-start | bytes 1253380
  23.0 25.9 %copy-start.7 = (f32[2,192,192]{2,1,0:T(8,128)S(1)}, f32[2,192,192]{2,1,0:T(8,128)}, u32[]{:S(2)}) copy-start(f32[2,192,192]{2,1,0:T(8,128)} %constant.13.clone.backward) | copy-start | bytes 884740
  23.0 25.9 %copy-start.8 = (f32[2,192,192]{2,1,0:T(8,128)S(1)}, f32[2,192,192]{2,1,0:T(8,128)}, u32[]{:S(2)}) copy-start(f32[2,192,192]{2,1,0:T(8,128)} %constant.12.clone.forward) | copy-start | bytes 884740
  48.9 35.8 %copy-start.4 = (f32[24,90,128]{2,0,1:T(8,128)S(1)}, f32[24,90,128]{2,0,1:T(8,128)}, u32[]{:S(2)}) copy-start(f32[24,90,128]{2,0,1:T(8,128)} %param.10) | copy-start | bytes 3317764
  69.6 15.1 %collective-permute-start.7 = (f32[32,24,128]{2,1,0:T(8,128)S(1)}, f32[32,24,128]{2,1,0:T(8,128)S(1)}, u32[]{:S(2)}, u32[]{:S(2)}) collective-permute-start(f32[32,24,128]{2,1,0:T(8,128)S(1)} %all_to_all.11.ret0), channel_id=1, source_target_pairs={{3,0},{4,7},{11,8},{12,15},{19,16},{20,23},{27,24},{28,31},{35,32}... | collective-permute-start | bytes 1179656 | tf_op jit(solution)/shard_map/ppermute | solution.py:475
  70.9 13.8 %collective-permute-start.6 = (f32[32,24,128]{2,1,0:T(8,128)S(1)}, f32[32,24,128]{2,1,0:T(8,128)S(1)}, u32[]{:S(2)}, u32[]{:S(2)}) collective-permute-start(f32[32,24,128]{2,1,0:T(8,128)S(1)} %all_to_all.11.ret0), channel_id=1, source_target_pairs={{1,0},{6,7},{9,8},{14,15},{17,16},{22,23},{25,24},{30,31},{33,32},... | collective-permute-start | bytes 1179656 | tf_op jit(solution)/shard_map/ppermute | solution.py:475
  71.6 13.1 %collective-permute-start.10 = (f32[2,90,128]{2,1,0:T(8,128)S(1)}, f32[2,90,128]{2,1,0:T(8,128)S(1)}, u32[]{:S(2)}, u32[]{:S(2)}) collective-permute-start(f32[2,90,128]{2,1,0:T(8,128)S(1)} %get-tuple-element.32), channel_id=1, source_target_pairs={{0,1},{1,2},{2,3},{4,5},{5,6},{6,7},{8,9},{9,10},{10,11},{12,13},{... | collective-permute-start | bytes 276488 | tf_op jit(solution)/shard_map/ppermute | solution.py:475
  72.9 11.8 %collective-permute-start.11 = (f32[2,90,128]{2,1,0:T(8,128)S(1)}, f32[2,90,128]{2,1,0:T(8,128)S(1)}, u32[]{:S(2)}, u32[]{:S(2)}) collective-permute-start(f32[2,90,128]{2,1,0:T(8,128)S(1)} %get-tuple-element.33), channel_id=1, source_target_pairs={{1,0},{2,1},{3,2},{5,4},{6,5},{7,6},{9,8},{10,9},{11,10},{13,12},{... | collective-permute-start | bytes 276488 | tf_op jit(solution)/shard_map/ppermute | solution.py:475
  77.5 1.7 %collective-permute-start.8 = (f32[3,24,128]{2,1,0:T(8,128)S(1)}, f32[3,24,128]{2,1,0:T(8,128)S(1)}, u32[]{:S(2)}, u32[]{:S(2)}) collective-permute-start(f32[3,24,128]{2,1,0:T(8,128)S(1)} %get-tuple-element.30), channel_id=1, source_target_pairs={{8,0},{16,8},{24,16},{32,24},{40,32},{48,40},{56,48},{64,56},{72,6... | collective-permute-start | bytes 110600 | tf_op jit(solution)/shard_map/ppermute | solution.py:515
  79.2 5.5 %collective-permute-start.9 = (f32[3,24,128]{2,1,0:T(8,128)S(1)}, f32[3,24,128]{2,1,0:T(8,128)S(1)}, u32[]{:S(2)}, u32[]{:S(2)}) collective-permute-start(f32[3,24,128]{2,1,0:T(8,128)S(1)} %get-tuple-element.31), channel_id=1, source_target_pairs={{0,8},{8,16},{16,24},{24,32},{32,40},{40,48},{48,56},{56,64},{64,7... | collective-permute-start | bytes 110600 | tf_op jit(solution)/shard_map/ppermute | solution.py:516

commit v4 on v3

--- a/solution.py
+++ b/solution.py
@@ -96,7 +96,11 @@
 
 def line_of(ref, row, count=COLS, first=0):
     rows = ref.shape[1]
-    return ref.reshape(ref.shape[0] * rows, LEV)[pl.ds(first * rows + row, count, stride=rows), :]
+    flat = ref.reshape(ref.shape[0] * rows, LEV)
+    start, whole_tiles = first * rows + row, count // 8 * 8
+    line = flat[pl.ds(start, whole_tiles, stride=rows), :]
+    rest = [flat[pl.ds(start + j * rows, 1), :] for j in range(whole_tiles, count)]
+    return jnp.concatenate([line] + rest, axis=0) if rest else line
 
 
 def shifted(x, above, below):

time: 87.8 us -> 87.8 us (level)
  no operation moved by 1% of the time
where the time goes in v4:
time: 87.8 us; the launch traced here: 87.4 us
  blocking collectives  44.2 us (50%)
  starting transfers between devices  19.2 us (22%)
  waiting for transfers between devices  11.5 us (13%)
  Pallas kernels  10.3 us (12%)
  local copies, waits for them, and re-layouts  1.29 us (1%)
  between operations  0.89 us (1%)
    all_to_all x1, blocking collectives, body(): lines = lax.all_to_all(lines, 'lon', 0, 0, tiled=True)  25.4 us
    all_to_all x1, blocking collectives, body(): back = lax.all_to_all(low, 'lon', 0, 0, tiled=True)  18.9 us
    ppermute x9, starting transfers between devices, moved(): return lax.ppermute(x, ('lon', 'lat'), full)  16.6 us
    ppermute x9, waiting for transfers between devices, moved(): return lax.ppermute(x, ('lon', 'lat'), full)  5.33 us
    ppermute x1, waiting for transfers between devices, body(): west = lax.ppermute(last_cols, 'lon', ring)  4.54 us
    pallas_call x1, Pallas kernels, body(): local_call(outputs, 'outputs', 1, 13, [whole_block] * 4, 9000000, [pltpu....  2.72 us
    pallas_call x1, Pallas kernels, body(): local_call(pack_stepped, 'pack_stepped', 2, 6, [chunk] * 3 + [(3, ROWS, L...  1.94 us
    pallas_call x1, Pallas kernels, body(): call(pole_row, 'pole_row', 1, [OUTER_TILES] * 2, [border], 1000000, vmem=...  1.93 us
  transfers between devices with their start and end apart: 12, of which 3 were waited for; matrix products, arithmetic and copies ran while one was open for 0% of the time, Pallas kernels for 4%

profile of v4, /device:TPU:6, one launch (start us, length us, event | category | flops | bytes accessed | tf_op | source)
XLA Modules:
  0.0 87.4 jit_solution(4622602740460897270)
XLA Ops:
  0.6 0.0 copy-start.2
  0.6 0.0 copy-start.9
  0.7 0.0 copy-start.1
  0.7 1.9 %pole_row.1 = f32[2,90,128]{2,1,0:T(8,128)} custom-call(s32[1]{0:T(128)} %bitcast.lat, f32[90,24,128]{2,1,0:T(8,128)} %bitcast.9, f32[90,24,128]{2,1,0:T(8,128)} %bitcast.12), custom_call_target="tpu_custom_call" | custom-call | flops 1000000 | bytes 1000000 | tf_op jit(solution)/shard_map/pole_row/pallas_call | solution.py:494
  2.6 0.0 copy-start
  2.6 1.6 %collective-permute-start.2 = (f32[2,90,128]{2,1,0:T(8,128)}, f32[2,90,128]{2,1,0:T(8,128)S(1)}, u32[]{:S(2)}, u32[]{:S(2)}) collective-permute-start(f32[2,90,128]{2,1,0:T(8,128)} %pole_row.1), channel_id=1, source_target_pairs={{0,128},{8,136},{16,144},{24,152},{32,160},{40,168},{48,176},{56,1... | collective-permute-start | bytes 276488 | tf_op jit(solution)/shard_map/ppermute | solution.py:497
  4.2 0.0 copy-done.2
  4.2 0.0 copy-done.9
  4.2 1.4 %pack_cotangent.1 = (f32[16,24,128]{2,1,0:T(8,128)S(1)}, f32[16,24,128]{2,1,0:T(8,128)S(1)}, f32[16,24,128]{2,1,0:T(8,128)S(1)}, f32[2,24,128]{2,1,0:T(8,128)S(1)}, f32[2,90,128]{2,1,0:T(8,128)S(1)}) custom-call(s32[1]{0:T(128)} %bitcast.lat, s32[24]{0:T(128)S(1)} %copy-done.9, f32[90,24,128]{2,1,0:T(8,128)S(1)} %bitcast.15), custom_call_target="tpu_custom_call" | custom-call | flops 1000000 | bytes 1000000 | tf_op jit(solution)/shard_map/pack_cotangent/pallas_call | solution.py:498
  5.6 0.7 collective-permute-start
  6.3 1.3 %collective-permute-start.1 = (f32[16,24,128]{2,1,0:T(8,128)S(1)}, f32[16,24,128]{2,1,0:T(8,128)S(1)}, u32[]{:S(2)}, u32[]{:S(2)}) collective-permute-start(f32[16,24,128]{2,1,0:T(8,128)S(1)} %get-tuple-element.23), channel_id=1, source_target_pairs={{0,3},{7,4},{8,11},{15,12},{16,19},{23,20},{24,27},{31,28},{32,35}... | collective-permute-start | bytes 589832 | tf_op jit(solution)/shard_map/ppermute | solution.py:479
  7.6 0.0 collective-permute-done.2.ac
  7.6 0.0 copy-done.1
  7.6 0.0 copy-done
  7.6 0.0 copy-start.3
  7.6 1.2 %copy-done.3 = f32[24,90,128]{2,0,1:T(8,128)S(1)} copy-done((f32[24,90,128]{2,0,1:T(8,128)S(1)}, f32[24,90,128]{2,0,1:T(8,128)}, u32[]{:S(2)}) %copy-start.3) | copy-done | bytes 1105944
  8.9 1.9 %pack_stepped.1 = (f32[16,24,128]{2,1,0:T(8,128)S(1)}, f32[16,24,128]{2,1,0:T(8,128)S(1)}, f32[16,24,128]{2,1,0:T(8,128)S(1)}, f32[3,24,128]{2,1,0:T(8,128)S(1)}...) custom-call(s32[1]{0:T(128)} %bitcast.lat, ...), custom_call_target="tpu_custom_call" | custom-call | flops 3000000 | bytes 3000000 | tf_op jit(solution)/shard_map/pack_stepped/pallas_call | solution.py:509
  10.8 0.7 collective-permute-start.3
  11.5 1.3 %collective-permute-start.4 = (f32[16,24,128]{2,1,0:T(8,128)S(1)}, f32[16,24,128]{2,1,0:T(8,128)S(1)}, u32[]{:S(2)}, u32[]{:S(2)}) collective-permute-start(f32[16,24,128]{2,1,0:T(8,128)S(1)} %get-tuple-element.28), channel_id=1, source_target_pairs={{0,3},{7,4},{8,11},{15,12},{16,19},{23,20},{24,27},{31,28},{32,35}... | collective-permute-start | bytes 589832 | tf_op jit(solution)/shard_map/ppermute | solution.py:479
  12.8 4.8 %collective-permute-start.5 = (f32[2,90,128]{2,1,0:T(8,128)S(1)}, f32[2,90,128]{2,1,0:T(8,128)S(1)}, u32[]{:S(2)}, u32[]{:S(2)}) collective-permute-start(f32[2,90,128]{2,1,0:T(8,128)S(1)} %get-tuple-element.29), channel_id=1, source_target_pairs={{3,4},{4,3},{11,12},{12,11},{19,20},{20,19},{27,28},{28,27},{35,36... | collective-permute-start | bytes 276488 | tf_op jit(solution)/shard_map/ppermute | solution.py:479
  17.6 5.3 %collective-permute-done.5.early = f32[2,90,128]{2,1,0:T(8,128)S(1)} collective-permute-done((f32[2,90,128]{2,1,0:T(8,128)S(1)}, f32[2,90,128]{2,1,0:T(8,128)S(1)}, u32[]{:S(2)}, u32[]{:S(2)}) %collective-permute-start.5) | collective-permute-done | bytes 92192 | tf_op jit(solution)/shard_map/ppermute | solution.py:479
  22.9 0.0 collective-permute-done.a_c
  22.9 0.0 collective-permute-done.1.b_c
  22.9 0.0 collective-permute-done.3.a_s
  22.9 0.0 collective-permute-done.4.b_s
  23.0 0.0 copy-start.5
  23.0 0.0 copy-start.6
  23.0 0.0 copy-start.7
  23.0 0.0 copy-start.8
  23.0 0.5 pick.1
  23.6 25.4 %all_to_all.10.x = f32[32,24,128]{2,1,0:T(8,128)S(1)} all-to-all(f32[32,24,128]{2,1,0:T(8,128)S(1)} %pick.1), channel_id=1, replica_groups=mesh['lon'=32,'lat'=8] {'lon'}, dimensions={0} | all-to-all | bytes 786432 | tf_op jit(solution)/shard_map/all_to_all | solution.py:527
  48.9 0.0 copy-done.5
  48.9 0.0 copy-done.6
  48.9 0.0 copy-done.7
  48.9 0.0 copy-done.8
  48.9 0.0 copy-start.4
  48.9 1.8 %keep_low.1 = f32[32,24,128]{2,1,0:T(8,128)S(1)} custom-call(f32[32,24,128]{2,1,0:T(8,128)S(1)} %all_to_all.10.x, f32[2,192,192]{2,1,0:T(8,128)S(1)} %copy-done.8, f32[2,192,192]{2,1,0:T(8,128)S(1)} %copy-done.7, f32[2,17,24,128]{3,2,1,0:T(8,128)S(1)} %copy-done.6, f32[2,17,24,128]{3,2,1,0:T(8,128)S(1)} %copy-done.5), custom_call_target="tpu_custom_call" | custom-call | flops 5000000 | bytes 3000000 | tf_op jit(solution)/shard_map/keep_low/pallas_call | solution.py:529
  50.7 18.9 %all_to_all.11.ret0 = f32[32,24,128]{2,1,0:T(8,128)S(1)} all-to-all(f32[32,24,128]{2,1,0:T(8,128)S(1)} %keep_low.1), channel_id=1, replica_groups=mesh['lon'=32,'lat'=8] {'lon'}, dimensions={0} | all-to-all | bytes 786432 | tf_op jit(solution)/shard_map/all_to_all | solution.py:542
  69.6 1.3 %collective-permute-start.7 = (f32[32,24,128]{2,1,0:T(8,128)S(1)}, f32[32,24,128]{2,1,0:T(8,128)S(1)}, u32[]{:S(2)}, u32[]{:S(2)}) collective-permute-start(f32[32,24,128]{2,1,0:T(8,128)S(1)} %all_to_all.11.ret0), channel_id=1, source_target_pairs={{3,0},{4,7},{11,8},{12,15},{19,16},{20,23},{27,24},{28,31},{35,32}... | collective-permute-start | bytes 1179656 | tf_op jit(solution)/shard_map/ppermute | solution.py:479
  70.9 0.7 collective-permute-start.6
  71.6 1.3 %collective-permute-start.10 = (f32[2,90,128]{2,1,0:T(8,128)S(1)}, f32[2,90,128]{2,1,0:T(8,128)S(1)}, u32[]{:S(2)}, u32[]{:S(2)}) collective-permute-start(f32[2,90,128]{2,1,0:T(8,128)S(1)} %get-tuple-element.32), channel_id=1, source_target_pairs={{0,1},{1,2},{2,3},{4,5},{5,6},{6,7},{8,9},{9,10},{10,11},{12,13},{... | collective-permute-start | bytes 276488 | tf_op jit(solution)/shard_map/ppermute | solution.py:479
  72.9 4.6 %collective-permute-start.11 = (f32[2,90,128]{2,1,0:T(8,128)S(1)}, f32[2,90,128]{2,1,0:T(8,128)S(1)}, u32[]{:S(2)}, u32[]{:S(2)}) collective-permute-start(f32[2,90,128]{2,1,0:T(8,128)S(1)} %get-tuple-element.33), channel_id=1, source_target_pairs={{1,0},{2,1},{3,2},{5,4},{6,5},{7,6},{9,8},{10,9},{11,10},{13,12},{... | collective-permute-start | bytes 276488 | tf_op jit(solution)/shard_map/ppermute | solution.py:479
  77.5 0.1 collective-permute-start.8
  77.5 1.6 %collective-permute-done.8.he = f32[3,24,128]{2,1,0:T(8,128)S(1)} collective-permute-done((f32[3,24,128]{2,1,0:T(8,128)S(1)}, f32[3,24,128]{2,1,0:T(8,128)S(1)}, u32[]{:S(2)}, u32[]{:S(2)}) %collective-permute-start.8) | collective-permute-done | bytes 36896 | tf_op jit(solution)/shard_map/ppermute | solution.py:519
  79.2 1.0 %collective-permute-start.9 = (f32[3,24,128]{2,1,0:T(8,128)S(1)}, f32[3,24,128]{2,1,0:T(8,128)S(1)}, u32[]{:S(2)}, u32[]{:S(2)}) collective-permute-start(f32[3,24,128]{2,1,0:T(8,128)S(1)} %get-tuple-element.31), channel_id=1, source_target_pairs={{0,8},{8,16},{16,24},{24,32},{32,40},{40,48},{48,56},{56,64},{64,7... | collective-permute-start | bytes 110600 | tf_op jit(solution)/shard_map/ppermute | solution.py:520
  80.1 4.5 %collective-permute-done.9.hw = f32[3,24,128]{2,1,0:T(8,128)S(1)} collective-permute-done((f32[3,24,128]{2,1,0:T(8,128)S(1)}, f32[3,24,128]{2,1,0:T(8,128)S(1)}, u32[]{:S(2)}, u32[]{:S(2)}) %collective-permute-start.9) | collective-permute-done | bytes 36896 | tf_op jit(solution)/shard_map/ppermute | solution.py:520
  84.7 0.0 collective-permute-done.10.n3
  84.7 0.0 collective-permute-done.11.s3
  84.7 0.0 collective-permute-done.7.ret2
  84.7 0.0 collective-permute-done.6.ret1
  84.7 0.0 copy-done.4
  84.7 2.7 %outputs.1 = (f32[90,24,128]{2,1,0:T(8,128)}, f32[90,24,128]{2,1,0:T(8,128)}, f32[90,24,128]{2,1,0:T(8,128)}, f32[90,24,128]{2,1,0:T(8,128)}) custom-call(s32[1]{0:T(128)} %bitcast.lat, f32[32,24,128]{2,1,0:T(8,128)S(1)} %all_to_all.11.ret0, f32[32,24,128]{2,1,0:T(8,128)S(1)} %collective-permute-done.6.ret1, f32[32,24,128]{2,1,0:T(8,128)S(1)} %collective-permute-done.7.ret2, ...), custom_call_target="tpu_custom_call" | custom-call | flops 9000000 | bytes 9000000 | tf_op jit(solution)/shard_map/outputs/pallas_call | solution.py:547
Async XLA Ops:
  0.6 3.5 %copy-start.2 = (f32[24,90,128]{2,0,1:T(8,128)S(1)}, f32[24,90,128]{2,0,1:T(8,128)}, u32[]{:S(2)}) copy-start(f32[24,90,128]{2,0,1:T(8,128)} %param.12) | copy-start | bytes 3317764
  0.6 3.5 %copy-start.9 = (s32[24]{0:T(128)S(1)}, s32[24]{0:T(128)}, u32[]{:S(2)}) copy-start(s32[24]{0:T(128)} %cutoff.3) | copy-start | bytes 292
  0.7 7.0 %copy-start.1 = (f32[24,90,128]{2,0,1:T(8,128)S(1)}, f32[24,90,128]{2,0,1:T(8,128)}, u32[]{:S(2)}) copy-start(f32[24,90,128]{2,0,1:T(8,128)} %param.11) | copy-start | bytes 3317764
  2.6 5.0 %copy-start = (f32[24,90,128]{2,0,1:T(8,128)S(1)}, f32[24,90,128]{2,0,1:T(8,128)}, u32[]{:S(2)}) copy-start(f32[24,90,128]{2,0,1:T(8,128)} %param.9) | copy-start | bytes 3317764
  2.6 5.0 %collective-permute-start.2 = (f32[2,90,128]{2,1,0:T(8,128)}, f32[2,90,128]{2,1,0:T(8,128)S(1)}, u32[]{:S(2)}, u32[]{:S(2)}) collective-permute-start(f32[2,90,128]{2,1,0:T(8,128)} %pole_row.1), channel_id=1, source_target_pairs={{0,128},{8,136},{16,144},{24,152},{32,160},{40,168},{48,176},{56,1... | collective-permute-start | bytes 276488 | tf_op jit(solution)/shard_map/ppermute | solution.py:497
  5.6 17.3 %collective-permute-start = (f32[16,24,128]{2,1,0:T(8,128)S(1)}, f32[16,24,128]{2,1,0:T(8,128)S(1)}, u32[]{:S(2)}, u32[]{:S(2)}) collective-permute-start(f32[16,24,128]{2,1,0:T(8,128)S(1)} %get-tuple-element.22), channel_id=1, source_target_pairs={{0,1},{7,6},{8,9},{15,14},{16,17},{23,22},{24,25},{31,30},{32,33},... | collective-permute-start | bytes 589832 | tf_op jit(solution)/shard_map/ppermute | solution.py:479
  6.3 16.6 %collective-permute-start.1 = (f32[16,24,128]{2,1,0:T(8,128)S(1)}, f32[16,24,128]{2,1,0:T(8,128)S(1)}, u32[]{:S(2)}, u32[]{:S(2)}) collective-permute-start(f32[16,24,128]{2,1,0:T(8,128)S(1)} %get-tuple-element.23), channel_id=1, source_target_pairs={{0,3},{7,4},{8,11},{15,12},{16,19},{23,20},{24,27},{31,28},{32,35}... | collective-permute-start | bytes 589832 | tf_op jit(solution)/shard_map/ppermute | solution.py:479
  7.6 1.2 %copy-start.3 = (f32[24,90,128]{2,0,1:T(8,128)S(1)}, f32[24,90,128]{2,0,1:T(8,128)}, u32[]{:S(2)}) copy-start(f32[24,90,128]{2,0,1:T(8,128)} %param.10) | copy-start | bytes 3317764
  10.8 12.1 %collective-permute-start.3 = (f32[16,24,128]{2,1,0:T(8,128)S(1)}, f32[16,24,128]{2,1,0:T(8,128)S(1)}, u32[]{:S(2)}, u32[]{:S(2)}) collective-permute-start(f32[16,24,128]{2,1,0:T(8,128)S(1)} %get-tuple-element.27), channel_id=1, source_target_pairs={{0,1},{7,6},{8,9},{15,14},{16,17},{23,22},{24,25},{31,30},{32,33},... | collective-permute-start | bytes 589832 | tf_op jit(solution)/shard_map/ppermute | solution.py:479
  11.5 11.4 %collective-permute-start.4 = (f32[16,24,128]{2,1,0:T(8,128)S(1)}, f32[16,24,128]{2,1,0:T(8,128)S(1)}, u32[]{:S(2)}, u32[]{:S(2)}) collective-permute-start(f32[16,24,128]{2,1,0:T(8,128)S(1)} %get-tuple-element.28), channel_id=1, source_target_pairs={{0,3},{7,4},{8,11},{15,12},{16,19},{23,20},{24,27},{31,28},{32,35}... | collective-permute-start | bytes 589832 | tf_op jit(solution)/shard_map/ppermute | solution.py:479
  12.8 10.1 %collective-permute-start.5 = (f32[2,90,128]{2,1,0:T(8,128)S(1)}, f32[2,90,128]{2,1,0:T(8,128)S(1)}, u32[]{:S(2)}, u32[]{:S(2)}) collective-permute-start(f32[2,90,128]{2,1,0:T(8,128)S(1)} %get-tuple-element.29), channel_id=1, source_target_pairs={{3,4},{4,3},{11,12},{12,11},{19,20},{20,19},{27,28},{28,27},{35,36... | collective-permute-start | bytes 276488 | tf_op jit(solution)/shard_map/ppermute | solution.py:479
  23.0 26.0 %copy-start.5 = (f32[2,17,24,128]{3,2,1,0:T(8,128)S(1)}, f32[2,17,24,128]{3,2,1,0:T(8,128)}, u32[]{:S(2)}) copy-start(f32[2,17,24,128]{3,2,1,0:T(8,128)} %constant.15.clone.back_twiddle) | copy-start | bytes 1253380
  23.0 25.9 %copy-start.6 = (f32[2,17,24,128]{3,2,1,0:T(8,128)S(1)}, f32[2,17,24,128]{3,2,1,0:T(8,128)}, u32[]{:S(2)}) copy-start(f32[2,17,24,128]{3,2,1,0:T(8,128)} %constant.14.clone.twiddle) | copy-start | bytes 1253380
  23.0 25.9 %copy-start.7 = (f32[2,192,192]{2,1,0:T(8,128)S(1)}, f32[2,192,192]{2,1,0:T(8,128)}, u32[]{:S(2)}) copy-start(f32[2,192,192]{2,1,0:T(8,128)} %constant.13.clone.backward) | copy-start | bytes 884740
  23.0 25.9 %copy-start.8 = (f32[2,192,192]{2,1,0:T(8,128)S(1)}, f32[2,192,192]{2,1,0:T(8,128)}, u32[]{:S(2)}) copy-start(f32[2,192,192]{2,1,0:T(8,128)} %constant.12.clone.forward) | copy-start | bytes 884740
  48.9 35.8 %copy-start.4 = (f32[24,90,128]{2,0,1:T(8,128)S(1)}, f32[24,90,128]{2,0,1:T(8,128)}, u32[]{:S(2)}) copy-start(f32[24,90,128]{2,0,1:T(8,128)} %param.10) | copy-start | bytes 3317764
  69.6 15.1 %collective-permute-start.7 = (f32[32,24,128]{2,1,0:T(8,128)S(1)}, f32[32,24,128]{2,1,0:T(8,128)S(1)}, u32[]{:S(2)}, u32[]{:S(2)}) collective-permute-start(f32[32,24,128]{2,1,0:T(8,128)S(1)} %all_to_all.11.ret0), channel_id=1, source_target_pairs={{3,0},{4,7},{11,8},{12,15},{19,16},{20,23},{27,24},{28,31},{35,32}... | collective-permute-start | bytes 1179656 | tf_op jit(solution)/shard_map/ppermute | solution.py:479
  70.9 13.8 %collective-permute-start.6 = (f32[32,24,128]{2,1,0:T(8,128)S(1)}, f32[32,24,128]{2,1,0:T(8,128)S(1)}, u32[]{:S(2)}, u32[]{:S(2)}) collective-permute-start(f32[32,24,128]{2,1,0:T(8,128)S(1)} %all_to_all.11.ret0), channel_id=1, source_target_pairs={{1,0},{6,7},{9,8},{14,15},{17,16},{22,23},{25,24},{30,31},{33,32},... | collective-permute-start | bytes 1179656 | tf_op jit(solution)/shard_map/ppermute | solution.py:479
  71.6 13.1 %collective-permute-start.10 = (f32[2,90,128]{2,1,0:T(8,128)S(1)}, f32[2,90,128]{2,1,0:T(8,128)S(1)}, u32[]{:S(2)}, u32[]{:S(2)}) collective-permute-start(f32[2,90,128]{2,1,0:T(8,128)S(1)} %get-tuple-element.32), channel_id=1, source_target_pairs={{0,1},{1,2},{2,3},{4,5},{5,6},{6,7},{8,9},{9,10},{10,11},{12,13},{... | collective-permute-start | bytes 276488 | tf_op jit(solution)/shard_map/ppermute | solution.py:479
  72.9 11.8 %collective-permute-start.11 = (f32[2,90,128]{2,1,0:T(8,128)S(1)}, f32[2,90,128]{2,1,0:T(8,128)S(1)}, u32[]{:S(2)}, u32[]{:S(2)}) collective-permute-start(f32[2,90,128]{2,1,0:T(8,128)S(1)} %get-tuple-element.33), channel_id=1, source_target_pairs={{1,0},{2,1},{3,2},{5,4},{6,5},{7,6},{9,8},{10,9},{11,10},{13,12},{... | collective-permute-start | bytes 276488 | tf_op jit(solution)/shard_map/ppermute | solution.py:479
  77.5 1.7 %collective-permute-start.8 = (f32[3,24,128]{2,1,0:T(8,128)S(1)}, f32[3,24,128]{2,1,0:T(8,128)S(1)}, u32[]{:S(2)}, u32[]{:S(2)}) collective-permute-start(f32[3,24,128]{2,1,0:T(8,128)S(1)} %get-tuple-element.30), channel_id=1, source_target_pairs={{8,0},{16,8},{24,16},{32,24},{40,32},{48,40},{56,48},{64,56},{72,6... | collective-permute-start | bytes 110600 | tf_op jit(solution)/shard_map/ppermute | solution.py:519
  79.2 5.5 %collective-permute-start.9 = (f32[3,24,128]{2,1,0:T(8,128)S(1)}, f32[3,24,128]{2,1,0:T(8,128)S(1)}, u32[]{:S(2)}, u32[]{:S(2)}) collective-permute-start(f32[3,24,128]{2,1,0:T(8,128)S(1)} %get-tuple-element.31), channel_id=1, source_target_pairs={{0,8},{8,16},{16,24},{24,32},{32,40},{40,48},{48,56},{56,64},{64,7... | collective-permute-start | bytes 110600 | tf_op jit(solution)/shard_map/ppermute | solution.py:520

commit v5 on v4

--- a/solution.py
+++ b/solution.py
@@ -24,8 +24,8 @@
 PITCH = 24
 CHUNK = 15
 
-SPREAD_A = ((0, 1), (7, 6))
-SPREAD_B = ((0, 3), (7, 4))
+SPREAD_A = ((0, 3), (7, 4))
+SPREAD_B = ((0, 1), (7, 6))
 EARLY = ((3, 4), (4, 3))
 SOUTHWARD = ((0, 1), (1, 2), (2, 3), (4, 5), (5, 6), (6, 7))
 NORTHWARD = ((1, 0), (2, 1), (3, 2), (5, 4), (6, 5), (7, 6))
@@ -265,7 +265,7 @@
 
 def pick(lat, own_c, a_c, b_c, own_s, a_s, b_s, early, out, sems):
     polar = (lat[0] == 0) | (lat[0] == LAT - 1)
-    in_a = (lat[0] == 1) | (lat[0] == LAT - 2)
+    in_a = (lat[0] == 3) | (lat[0] == LAT - 4)
 
     def copies(c, s):
         return [

time: 87.8 us -> 87.8 us (level)
  no operation moved by 1% of the time
where the time goes in v5:
time: 87.8 us; the launch traced here: 87.4 us
  blocking collectives  44.2 us (50%)
  starting transfers between devices  19.2 us (22%)
  waiting for transfers between devices  11.5 us (13%)
  Pallas kernels  10.3 us (12%)
  local copies, waits for them, and re-layouts  1.29 us (1%)
  between operations  0.89 us (1%)
    all_to_all x1, blocking collectives, body(): lines = lax.all_to_all(lines, 'lon', 0, 0, tiled=True)  25.4 us
    all_to_all x1, blocking collectives, body(): back = lax.all_to_all(low, 'lon', 0, 0, tiled=True)  18.9 us
    ppermute x9, starting transfers between devices, moved(): return lax.ppermute(x, ('lon', 'lat'), full)  16.6 us
    ppermute x9, waiting for transfers between devices, moved(): return lax.ppermute(x, ('lon', 'lat'), full)  5.33 us
    ppermute x1, waiting for transfers between devices, body(): west = lax.ppermute(last_cols, 'lon', ring)  4.54 us
    pallas_call x1, Pallas kernels, body(): local_call(outputs, 'outputs', 1, 13, [whole_block] * 4, 9000000, [pltpu....  2.72 us
    pallas_call x1, Pallas kernels, body(): local_call(pack_stepped, 'pack_stepped', 2, 6, [chunk] * 3 + [(3, ROWS, L...  1.94 us
    pallas_call x1, Pallas kernels, body(): call(pole_row, 'pole_row', 1, [OUTER_TILES] * 2, [border], 1000000, vmem=...  1.93 us
  transfers between devices with their start and end apart: 12, of which 3 were waited for; matrix products, arithmetic and copies ran while one was open for 0% of the time, Pallas kernels for 4%

profile of v5, /device:TPU:6, one launch (start us, length us, event | category | flops | bytes accessed | tf_op | source)
XLA Modules:
  0.0 87.4 jit_solution(8193089958588453805)
XLA Ops:
  0.6 0.0 copy-start.2
  0.6 0.0 copy-start.9
  0.7 0.0 copy-start.1
  0.7 1.9 %pole_row.1 = f32[2,90,128]{2,1,0:T(8,128)} custom-call(s32[1]{0:T(128)} %bitcast.lat, f32[90,24,128]{2,1,0:T(8,128)} %bitcast.9, f32[90,24,128]{2,1,0:T(8,128)} %bitcast.12), custom_call_target="tpu_custom_call" | custom-call | flops 1000000 | bytes 1000000 | tf_op jit(solution)/shard_map/pole_row/pallas_call | solution.py:494
  2.6 0.0 copy-start
  2.6 1.6 %collective-permute-start.2 = (f32[2,90,128]{2,1,0:T(8,128)}, f32[2,90,128]{2,1,0:T(8,128)S(1)}, u32[]{:S(2)}, u32[]{:S(2)}) collective-permute-start(f32[2,90,128]{2,1,0:T(8,128)} %pole_row.1), channel_id=1, source_target_pairs={{0,128},{8,136},{16,144},{24,152},{32,160},{40,168},{48,176},{56,1... | collective-permute-start | bytes 276488 | tf_op jit(solution)/shard_map/ppermute | solution.py:497
  4.2 0.0 copy-done.2
  4.2 0.0 copy-done.9
  4.2 1.4 %pack_cotangent.1 = (f32[16,24,128]{2,1,0:T(8,128)S(1)}, f32[16,24,128]{2,1,0:T(8,128)S(1)}, f32[16,24,128]{2,1,0:T(8,128)S(1)}, f32[2,24,128]{2,1,0:T(8,128)S(1)}, f32[2,90,128]{2,1,0:T(8,128)S(1)}) custom-call(s32[1]{0:T(128)} %bitcast.lat, s32[24]{0:T(128)S(1)} %copy-done.9, f32[90,24,128]{2,1,0:T(8,128)S(1)} %bitcast.15), custom_call_target="tpu_custom_call" | custom-call | flops 1000000 | bytes 1000000 | tf_op jit(solution)/shard_map/pack_cotangent/pallas_call | solution.py:498
  5.6 1.3 %collective-permute-start = (f32[16,24,128]{2,1,0:T(8,128)S(1)}, f32[16,24,128]{2,1,0:T(8,128)S(1)}, u32[]{:S(2)}, u32[]{:S(2)}) collective-permute-start(f32[16,24,128]{2,1,0:T(8,128)S(1)} %get-tuple-element.22), channel_id=1, source_target_pairs={{0,3},{7,4},{8,11},{15,12},{16,19},{23,20},{24,27},{31,28},{32,35}... | collective-permute-start | bytes 589832 | tf_op jit(solution)/shard_map/ppermute | solution.py:479
  6.9 0.7 collective-permute-start.1
  7.6 0.0 collective-permute-done.2.ac
  7.6 0.0 copy-done.1
  7.6 0.0 copy-done
  7.6 0.0 copy-start.3
  7.6 1.2 %copy-done.3 = f32[24,90,128]{2,0,1:T(8,128)S(1)} copy-done((f32[24,90,128]{2,0,1:T(8,128)S(1)}, f32[24,90,128]{2,0,1:T(8,128)}, u32[]{:S(2)}) %copy-start.3) | copy-done | bytes 1105944
  8.9 1.9 %pack_stepped.1 = (f32[16,24,128]{2,1,0:T(8,128)S(1)}, f32[16,24,128]{2,1,0:T(8,128)S(1)}, f32[16,24,128]{2,1,0:T(8,128)S(1)}, f32[3,24,128]{2,1,0:T(8,128)S(1)}...) custom-call(s32[1]{0:T(128)} %bitcast.lat, ...), custom_call_target="tpu_custom_call" | custom-call | flops 3000000 | bytes 3000000 | tf_op jit(solution)/shard_map/pack_stepped/pallas_call | solution.py:509
  10.8 1.3 %collective-permute-start.3 = (f32[16,24,128]{2,1,0:T(8,128)S(1)}, f32[16,24,128]{2,1,0:T(8,128)S(1)}, u32[]{:S(2)}, u32[]{:S(2)}) collective-permute-start(f32[16,24,128]{2,1,0:T(8,128)S(1)} %get-tuple-element.27), channel_id=1, source_target_pairs={{0,3},{7,4},{8,11},{15,12},{16,19},{23,20},{24,27},{31,28},{32,35}... | collective-permute-start | bytes 589832 | tf_op jit(solution)/shard_map/ppermute | solution.py:479
  12.1 0.7 collective-permute-start.4
  12.8 4.8 %collective-permute-start.5 = (f32[2,90,128]{2,1,0:T(8,128)S(1)}, f32[2,90,128]{2,1,0:T(8,128)S(1)}, u32[]{:S(2)}, u32[]{:S(2)}) collective-permute-start(f32[2,90,128]{2,1,0:T(8,128)S(1)} %get-tuple-element.29), channel_id=1, source_target_pairs={{3,4},{4,3},{11,12},{12,11},{19,20},{20,19},{27,28},{28,27},{35,36... | collective-permute-start | bytes 276488 | tf_op jit(solution)/shard_map/ppermute | solution.py:479
  17.6 5.3 %collective-permute-done.5.early = f32[2,90,128]{2,1,0:T(8,128)S(1)} collective-permute-done((f32[2,90,128]{2,1,0:T(8,128)S(1)}, f32[2,90,128]{2,1,0:T(8,128)S(1)}, u32[]{:S(2)}, u32[]{:S(2)}) %collective-permute-start.5) | collective-permute-done | bytes 92192 | tf_op jit(solution)/shard_map/ppermute | solution.py:479
  22.9 0.0 collective-permute-done.a_c
  22.9 0.0 collective-permute-done.1.b_c
  22.9 0.0 collective-permute-done.3.a_s
  22.9 0.0 collective-permute-done.4.b_s
  23.0 0.0 copy-start.5
  23.0 0.0 copy-start.6
  23.0 0.0 copy-start.7
  23.0 0.0 copy-start.8
  23.0 0.5 pick.1
  23.6 25.4 %all_to_all.10.x = f32[32,24,128]{2,1,0:T(8,128)S(1)} all-to-all(f32[32,24,128]{2,1,0:T(8,128)S(1)} %pick.1), channel_id=1, replica_groups=mesh['lon'=32,'lat'=8] {'lon'}, dimensions={0} | all-to-all | bytes 786432 | tf_op jit(solution)/shard_map/all_to_all | solution.py:527
  48.9 0.0 copy-done.5
  48.9 0.0 copy-done.6
  48.9 0.0 copy-done.7
  48.9 0.0 copy-done.8
  48.9 0.0 copy-start.4
  48.9 1.8 %keep_low.1 = f32[32,24,128]{2,1,0:T(8,128)S(1)} custom-call(f32[32,24,128]{2,1,0:T(8,128)S(1)} %all_to_all.10.x, f32[2,192,192]{2,1,0:T(8,128)S(1)} %copy-done.8, f32[2,192,192]{2,1,0:T(8,128)S(1)} %copy-done.7, f32[2,17,24,128]{3,2,1,0:T(8,128)S(1)} %copy-done.6, f32[2,17,24,128]{3,2,1,0:T(8,128)S(1)} %copy-done.5), custom_call_target="tpu_custom_call" | custom-call | flops 5000000 | bytes 3000000 | tf_op jit(solution)/shard_map/keep_low/pallas_call | solution.py:529
  50.7 18.9 %all_to_all.11.ret0 = f32[32,24,128]{2,1,0:T(8,128)S(1)} all-to-all(f32[32,24,128]{2,1,0:T(8,128)S(1)} %keep_low.1), channel_id=1, replica_groups=mesh['lon'=32,'lat'=8] {'lon'}, dimensions={0} | all-to-all | bytes 786432 | tf_op jit(solution)/shard_map/all_to_all | solution.py:542
  69.6 0.7 collective-permute-start.7
  70.3 1.3 %collective-permute-start.6 = (f32[32,24,128]{2,1,0:T(8,128)S(1)}, f32[32,24,128]{2,1,0:T(8,128)S(1)}, u32[]{:S(2)}, u32[]{:S(2)}) collective-permute-start(f32[32,24,128]{2,1,0:T(8,128)S(1)} %all_to_all.11.ret0), channel_id=1, source_target_pairs={{3,0},{4,7},{11,8},{12,15},{19,16},{20,23},{27,24},{28,31},{35,32}... | collective-permute-start | bytes 1179656 | tf_op jit(solution)/shard_map/ppermute | solution.py:479
  71.6 1.3 %collective-permute-start.10 = (f32[2,90,128]{2,1,0:T(8,128)S(1)}, f32[2,90,128]{2,1,0:T(8,128)S(1)}, u32[]{:S(2)}, u32[]{:S(2)}) collective-permute-start(f32[2,90,128]{2,1,0:T(8,128)S(1)} %get-tuple-element.32), channel_id=1, source_target_pairs={{0,1},{1,2},{2,3},{4,5},{5,6},{6,7},{8,9},{9,10},{10,11},{12,13},{... | collective-permute-start | bytes 276488 | tf_op jit(solution)/shard_map/ppermute | solution.py:479
  72.9 4.6 %collective-permute-start.11 = (f32[2,90,128]{2,1,0:T(8,128)S(1)}, f32[2,90,128]{2,1,0:T(8,128)S(1)}, u32[]{:S(2)}, u32[]{:S(2)}) collective-permute-start(f32[2,90,128]{2,1,0:T(8,128)S(1)} %get-tuple-element.33), channel_id=1, source_target_pairs={{1,0},{2,1},{3,2},{5,4},{6,5},{7,6},{9,8},{10,9},{11,10},{13,12},{... | collective-permute-start | bytes 276488 | tf_op jit(solution)/shard_map/ppermute | solution.py:479
  77.5 0.1 collective-permute-start.8
  77.5 1.6 %collective-permute-done.8.he = f32[3,24,128]{2,1,0:T(8,128)S(1)} collective-permute-done((f32[3,24,128]{2,1,0:T(8,128)S(1)}, f32[3,24,128]{2,1,0:T(8,128)S(1)}, u32[]{:S(2)}, u32[]{:S(2)}) %collective-permute-start.8) | collective-permute-done | bytes 36896 | tf_op jit(solution)/shard_map/ppermute | solution.py:519
  79.2 1.0 %collective-permute-start.9 = (f32[3,24,128]{2,1,0:T(8,128)S(1)}, f32[3,24,128]{2,1,0:T(8,128)S(1)}, u32[]{:S(2)}, u32[]{:S(2)}) collective-permute-start(f32[3,24,128]{2,1,0:T(8,128)S(1)} %get-tuple-element.31), channel_id=1, source_target_pairs={{0,8},{8,16},{16,24},{24,32},{32,40},{40,48},{48,56},{56,64},{64,7... | collective-permute-start | bytes 110600 | tf_op jit(solution)/shard_map/ppermute | solution.py:520
  80.1 4.5 %collective-permute-done.9.hw = f32[3,24,128]{2,1,0:T(8,128)S(1)} collective-permute-done((f32[3,24,128]{2,1,0:T(8,128)S(1)}, f32[3,24,128]{2,1,0:T(8,128)S(1)}, u32[]{:S(2)}, u32[]{:S(2)}) %collective-permute-start.9) | collective-permute-done | bytes 36896 | tf_op jit(solution)/shard_map/ppermute | solution.py:520
  84.7 0.0 collective-permute-done.10.n3
  84.7 0.0 collective-permute-done.11.s3
  84.7 0.0 collective-permute-done.7.ret2
  84.7 0.0 collective-permute-done.6.ret1
  84.7 0.0 copy-done.4
  84.7 2.7 %outputs.1 = (f32[90,24,128]{2,1,0:T(8,128)}, f32[90,24,128]{2,1,0:T(8,128)}, f32[90,24,128]{2,1,0:T(8,128)}, f32[90,24,128]{2,1,0:T(8,128)}) custom-call(s32[1]{0:T(128)} %bitcast.lat, f32[32,24,128]{2,1,0:T(8,128)S(1)} %all_to_all.11.ret0, f32[32,24,128]{2,1,0:T(8,128)S(1)} %collective-permute-done.6.ret1, f32[32,24,128]{2,1,0:T(8,128)S(1)} %collective-permute-done.7.ret2, ...), custom_call_target="tpu_custom_call" | custom-call | flops 9000000 | bytes 9000000 | tf_op jit(solution)/shard_map/outputs/pallas_call | solution.py:547
Async XLA Ops:
  0.6 3.5 %copy-start.2 = (f32[24,90,128]{2,0,1:T(8,128)S(1)}, f32[24,90,128]{2,0,1:T(8,128)}, u32[]{:S(2)}) copy-start(f32[24,90,128]{2,0,1:T(8,128)} %param.12) | copy-start | bytes 3317764
  0.6 3.5 %copy-start.9 = (s32[24]{0:T(128)S(1)}, s32[24]{0:T(128)}, u32[]{:S(2)}) copy-start(s32[24]{0:T(128)} %cutoff.3) | copy-start | bytes 292
  0.7 7.0 %copy-start.1 = (f32[24,90,128]{2,0,1:T(8,128)S(1)}, f32[24,90,128]{2,0,1:T(8,128)}, u32[]{:S(2)}) copy-start(f32[24,90,128]{2,0,1:T(8,128)} %param.11) | copy-start | bytes 3317764
  2.6 5.0 %copy-start = (f32[24,90,128]{2,0,1:T(8,128)S(1)}, f32[24,90,128]{2,0,1:T(8,128)}, u32[]{:S(2)}) copy-start(f32[24,90,128]{2,0,1:T(8,128)} %param.9) | copy-start | bytes 3317764
  2.6 5.0 %collective-permute-start.2 = (f32[2,90,128]{2,1,0:T(8,128)}, f32[2,90,128]{2,1,0:T(8,128)S(1)}, u32[]{:S(2)}, u32[]{:S(2)}) collective-permute-start(f32[2,90,128]{2,1,0:T(8,128)} %pole_row.1), channel_id=1, source_target_pairs={{0,128},{8,136},{16,144},{24,152},{32,160},{40,168},{48,176},{56,1... | collective-permute-start | bytes 276488 | tf_op jit(solution)/shard_map/ppermute | solution.py:497
  5.6 17.3 %collective-permute-start = (f32[16,24,128]{2,1,0:T(8,128)S(1)}, f32[16,24,128]{2,1,0:T(8,128)S(1)}, u32[]{:S(2)}, u32[]{:S(2)}) collective-permute-start(f32[16,24,128]{2,1,0:T(8,128)S(1)} %get-tuple-element.22), channel_id=1, source_target_pairs={{0,3},{7,4},{8,11},{15,12},{16,19},{23,20},{24,27},{31,28},{32,35}... | collective-permute-start | bytes 589832 | tf_op jit(solution)/shard_map/ppermute | solution.py:479
  6.9 16.0 %collective-permute-start.1 = (f32[16,24,128]{2,1,0:T(8,128)S(1)}, f32[16,24,128]{2,1,0:T(8,128)S(1)}, u32[]{:S(2)}, u32[]{:S(2)}) collective-permute-start(f32[16,24,128]{2,1,0:T(8,128)S(1)} %get-tuple-element.23), channel_id=1, source_target_pairs={{0,1},{7,6},{8,9},{15,14},{16,17},{23,22},{24,25},{31,30},{32,33},... | collective-permute-start | bytes 589832 | tf_op jit(solution)/shard_map/ppermute | solution.py:479
  7.6 1.2 %copy-start.3 = (f32[24,90,128]{2,0,1:T(8,128)S(1)}, f32[24,90,128]{2,0,1:T(8,128)}, u32[]{:S(2)}) copy-start(f32[24,90,128]{2,0,1:T(8,128)} %param.10) | copy-start | bytes 3317764
  10.8 12.1 %collective-permute-start.3 = (f32[16,24,128]{2,1,0:T(8,128)S(1)}, f32[16,24,128]{2,1,0:T(8,128)S(1)}, u32[]{:S(2)}, u32[]{:S(2)}) collective-permute-start(f32[16,24,128]{2,1,0:T(8,128)S(1)} %get-tuple-element.27), channel_id=1, source_target_pairs={{0,3},{7,4},{8,11},{15,12},{16,19},{23,20},{24,27},{31,28},{32,35}... | collective-permute-start | bytes 589832 | tf_op jit(solution)/shard_map/ppermute | solution.py:479
  12.1 10.8 %collective-permute-start.4 = (f32[16,24,128]{2,1,0:T(8,128)S(1)}, f32[16,24,128]{2,1,0:T(8,128)S(1)}, u32[]{:S(2)}, u32[]{:S(2)}) collective-permute-start(f32[16,24,128]{2,1,0:T(8,128)S(1)} %get-tuple-element.28), channel_id=1, source_target_pairs={{0,1},{7,6},{8,9},{15,14},{16,17},{23,22},{24,25},{31,30},{32,33},... | collective-permute-start | bytes 589832 | tf_op jit(solution)/shard_map/ppermute | solution.py:479
  12.8 10.1 %collective-permute-start.5 = (f32[2,90,128]{2,1,0:T(8,128)S(1)}, f32[2,90,128]{2,1,0:T(8,128)S(1)}, u32[]{:S(2)}, u32[]{:S(2)}) collective-permute-start(f32[2,90,128]{2,1,0:T(8,128)S(1)} %get-tuple-element.29), channel_id=1, source_target_pairs={{3,4},{4,3},{11,12},{12,11},{19,20},{20,19},{27,28},{28,27},{35,36... | collective-permute-start | bytes 276488 | tf_op jit(solution)/shard_map/ppermute | solution.py:479
  23.0 26.0 %copy-start.5 = (f32[2,17,24,128]{3,2,1,0:T(8,128)S(1)}, f32[2,17,24,128]{3,2,1,0:T(8,128)}, u32[]{:S(2)}) copy-start(f32[2,17,24,128]{3,2,1,0:T(8,128)} %constant.15.clone.back_twiddle) | copy-start | bytes 1253380
  23.0 25.9 %copy-start.6 = (f32[2,17,24,128]{3,2,1,0:T(8,128)S(1)}, f32[2,17,24,128]{3,2,1,0:T(8,128)}, u32[]{:S(2)}) copy-start(f32[2,17,24,128]{3,2,1,0:T(8,128)} %constant.14.clone.twiddle) | copy-start | bytes 1253380
  23.0 25.9 %copy-start.7 = (f32[2,192,192]{2,1,0:T(8,128)S(1)}, f32[2,192,192]{2,1,0:T(8,128)}, u32[]{:S(2)}) copy-start(f32[2,192,192]{2,1,0:T(8,128)} %constant.13.clone.backward) | copy-start | bytes 884740
  23.0 25.9 %copy-start.8 = (f32[2,192,192]{2,1,0:T(8,128)S(1)}, f32[2,192,192]{2,1,0:T(8,128)}, u32[]{:S(2)}) copy-start(f32[2,192,192]{2,1,0:T(8,128)} %constant.12.clone.forward) | copy-start | bytes 884740
  48.9 35.8 %copy-start.4 = (f32[24,90,128]{2,0,1:T(8,128)S(1)}, f32[24,90,128]{2,0,1:T(8,128)}, u32[]{:S(2)}) copy-start(f32[24,90,128]{2,0,1:T(8,128)} %param.10) | copy-start | bytes 3317764
  69.6 15.1 %collective-permute-start.7 = (f32[32,24,128]{2,1,0:T(8,128)S(1)}, f32[32,24,128]{2,1,0:T(8,128)S(1)}, u32[]{:S(2)}, u32[]{:S(2)}) collective-permute-start(f32[32,24,128]{2,1,0:T(8,128)S(1)} %all_to_all.11.ret0), channel_id=1, source_target_pairs={{1,0},{6,7},{9,8},{14,15},{17,16},{22,23},{25,24},{30,31},{33,32},... | collective-permute-start | bytes 1179656 | tf_op jit(solution)/shard_map/ppermute | solution.py:479
  70.3 14.4 %collective-permute-start.6 = (f32[32,24,128]{2,1,0:T(8,128)S(1)}, f32[32,24,128]{2,1,0:T(8,128)S(1)}, u32[]{:S(2)}, u32[]{:S(2)}) collective-permute-start(f32[32,24,128]{2,1,0:T(8,128)S(1)} %all_to_all.11.ret0), channel_id=1, source_target_pairs={{3,0},{4,7},{11,8},{12,15},{19,16},{20,23},{27,24},{28,31},{35,32}... | collective-permute-start | bytes 1179656 | tf_op jit(solution)/shard_map/ppermute | solution.py:479
  71.6 13.1 %collective-permute-start.10 = (f32[2,90,128]{2,1,0:T(8,128)S(1)}, f32[2,90,128]{2,1,0:T(8,128)S(1)}, u32[]{:S(2)}, u32[]{:S(2)}) collective-permute-start(f32[2,90,128]{2,1,0:T(8,128)S(1)} %get-tuple-element.32), channel_id=1, source_target_pairs={{0,1},{1,2},{2,3},{4,5},{5,6},{6,7},{8,9},{9,10},{10,11},{12,13},{... | collective-permute-start | bytes 276488 | tf_op jit(solution)/shard_map/ppermute | solution.py:479
  72.9 11.8 %collective-permute-start.11 = (f32[2,90,128]{2,1,0:T(8,128)S(1)}, f32[2,90,128]{2,1,0:T(8,128)S(1)}, u32[]{:S(2)}, u32[]{:S(2)}) collective-permute-start(f32[2,90,128]{2,1,0:T(8,128)S(1)} %get-tuple-element.33), channel_id=1, source_target_pairs={{1,0},{2,1},{3,2},{5,4},{6,5},{7,6},{9,8},{10,9},{11,10},{13,12},{... | collective-permute-start | bytes 276488 | tf_op jit(solution)/shard_map/ppermute | solution.py:479
  77.5 1.7 %collective-permute-start.8 = (f32[3,24,128]{2,1,0:T(8,128)S(1)}, f32[3,24,128]{2,1,0:T(8,128)S(1)}, u32[]{:S(2)}, u32[]{:S(2)}) collective-permute-start(f32[3,24,128]{2,1,0:T(8,128)S(1)} %get-tuple-element.30), channel_id=1, source_target_pairs={{8,0},{16,8},{24,16},{32,24},{40,32},{48,40},{56,48},{64,56},{72,6... | collective-permute-start | bytes 110600 | tf_op jit(solution)/shard_map/ppermute | solution.py:519
  79.2 5.5 %collective-permute-start.9 = (f32[3,24,128]{2,1,0:T(8,128)S(1)}, f32[3,24,128]{2,1,0:T(8,128)S(1)}, u32[]{:S(2)}, u32[]{:S(2)}) collective-permute-start(f32[3,24,128]{2,1,0:T(8,128)S(1)} %get-tuple-element.31), channel_id=1, source_target_pairs={{0,8},{8,16},{16,24},{24,32},{32,40},{40,48},{48,56},{56,64},{64,7... | collective-permute-start | bytes 110600 | tf_op jit(solution)/shard_map/ppermute | solution.py:520
